TPU v7x, 256 devices: a whole 4x4x8 slice. The times are simulated.
256 devices in a mesh: expert: 8 (over z), ray: 32 (over x, y, core).
Axes of the slice: x: 4, y: 4, z: 8, core: 2. Of those that a mesh axis runs over, the one named last changes fastest.
Arguments:
- features: bfloat16 [4096, 128, 256], P(('expert', 'ray')), may hold values from -6 to 6
- routes: int32 [4096, 128, 1], P(('expert', 'ray')), may hold values from 0 to 15; in each aligned block of 2048 rows (0 to 2047, 2048 to 4095, ..., all dimensions but the last counted through in order) at most 256 rows name the same one
- gate_values: bfloat16 [4096, 128], P(('expert', 'ray')), may hold values from 0.29882812 to 1
- deltas: float32 [4096, 128], P(('expert', 'ray')), may hold values from 0.004 to 0.04
- target: float32 [3, 4096], P(None, ('expert', 'ray')), may hold values from 0 to 1
- w_hidden: bfloat16 [16, 4, 256, 256], P('expert', None, 'ray'), may hold values from -0.375 to 0.375
- b_hidden: bfloat16 [16, 4, 256], P('expert', None, 'ray'), may hold values from -1.5 to 1.5
- w_head: bfloat16 [16, 4, 256], P('expert', None, 'ray'), may hold values from -0.375 to 0.375
Outputs:
- rendered: float32 [3, 4096], P(None, ('expert', 'ray'))
- grad_hidden: float32 [16, 4, 256, 256], P('expert', None, 'ray')
- grad_bias: float32 [16, 4, 256], P('expert', None, 'ray')
- grad_head: float32 [16, 4, 256], P('expert', None, 'ray')
Inputs may be any that keep to these rules, and one draw needn't show every extreme that they name: `routes`: among the rows of one device (aligned blocks of 2048 samples), no expert is named by more than 256 samples, a bound that some block reaches.
All inputs are finite; a program needn't handle non-finite values.
Results may differ from a plain program's by a relative error of at most 0.0035.
Values may be sent and summed in bfloat16 or wider, within the bound.
No kernel may reach another device: no remote copies, remote signals or barrier semaphores. Data moves between devices by JAX's collectives and lax.ppermute only.
A program may use at most 128 MiB of HBM per device.

v0:
```python
from functools import partial

import jax
import jax.numpy as jnp
from jax import lax
from jax.sharding import PartitionSpec as P


def gelu_tanh(value):
    return jax.nn.gelu(value, approximate=True)


def gelu_slope(value):
    return jax.vjp(gelu_tanh, value)[1](jnp.ones_like(value))[0]


def composite(gated_out, deltas):
    density = jax.nn.softplus(gated_out[0])
    radiance = jax.nn.sigmoid(gated_out[1:])
    optical = density * deltas
    before = jnp.cumsum(optical, axis=1) - optical
    weight = jnp.exp(-before) * (1.0 - jnp.exp(-optical))
    return jnp.sum(weight[None] * radiance, axis=2)


def expert_forward(layer_weights, layer_biases, head_weights, inputs):
    hidden = inputs
    activations = [hidden]
    pre_acts = []
    for layer in range(layer_weights.shape[1]):
        pre_act = jnp.einsum(
            "emd,edf->emf", hidden, layer_weights[:, layer], preferred_element_type=jnp.float32
        )
        pre_act = pre_act + layer_biases[:, layer][:, None, :].astype(jnp.float32)
        pre_acts.append(pre_act)
        hidden = gelu_tanh(pre_act).astype(jnp.bfloat16)
        activations.append(hidden)
    output = jnp.einsum("ecd,emd->ecm", head_weights, hidden, preferred_element_type=jnp.float32)
    return (activations, pre_acts, output)


def local(features, routes, gate_values, deltas, target, w_hidden, b_hidden, w_head):
    expert_count = lax.axis_size("expert")
    rays_dev, samples, feat_width = features.shape
    exp_dev = w_hidden.shape[0]
    layers = w_hidden.shape[1]
    experts = exp_dev * expert_count
    row_count = rays_dev * samples
    capacity = 2 * row_count // experts
    route_flat = routes.reshape(row_count)
    onehot = (route_flat[:, None] == jnp.arange(experts, dtype=jnp.int32)[None, :]).astype(
        jnp.int32
    )
    slot_pos = jnp.sum(onehot * (jnp.cumsum(onehot, axis=0) - 1), axis=1)
    slot_index = route_flat * capacity + slot_pos
    outgoing = jnp.zeros((experts * capacity, feat_width), jnp.bfloat16)
    outgoing = outgoing.at[slot_index].set(features.reshape(row_count, feat_width))
    outgoing = outgoing.reshape(expert_count, exp_dev, capacity, feat_width)
    layer_weights, head_weights, layer_biases = (
        lax.all_gather(w_hidden, "ray", axis=2, tiled=True),
        lax.all_gather(w_head, "ray", axis=2, tiled=True),
        lax.all_gather(b_hidden, "ray", axis=2, tiled=True),
    )
    gate_float = gate_values.astype(jnp.float32)
    received = lax.all_to_all(outgoing, "expert", split_axis=0, concat_axis=2, tiled=True)
    activations, pre_acts, output = expert_forward(
        layer_weights, layer_biases, head_weights, received[0]
    )
    returned = lax.all_to_all(
        output.reshape(exp_dev, 4, expert_count, capacity).astype(jnp.bfloat16),
        "expert",
        split_axis=2,
        concat_axis=2,
        tiled=True,
    ).astype(jnp.float32)
    out_slots = returned.transpose(2, 0, 3, 1).reshape(experts * capacity, 4)
    raw_out = out_slots[slot_index].T.reshape(4, rays_dev, samples)
    gated_out = gate_float[None] * raw_out
    rendered, pullback = jax.vjp(partial(composite, deltas=deltas), gated_out)
    grad_gated = pullback(rendered - target)[0]
    cotangent = (gate_float[None] * grad_gated).astype(jnp.bfloat16).reshape(4, row_count)
    cot_slots = jnp.zeros((4, experts * capacity), jnp.bfloat16).at[:, slot_index].set(cotangent)
    cot_slots = cot_slots.reshape(4, expert_count, exp_dev, capacity).transpose(1, 2, 0, 3)
    cot_recv = lax.all_to_all(cot_slots, "expert", split_axis=0, concat_axis=3, tiled=True)[0]
    grad_head = jnp.einsum(
        "ecm,emd->ecd", cot_recv, activations[-1], preferred_element_type=jnp.float32
    )
    grad_hidden = jnp.einsum(
        "ecm,ecd->emd", cot_recv, head_weights, preferred_element_type=jnp.float32
    )
    weight_list = [None] * layers
    shift_list = [None] * layers
    head_share = grad_head
    for layer in range(layers - 1, -1, -1):
        grad_pre = (grad_hidden * gelu_slope(pre_acts[layer])).astype(jnp.bfloat16)
        grad_weight = jnp.einsum(
            "emd,emf->edf", activations[layer], grad_pre, preferred_element_type=jnp.float32
        )
        grad_shift = jnp.sum(grad_pre, axis=1, dtype=jnp.float32)
        if layer > 0:
            grad_hidden = jnp.einsum(
                "emf,edf->emd",
                grad_pre,
                layer_weights[:, layer],
                preferred_element_type=jnp.float32,
            )
        extra = (grad_head.transpose(0, 2, 1),) if layer == layers - 1 else ()
        reduced = lax.psum_scatter(
            (grad_weight, grad_shift) + extra, "ray", scatter_dimension=1, tiled=True
        )
        weight_list[layer] = reduced[0]
        shift_list[layer] = reduced[1]
        if layer == layers - 1:
            head_share = reduced[2].transpose(0, 2, 1)
    weight_out = jnp.stack(weight_list, axis=1)
    shift_out = jnp.stack(shift_list, axis=1)
    return (rendered, weight_out, shift_out, head_share)


def solution(mesh):
    in_specs = (
        P(("expert", "ray"), None, None),
        P(("expert", "ray"), None, None),
        P(("expert", "ray"), None),
        P(("expert", "ray"), None),
        P(None, ("expert", "ray")),
        P("expert", None, "ray", None),
        P("expert", None, "ray"),
        P("expert", None, "ray"),
    )
    out_specs = (
        P(None, ("expert", "ray")),
        P("expert", None, "ray", None),
        P("expert", None, "ray"),
        P("expert", None, "ray"),
    )
    return jax.shard_map(local, mesh=mesh, in_specs=in_specs, out_specs=out_specs, check_vma=False)
```

profile of v0, /device:TPU:1, one launch (start us, length us, event | category | flops | bytes accessed | tf_op | source)
XLA Modules:
  0.0 512.6 jit_solution(13713376391407190017)
XLA Ops:
  7.2 0.7 fusion.42
  7.9 4.5 reduce-window.6
  12.5 0.4 slice_reduce_fusion
  12.9 0.2 reduce-window.9
  13.1 0.1 add_add_fusion
  13.2 0.8 fusion.41
  13.9 0.7 compare_select_fusion
  14.7 11.3 %scatter_custom_fusion = bf16[4096,256]{1,0:T(8,128)(2,1)} fusion(s32[2048]{0:T(1024)S(1)} %bitcast.161, bf16[2048,256]{1,0:T(8,128)(2,1)} %bitcast.169, bf16[]{:T(256)} %constant.14.clone.1), kind=kCustom, calls=%fused_computation.52 | custom fusion | bytes 2097664 | tf_op jit(solution)/shard_map/scatter | solution.py:57
  25.9 9.0 %all-to-all-start = ((bf16[8,2,256,256]{3,2,1,0:T(8,128)(2,1)}), bf16[8,2,256,256]{3,2,1,0:T(8,128)(2,1)S(1)}, u32[]{:S(2)}, u32[]{:S(2)}) async-start(bf16[8,2,256,256]{3,2,1,0:T(8,128)(2,1)} %bitcast.150), calls=%async_computation | async-start | bytes 4194304 | tf_op jit(solution)/shard_map/all_to_all | solution.py:65
  35.0 0.6 copy.58
  35.6 0.1 all-gather.2.cloned.1.call-update
  35.7 0.1 copy.59
  35.8 25.7 %all_gather.10 = bf16[2,4,256]{1,0,2:T(2,128)(2,1)S(1)} all-gather(bf16[2,4,8]{1,0,2:T(2,128)(2,1)S(1)} %copy.59), channel_id=1, replica_groups=mesh['expert'=8,'ray'=32] {'ray'}, dimensions={2}, use_global_device_ids=true | all-gather | bytes 4224 | tf_op jit(solution)/shard_map/all_gather | solution.py:62
  61.5 0.5 fusion.57
  62.0 0.1 copy.95
  62.1 0.1 copy.96
  62.2 0.1 copy.97
  62.3 0.1 copy.98
  62.4 0.1 copy.64
  62.5 24.1 %all_gather.11 = bf16[2,4,256]{1,0,2:T(2,128)(2,1)S(1)} all-gather(bf16[2,4,8]{1,0,2:T(2,128)(2,1)S(1)} %copy.64), channel_id=1, replica_groups=mesh['expert'=8,'ray'=32] {'ray'}, dimensions={2}, use_global_device_ids=true | all-gather | bytes 4224 | tf_op jit(solution)/shard_map/all_gather | solution.py:61
  86.7 0.1 copy.65
  86.8 1.3 copy-done.4
  88.1 1.7 copy.57
  89.9 4.7 multiply_convert_fusion.3
  94.6 3.5 multiply_convert_fusion.2
  98.1 3.5 multiply_convert_fusion.1
  101.6 3.5 multiply_convert_fusion
  105.1 1.3 copy-done
  106.5 0.6 convolution_convert_fusion
  107.1 0.6 copy.103
  107.8 6.9 %all-to-all-start.1 = ((bf16[2,4,8,256]{3,1,0,2:T(4,128)(2,1)}), bf16[2,4,8,256]{3,1,0,2:T(4,128)(2,1)S(1)}, u32[]{:S(2)}, u32[]{:S(2)}) async-start(bf16[2,4,8,256]{3,1,0,2:T(4,128)(2,1)} %bitcast.144), calls=%async_computation.1 | async-start | bytes 65536 | tf_op jit(solution)/shard_map/all_to_all | solution.py:69
  114.8 6.8 %all-to-all-done.1 = bf16[2,4,8,256]{3,1,0,2:T(4,128)(2,1)S(1)} async-done(((bf16[2,4,8,256]{3,1,0,2:T(4,128)(2,1)}), bf16[2,4,8,256]{3,1,0,2:T(4,128)(2,1)S(1)}, u32[]{:S(2)}, u32[]{:S(2)}) %all-to-all-start.1) | async-done | bytes 32800 | tf_op jit(solution)/shard_map/all_to_all | solution.py:69
  121.6 0.6 copy.67
  122.2 5.5 %gather_fusion = f32[2048,4]{1,0:T(8,128)S(1)} fusion(f32[4096,4]{1,0:T(8,128)S(1)} %bitcast.146, s32[2048]{0:T(1024)S(1)} %broadcast_clamp_fusion), kind=kCustom, calls=%fused_computation | custom fusion | bytes 73728 | tf_op jit(solution)/shard_map/gather | solution.py:77
  127.7 0.3 copy.83
  128.1 0.3 reduce_window_sum.36
  128.4 0.1 multiply_reduce_fusion.1
  128.5 0.1 fusion.43
  128.6 1.2 reduce_window_sum.37
  129.9 0.3 copy.84
  130.2 6.3 %scatter_custom_fusion.1 = bf16[4,4096]{0,1:T(8,128)(2,1)S(1)} fusion(s32[2048]{0:T(1024)S(1)} %bitcast.163, bf16[2048,4]{1,0:T(8,128)(2,1)S(1)} %bitcast.153, bf16[]{:T(256)} %constant.14.clone.1), kind=kCustom, calls=%fused_computation.54 | custom fusion | bytes 32770 | tf_op jit(solution)/shard_map/scatter | solution.py:82
  136.5 0.4 copy.70
  136.9 9.3 %all_to_all.35 = bf16[8,2,4,256]{3,2,1,0:T(4,128)(2,1)S(1)} all-to-all(bf16[8,2,4,256]{3,2,1,0:T(4,128)(2,1)S(1)} %bitcast.156), channel_id=1, replica_groups=mesh['expert'=8,'ray'=32] {'expert'}, dimensions={0} | all-to-all | bytes 65536 | tf_op jit(solution)/shard_map/all_to_all | solution.py:84
  146.3 5.0 convert_reduce_fusion
  151.4 3.3 convert_reduce_fusion.1
  154.7 3.3 convert_reduce_fusion.2
  158.0 3.3 convert_reduce_fusion.3
  161.3 1.7 fusion.58
  163.1 0.0 reduce-scatter.12.cloned.1.call-start
  163.2 3.3 fusion.59
  166.6 4.1 fusion.60
  170.7 4.0 fusion.61
  174.8 0.6 dynamic-slice
  176.0 0.4 fusion.62
  176.4 120.9 %all-reduce.7 = (f32[2,256]{1,0:T(2,128)S(1)}, f32[2,256]{1,0:T(2,128)S(1)}, f32[2,256]{1,0:T(2,128)S(1)}, f32[2,256]{1,0:T(2,128)S(1)}, f32[2,256,4]{1,2,0:T(4,128)S(1)}) all-reduce(f32[2,256]{1,0:T(2,128)S(1)} %get-tuple-element.39, f32[2,256]{1,0:T(2,128)S(1)} %get-tuple-element.41, ...), channel_id=9, replica_groups=mesh['expert'=8,'ray'=32] {'ray'}, use_global_device_ids=true, to_apply=%region_20.21.clone | all-reduce | flops 4096 | bytes 32768
  297.3 0.1 fusion.53
  297.3 0.1 fusion.55
  297.4 0.6 copy.78
  298.0 0.7 dynamic-slice_bitcast_fusion
  298.7 30.8 %reduce-scatter.12.cloned.1.call-done = f32[2,8,256]{2,1,0:T(8,128)} async-done(((f32[2,256,256]{2,1,0:T(8,128)}), f32[2,8,256]{2,1,0:T(8,128)}) %reduce-scatter.12.cloned.1.call-update) | async-done | bytes 16400 | tf_op jit(solution)/shard_map/reduce_scatter | solution.py:108
  329.4 87.6 %reduce-scatter.14.cloned.1.call-done = f32[2,8,256]{2,1,0:T(8,128)} async-done(((f32[2,256,256]{2,1,0:T(8,128)}), f32[2,8,256]{2,1,0:T(8,128)}) %reduce-scatter.14.cloned.1.call-update) | async-done | bytes 16400 | tf_op jit(solution)/shard_map/reduce_scatter | solution.py:108
  417.1 87.6 %reduce-scatter.16.cloned.1.call-done = f32[2,8,256]{2,1,0:T(8,128)} async-done(((f32[2,256,256]{2,1,0:T(8,128)}), f32[2,8,256]{2,1,0:T(8,128)}) %reduce-scatter.16.cloned.1.call-update) | async-done | bytes 16400 | tf_op jit(solution)/shard_map/reduce_scatter | solution.py:108
  504.7 0.8 pad_maximum_fusion
  505.5 0.6 copy.77
  (76 shorter events, 0.5 us)
Async XLA Ops:
  7.2 27.8 %copy-start.13 = (bf16[2,4,8,256]{3,2,1,0:T(8,128)(2,1)S(1)}, bf16[2,4,8,256]{3,2,1,0:T(8,128)(2,1)}, u32[]{:S(2)}) copy-start(bf16[2,4,8,256]{3,2,1,0:T(8,128)(2,1)} %param.13) | copy-start | bytes 98308
  7.2 28.5 %copy-start.16 = (bf16[2,4,8]{2,1,0:T(4,128)(2,1)S(1)}, bf16[2,4,8]{2,1,0:T(4,128)(2,1)}, u32[]{:S(2)}) copy-start(bf16[2,4,8]{2,1,0:T(4,128)(2,1)} %param.14) | copy-start | bytes 388
  13.2 49.3 %copy-start.17 = (bf16[2,4,8]{2,1,0:T(4,128)(2,1)S(1)}, bf16[2,4,8]{2,1,0:T(4,128)(2,1)}, u32[]{:S(2)}) copy-start(bf16[2,4,8]{2,1,0:T(4,128)(2,1)} %param.15) | copy-start | bytes 388
  25.9 60.8 %all-to-all-start = ((bf16[8,2,256,256]{3,2,1,0:T(8,128)(2,1)}), bf16[8,2,256,256]{3,2,1,0:T(8,128)(2,1)S(1)}, u32[]{:S(2)}, u32[]{:S(2)}) async-start(bf16[8,2,256,256]{3,2,1,0:T(8,128)(2,1)} %bitcast.150), calls=%async_computation | async-start | bytes 4194304 | tf_op jit(solution)/shard_map/all_to_all | solution.py:65
  35.0 54.9 %all-gather.2.cloned.1.call-start = ((), (), s32[]{:S(2)}) async-start(), calls=%async_computation.7 | async-start | bytes 1081344 | tf_op jit(solution)/shard_map/all_gather | solution.py:60
  86.8 1.3 copy-start.4
  89.9 4.7 copy-start.2
  89.9 4.7 copy-start.19
  94.6 3.5 copy-start.7
  98.1 3.5 copy-start.6
  101.6 3.5 copy-start.5
  101.6 13.1 %copy-start.15 = (bf16[16,128]{1,0:T(8,128)(2,1)S(1)}, bf16[16,128]{1,0:T(8,128)(2,1)}, u32[]{:S(2)}) copy-start(bf16[16,128]{1,0:T(8,128)(2,1)} %param.10) | copy-start | bytes 12292
  105.1 1.3 copy-start
  107.8 13.8 %all-to-all-start.1 = ((bf16[2,4,8,256]{3,1,0,2:T(4,128)(2,1)}), bf16[2,4,8,256]{3,1,0,2:T(4,128)(2,1)S(1)}, u32[]{:S(2)}, u32[]{:S(2)}) async-start(bf16[2,4,8,256]{3,1,0,2:T(4,128)(2,1)} %bitcast.144), calls=%async_computation.1 | async-start | bytes 65536 | tf_op jit(solution)/shard_map/all_to_all | solution.py:69
  114.7 184.0 %reduce-scatter.10.cloned.1.call-start = ((), (), s32[]{:S(2)}) async-start(), calls=%async_computation.8 | async-start | bytes 540672 | tf_op jit(solution)/shard_map/reduce_scatter | solution.py:108
  122.2 5.8 %copy-start.12 = (f32[16,128]{1,0:T(8,128)S(1)}, f32[16,128]{1,0:T(8,128)}, u32[]{:S(2)}) copy-start(f32[16,128]{1,0:T(8,128)} %param.11) | copy-start | bytes 24580
  122.2 6.3 %copy-start.18 = (f32[3,16]{1,0:T(4,128)S(1)}, f32[3,16]{1,0:T(4,128)}, u32[]{:S(2)}) copy-start(f32[3,16]{1,0:T(4,128)} %param.12) | copy-start | bytes 580
  128.5 22.9 %copy-start.14 = (f32[3,16]{1,0:T(4,128)}, f32[3,16]{1,0:T(4,128)S(1)}, u32[]{:S(2)}) copy-start(f32[3,16]{1,0:T(4,128)S(1)} %multiply_reduce_fusion.1) | copy-start | bytes 580
  146.3 5.1 copy-start.20
  146.3 5.1 copy-start.24
  151.4 3.3 copy-start.9
  151.4 3.3 copy-start.23
  154.7 3.3 copy-start.10
  154.7 3.3 copy-start.22
  158.0 3.3 copy-start.11
  158.0 3.3 copy-start.3
  161.3 1.8 copy-start.8
  163.1 166.4 %reduce-scatter.12.cloned.1.call-start = ((), (), s32[]{:S(2)}) async-start(), calls=%async_computation.9 | async-start | bytes 540672 | tf_op jit(solution)/shard_map/reduce_scatter | solution.py:108
  166.5 8.3 %copy-start.21 = (u32[256]{0:T(256)S(1)}, u32[256]{0:T(256)}, u32[]{:S(2)}) copy-start(u32[256]{0:T(256)} %constant.61) | copy-start | bytes 3076
  166.5 9.5 %copy-start.1 = (bf16[2,2048,256]{2,1,0:T(8,128)(2,1)S(1)}, bf16[2,2048,256]{2,1,0:T(8,128)(2,1)}, u32[]{:S(2)}) copy-start(bf16[2,2048,256]{2,1,0:T(8,128)(2,1)} %copy-done) | copy-start | bytes 6291460
  166.5 250.6 %reduce-scatter.14.cloned.1.call-start = ((), (), s32[]{:S(2)}) async-start(), calls=%async_computation.10 | async-start | bytes 540672 | tf_op jit(solution)/shard_map/reduce_scatter | solution.py:108
  170.7 334.0 %reduce-scatter.16.cloned.1.call-start = ((), (), s32[]{:S(2)}) async-start(), calls=%async_computation.11 | async-start | bytes 540672 | tf_op jit(solution)/shard_map/reduce_scatter | solution.py:108
Sparse Core Ops, SparseCore 0:
  38.8 50.4 all-gather.1
  163.2 78.4 reduce-scatter.9
  245.5 83.8 reduce-scatter.11
  333.0 83.9 reduce-scatter.13
  420.7 84.0 reduce-scatter.15
where the time goes:
time: 514 us; the launch traced here: 513 us
  waiting for transfers between devices  213 us (41%)
  blocking collectives  180 us (35%)
  matrix products  44.2 us (9%)
  local copies, waits for them, and re-layouts  34.8 us (7%)
  starting transfers between devices  16.1 us (3%)
  between operations  14.9 us (3%)
  other arithmetic  9.61 us (2%)
    reduce_scatter x4, waiting for transfers between devices, local(): lax.psum_scatter((grad_weight, grad_shift) + extra, 'ray', scatter_dimens...  206 us
    unnamed x1, blocking collectives  121 us
    all_gather x1, blocking collectives, local(): lax.all_gather(b_hidden, 'ray', axis=2, tiled=True)  25.7 us
    all_gather x1, blocking collectives, local(): lax.all_gather(w_head, 'ray', axis=2, tiled=True)  24.1 us
    dot_general x4, matrix products, expert_forward(): jnp.einsum('emd,edf->emf', hidden, layer_weights[:, layer], preferred_ele...  15.2 us
    dot_general x4, matrix products, local(): jnp.einsum('emd,emf->edf', activations[layer], grad_pre, preferred_elemen...  13.1 us
    scatter x1, local copies, waits for them, and re-layouts, local(): outgoing.at[slot_index].set(features.reshape(row_count, feat_width))  11.3 us
  transfers between devices with their start and end apart: 7, of which 4 were waited for; matrix products, arithmetic and copies ran while one was open for 3% of the time, Pallas kernels for 0%

commit v1 on v0

v1 whole, which is shorter than its diff:
```python
import jax
import jax.numpy as jnp
import numpy as np
from jax import lax
from jax.experimental import pallas as pl
from jax.experimental.pallas import tpu as pltpu
from jax.sharding import Mesh
from jax.sharding import PartitionSpec as P

BF = jnp.bfloat16
F32 = jnp.float32
I32 = jnp.int32
K0 = float(np.sqrt(2.0 / np.pi))
K1 = 0.044715
EXPERTS = 16
CAP = 256
ROWS = 2048
RAYS = 16
S = 128
D = 256
LAYERS = 4
CH = 72


def dot(a, b, dims, **kw):
    return lax.dot_general(a, b, (dims, ((), ())), preferred_element_type=F32, **kw)


def params(mb=48):
    return pltpu.CompilerParams(vmem_limit_bytes=mb * 2**20)


def prep_kernel(w_ref, b_ref, h_ref, out_ref):
    eye = (
        lax.broadcasted_iota(I32, (8, 128), 0) == lax.broadcasted_iota(I32, (8, 128), 1)
    ).astype(F32)
    for e in range(2):
        parts = []
        for l in range(LAYERS):
            rows = w_ref[e, l].astype(F32)
            parts += [rows[:, :128], rows[:, 128:]]
        extra = jnp.concatenate([b_ref[e].astype(F32), h_ref[e].astype(F32)], axis=0)
        parts.append(dot(extra.astype(BF), eye.astype(BF), ((0,), (0,))))
        out_ref[e] = jnp.concatenate(parts, axis=0).astype(BF)


def prep(w, b, h):
    return pl.pallas_call(
        prep_kernel, out_shape=jax.ShapeDtypeStruct((2, CH, 128), BF), compiler_params=params()
    )(w, b, h)


def pack_kernel(route_ref, x_ref, out_ref, slot_ref):
    @pl.when(pl.program_id(0) == 0)
    def _():
        route = route_ref[...]
        member = jnp.concatenate([(route == e).astype(F32) for e in range(EXPERTS)], axis=0)
        member16 = member.astype(BF)
        row = lax.broadcasted_iota(I32, (256, 256), 0)
        col = lax.broadcasted_iota(I32, (256, 256), 1)
        before = ((row // RAYS == col // RAYS) & (col < row)).astype(BF)
        lane_r = lax.broadcasted_iota(I32, (128, 128), 0)
        lane_c = lax.broadcasted_iota(I32, (128, 128), 1)
        upto = (lane_r <= lane_c).astype(BF)
        within = dot(member16, upto, ((1,), (0,)))
        earlier = dot(before, member16, ((1,), (0,)))
        earlier = dot(earlier.astype(BF), jnp.ones((128, 128), BF), ((1,), (0,)))
        rank = within + earlier - 1.0
        slot = jnp.zeros((RAYS, S), F32)
        for e in range(EXPERTS):
            part = slice(e * RAYS, (e + 1) * RAYS)
            slot = slot + member[part] * (rank[part] + float(e * CAP))
        slot_ref[...] = slot.astype(I32)

    step = pl.program_id(0)
    place = lax.broadcasted_iota(I32, (CAP, S), 0)
    for half in range(2):
        base = (step * 2 + half) * CAP
        hot = jnp.concatenate(
            [
                jnp.where(slot_ref[j : j + 1, :] - base == place, 1.0, 0.0).astype(BF)
                for j in range(RAYS)
            ],
            axis=1,
        )
        out_ref[half] = dot(hot, x_ref[...], ((1,), (0,))).astype(BF)


def pack(route, x):
    return pl.pallas_call(
        pack_kernel,
        grid=(8,),
        in_specs=[
            pl.BlockSpec((RAYS, S), lambda i: (0, 0)),
            pl.BlockSpec((ROWS, D), lambda i: (0, 0)),
        ],
        out_specs=[
            pl.BlockSpec((2, CAP, D), lambda i: (i, 0, 0)),
            pl.BlockSpec((RAYS, S), lambda i: (0, 0)),
        ],
        out_shape=[
            jax.ShapeDtypeStruct((EXPERTS, CAP, D), BF),
            jax.ShapeDtypeStruct((RAYS, S), I32),
        ],
        compiler_params=params(),
    )(route, x)


def forward_kernel(core_ref, g_ref, x_ref, h_ref, slope_ref, out_ref, w_ref, v_ref):
    @pl.when(pl.program_id(0) == 0)
    def _():
        for l in range(LAYERS):
            for half in range(2):
                at = (l * 2 + half) * 8
                part = g_ref[:, 0, at : at + 8, :].astype(F32).reshape(D, 128)
                w_ref[l, :, half * 128 : half * 128 + 128] = part.astype(BF)
        extra = g_ref[:, 0, 64:72, :].astype(F32).reshape(D, 128)
        v_ref[...] = extra.T[0:8]

    hidden = x_ref[...].reshape(2 * CAP, D)
    for l in range(LAYERS):
        pre = dot(hidden, w_ref[l], ((1,), (0,))) + v_ref[l : l + 1, :]
        square = pre * pre
        t = jnp.tanh(pre * (K0 + (K0 * K1) * square))
        cdf = 0.5 + 0.5 * t
        value = pre * cdf
        slope_ref[l] = cdf + value * (1.0 - t) * (K0 + (3.0 * K0 * K1) * square)
        hidden = value.astype(BF)
        h_ref[l] = hidden
    out = dot(v_ref[...].astype(BF), hidden, ((1,), (1,))).astype(BF).astype(F32)
    for s in range(2):
        at = s * CAP
        out_ref[s, 0:4, :] = out[4:8, at : at + 128]
        out_ref[s, 4:8, :] = out[4:8, at + 128 : at + 256]


def forward(core, gathered, x):
    return pl.pallas_call(
        forward_kernel,
        grid_spec=pltpu.PrefetchScalarGridSpec(
            num_scalar_prefetch=1,
            grid=(8,),
            in_specs=[
                pl.BlockSpec((32, 1, CH, 128), lambda i, c: (0, c[0], 0, 0)),
                pl.BlockSpec((2, CAP, D), lambda i, c: (i, 0, 0)),
            ],
            out_specs=[
                pl.BlockSpec((LAYERS, 2 * CAP, D), lambda i, c: (0, i, 0)),
                pl.BlockSpec((LAYERS, 2 * CAP, D), lambda i, c: (0, i, 0)),
                pl.BlockSpec((2, 8, 128), lambda i, c: (i, 0, 0)),
                pl.BlockSpec((LAYERS, D, D), lambda i, c: (0, 0, 0)),
                pl.BlockSpec((8, D), lambda i, c: (0, 0)),
            ],
        ),
        out_shape=[
            jax.ShapeDtypeStruct((LAYERS, EXPERTS * CAP, D), BF),
            jax.ShapeDtypeStruct((LAYERS, EXPERTS * CAP, D), F32),
            jax.ShapeDtypeStruct((EXPERTS, 8, 128), F32),
            jax.ShapeDtypeStruct((LAYERS, D, D), BF),
            jax.ShapeDtypeStruct((8, D), F32),
        ],
        compiler_params=params(),
    )(core, gathered, x)


def composite_kernel(table_ref, slot_ref, gate_ref, delta_ref, target_ref, rend_ref, cot_ref):
    table = jnp.concatenate(
        [
            jnp.concatenate([table_ref[:, c, :], table_ref[:, 4 + c, :]], axis=1)
            for c in range(4)
        ],
        axis=0,
    ).astype(BF)
    slot = slot_ref[...]
    place = lax.broadcasted_iota(I32, (CAP, S), 0)
    expert = lax.broadcasted_iota(I32, (EXPERTS, S), 0)
    hots, members, rows = [], [], []
    for j in range(RAYS):
        at = slot[j : j + 1, :]
        hot = jnp.where((at & (CAP - 1)) == place, 1.0, 0.0).astype(BF)
        member = jnp.where(lax.shift_right_logical(at, 8) == expert, 1.0, 0.0)
        found = dot(table, hot, ((1,), (0,)))
        rows.append(
            [
                jnp.sum(found[c * 16 : c * 16 + 16] * member, axis=0, keepdims=True)
                for c in range(4)
            ]
        )
        hots.append(hot)
        members.append(member)
    raw = [jnp.concatenate([rows[j][c] for j in range(RAYS)], axis=0) for c in range(4)]
    gate = gate_ref[...].astype(F32)
    delta = delta_ref[...]
    gated = [gate * r for r in raw]
    lane_r = lax.broadcasted_iota(I32, (128, 128), 0)
    lane_c = lax.broadcasted_iota(I32, (128, 128), 1)
    earlier = (lane_r < lane_c).astype(F32)
    later = (lane_r > lane_c).astype(F32)
    g0 = gated[0]
    density = jnp.maximum(g0, 0.0) + jnp.log1p(jnp.exp(-jnp.abs(g0)))
    radiance = [jax.nn.sigmoid(g) for g in gated[1:]]
    optical = density * delta
    before = dot(optical, earlier, ((1,), (0,)), precision=lax.Precision.HIGHEST)
    reach = jnp.exp(-before)
    passed = jnp.exp(-optical)
    weight = reach * (1.0 - passed)
    eye = lax.broadcasted_iota(I32, (RAYS, RAYS), 0) == lax.broadcasted_iota(I32, (RAYS, RAYS), 1)
    q = jnp.zeros((RAYS, S), F32)
    grads = [None]
    for c in range(3):
        rendered = jnp.sum(weight * radiance[c], axis=1, keepdims=True)
        goal = jnp.sum(jnp.where(eye, target_ref[c : c + 1, :], 0.0), axis=1, keepdims=True)
        rend_ref[c : c + 1, :] = jnp.sum(jnp.where(eye, rendered, 0.0), axis=0, keepdims=True)
        diff = rendered - goal
        q = q + diff * radiance[c]
        grads.append(diff * weight * radiance[c] * (1.0 - radiance[c]))
    push = dot(q * weight, later, ((1,), (0,)), precision=lax.Precision.HIGHEST)
    grads[0] = (q * reach * passed - push) * delta * jax.nn.sigmoid(g0)
    cots = [(gate * g).astype(BF).astype(F32) for g in grads]
    total = jnp.zeros((64, CAP), F32)
    for j in range(RAYS):
        spread = jnp.concatenate([cots[c][j : j + 1, :] * members[j] for c in range(4)], axis=0)
        total = total + dot(spread.astype(BF), hots[j], ((1,), (1,)))
    for c in range(4):
        cot_ref[:, c, :] = total[c * 16 : c * 16 + 16, :128]
        cot_ref[:, 4 + c, :] = total[c * 16 : c * 16 + 16, 128:]


def composite(table, slot, gate, delta, target):
    return pl.pallas_call(
        composite_kernel,
        out_shape=[
            jax.ShapeDtypeStruct((3, RAYS), F32),
            jax.ShapeDtypeStruct((EXPERTS, 8, 128), F32),
        ],
        compiler_params=params(),
    )(table, slot, gate, delta, target)


def backward_kernel(cot_ref, x_ref, h_ref, slope_ref, w_ref, v_ref, out_ref, gw_ref, gv_ref):
    step = pl.program_id(0)

    @pl.when(step == 0)
    def _():
        gw_ref[...] = jnp.zeros_like(gw_ref)
        gv_ref[...] = jnp.zeros_like(gv_ref)

    cot = jnp.concatenate(
        [cot_ref[0, 0:4], cot_ref[0, 4:8], cot_ref[1, 0:4], cot_ref[1, 4:8]], axis=1
    ).astype(BF)
    head = v_ref[4:8, :].astype(BF)
    gv_ref[4:8, :] += dot(cot, h_ref[LAYERS - 1], ((1,), (0,)))
    grad = dot(cot, head, ((0,), (0,)))
    ones = jnp.ones((8, 2 * CAP), BF)
    for l in range(LAYERS - 1, -1, -1):
        grad_pre = (grad * slope_ref[l]).astype(BF)
        below = h_ref[l - 1] if l > 0 else x_ref[...].reshape(2 * CAP, D)
        gw_ref[l] += dot(below, grad_pre, ((0,), (0,)))
        gv_ref[l : l + 1, :] += dot(ones, grad_pre, ((1,), (0,)))[0:1]
        if l > 0:
            grad = dot(grad_pre, w_ref[l], ((1,), (1,)))

    @pl.when(step == pl.num_programs(0) - 1)
    def _():
        for l in range(LAYERS):
            for half in range(2):
                at = (l * 2 + half) * 8
                part = gw_ref[l, :, half * 128 : half * 128 + 128]
                out_ref[:, at : at + 8, :] = part.reshape(32, 8, 128)
        extra = jnp.concatenate([gv_ref[...], jnp.zeros((120, D), F32)], axis=0)
        out_ref[:, 64:72, :] = extra.T.reshape(32, 8, 128)


def backward(cot, x, h, slope, w, v):
    return pl.pallas_call(
        backward_kernel,
        grid=(8,),
        in_specs=[
            pl.BlockSpec((2, 8, 128), lambda i: (i, 0, 0)),
            pl.BlockSpec((2, CAP, D), lambda i: (i, 0, 0)),
            pl.BlockSpec((LAYERS, 2 * CAP, D), lambda i: (0, i, 0)),
            pl.BlockSpec((LAYERS, 2 * CAP, D), lambda i: (0, i, 0)),
            pl.BlockSpec((LAYERS, D, D), lambda i: (0, 0, 0)),
            pl.BlockSpec((8, D), lambda i: (0, 0)),
        ],
        out_specs=pl.BlockSpec((32, CH, 128), lambda i: (0, 0, 0)),
        out_shape=jax.ShapeDtypeStruct((32, CH, 128), F32),
        scratch_shapes=[pltpu.VMEM((LAYERS, D, D), F32), pltpu.VMEM((8, D), F32)],
        compiler_params=params(),
    )(cot, x, h, slope, w, v)


def finish_kernel(parts_ref, gw_ref, gb_ref, gh_ref):
    for e in range(2):
        total = parts_ref[0, e]
        for j in range(1, 16):
            total = total + parts_ref[j, e]
        for l in range(LAYERS):
            at = l * 16
            gw_ref[e, l] = jnp.concatenate([total[at : at + 8], total[at + 8 : at + 16]], axis=1)
        extra = jnp.concatenate([total[64:72], jnp.zeros((120, 128), F32)], axis=0).T
        gb_ref[e] = extra[0:4, 0:8]
        gh_ref[e] = extra[4:8, 0:8]


def finish(parts):
    return pl.pallas_call(
        finish_kernel,
        out_shape=[
            jax.ShapeDtypeStruct((2, LAYERS, 8, D), F32),
            jax.ShapeDtypeStruct((2, LAYERS, 8), F32),
            jax.ShapeDtypeStruct((2, 4, 8), F32),
        ],
        compiler_params=params(),
    )(parts)


def local(features, routes, gate_values, deltas, target, w_hidden, b_hidden, w_head):
    core = lax.axis_index("c").astype(I32).reshape(1)
    shard = prep(w_hidden, b_hidden, w_head)
    gathered = lax.all_gather(shard, ("xy", "c"), axis=0, tiled=False)
    outgoing, slot = pack(routes.reshape(RAYS, S), features.reshape(ROWS, D))
    received = lax.all_to_all(outgoing, ("z", "c"), 0, 0, tiled=True)
    h, slope, out, w, v = forward(core, gathered, received)
    table = lax.all_to_all(out, ("z", "c"), 0, 0, tiled=True)
    rendered, cot = composite(table, slot, gate_values, deltas, target)
    cot = lax.all_to_all(cot, ("z", "c"), 0, 0, tiled=True)
    grads = backward(cot, received, h, slope, w, v)
    parts = lax.all_to_all(grads, ("xy", "c"), 0, 0, tiled=True)
    grad_w, grad_b, grad_h = finish(parts.reshape(16, 2, CH, 128))
    return rendered, grad_w, grad_b, grad_h


def solution(mesh):
    split = Mesh(mesh.devices.reshape(8, 16, 2), ("z", "xy", "c"))
    every = ("z", "xy", "c")
    ray = ("xy", "c")
    in_specs = (
        P(every, None, None),
        P(every, None, None),
        P(every, None),
        P(every, None),
        P(None, every),
        P("z", None, ray, None),
        P("z", None, ray),
        P("z", None, ray),
    )
    out_specs = (P(None, every), P("z", None, ray, None), P("z", None, ray), P("z", None, ray))
    return jax.shard_map(local, mesh=split, in_specs=in_specs, out_specs=out_specs, check_vma=False)
```

time: 514 us -> 169 us (0.33)
  waiting for transfers between devices: 213 us -> 52.6 us
  blocking collectives: 180 us -> 49.1 us
  matrix products: 44.2 us -> 0 us
  Pallas kernels: 0 us -> 37.7 us
  local copies, waits for them, and re-layouts: 34.8 us -> 4.54 us
  other arithmetic: 9.61 us -> 0 us
  starting transfers between devices: 16.1 us -> 10.2 us
    reduce_scatter x4 -> x0, waiting for transfers between devices: 206 us -> none  [local(): lax.psum_scatter((grad_weight, grad_shift) + extra, 'ray', scatter_dimens...]
    unnamed x1 -> x0, blocking collectives: 121 us -> none
    all_gather x1, waiting for transfers between devices: 0.02 us -> 52.6 us  [local(): gathered = lax.all_gather(shard, ('xy', 'c'), axis=0, tiled=False)]
    all_gather x2 -> x0, blocking collectives: 49.8 us -> none  [the longest x1 25.7 us: local(): lax.all_gather(b_hidden, 'ray', axis=2, tiled=True)]
    dot_general x14 -> x0, matrix products: 44.2 us -> none  [the longest x4 15.2 us: expert_forward(): jnp.einsum('emd,edf->emf', hidden, layer_weights[:, layer], preferred_ele...]
    all_to_all x1 -> x3, blocking collectives: 9.34 us -> 49.1 us  [the longest x1 23.9 us: local(): parts = lax.all_to_all(grads, ('xy', 'c'), 0, 0, tiled=True)]
    pallas_call x0 -> x6, Pallas kernels: none -> 37.7 us  [the longest x1 15.1 us: backward(): pl.pallas_call(backward_kernel, grid=(8,), in_specs=[pl.BlockSpec((2, 8,...]
    scatter x2 -> x0, local copies, waits for them, and re-layouts: 17.6 us -> none  [the longest x1 11.3 us: local(): outgoing.at[slot_index].set(features.reshape(row_count, feat_width))]
  transfers between devices with their start and end apart: 7 -> 2, of which waited for: 4 -> 1; matrix products, arithmetic and copies ran while one was open for 3% -> 0% of each run, Pallas kernels for 0% -> 0%
where the time goes in v1:
time: 169 us; the launch traced here: 168 us
  waiting for transfers between devices  52.6 us (31%)
  blocking collectives  49.1 us (29%)
  Pallas kernels  37.7 us (22%)
  between operations  14.1 us (8%)
  starting transfers between devices  10.2 us (6%)
  local copies, waits for them, and re-layouts  4.54 us (3%)
    all_gather x1, waiting for transfers between devices, local(): gathered = lax.all_gather(shard, ('xy', 'c'), axis=0, tiled=False)  52.6 us
    all_to_all x1, blocking collectives, local(): parts = lax.all_to_all(grads, ('xy', 'c'), 0, 0, tiled=True)  23.9 us
    pallas_call x1, Pallas kernels, backward(): pl.pallas_call(backward_kernel, grid=(8,), in_specs=[pl.BlockSpec((2, 8,...  15.1 us
    all_to_all x1, blocking collectives, local(): table = lax.all_to_all(out, ('z', 'c'), 0, 0, tiled=True)  14.8 us
    pallas_call x1, Pallas kernels, forward(): pl.pallas_call(forward_kernel, grid_spec=pltpu.PrefetchScalarGridSpec(num...  13.5 us
    all_to_all x1, blocking collectives, local(): cot = lax.all_to_all(cot, ('z', 'c'), 0, 0, tiled=True)  10.4 us
    all_to_all x1, starting transfers between devices, local(): received = lax.all_to_all(outgoing, ('z', 'c'), 0, 0, tiled=True)  10.1 us
    pallas_call x1, Pallas kernels, pack(): pl.pallas_call(pack_kernel, grid=(8,), in_specs=[pl.BlockSpec((RAYS, S),...  6.07 us
  transfers between devices with their start and end apart: 2, of which 1 were waited for; matrix products, arithmetic and copies ran while one was open for 0% of the time, Pallas kernels for 0%

profile of v1, /device:TPU:1, one launch (start us, length us, event | category | flops | bytes accessed | tf_op | source)
XLA Modules:
  0.0 168.2 jit_solution(6841765349846941105)
XLA Ops:
  7.2 0.0 copy-start.2
  7.2 1.2 copy-done.2
  8.4 0.0 copy-start.4
  8.4 0.7 copy-done.4
  9.1 6.1 %shard_map.112 = (bf16[16,256,256]{2,1,0:T(8,128)(2,1)S(1)}, s32[16,128]{1,0:T(8,128)S(1)}) custom-call(s32[16,128]{1,0:T(8,128)S(1)} %bitcast.8, bf16[2048,256]{1,0:T(8,128)(2,1)S(1)} %bitcast.7), custom_call_target="tpu_custom_call" | custom-call | tf_op jit(solution)/shard_map/pallas_call | solution.py:90
  15.2 0.0 copy-start
  15.2 1.3 copy-done
  16.5 0.0 copy-start.3
  16.5 0.0 copy-start.7
  16.5 0.0 copy-start.8
  16.5 10.1 %all-to-all-start = ((bf16[16,256,256]{2,1,0:T(8,128)(2,1)}), bf16[16,256,256]{2,1,0:T(8,128)(2,1)S(1)}, u32[]{:S(2)}, u32[]{:S(2)}) async-start(bf16[16,256,256]{2,1,0:T(8,128)(2,1)} %copy-done), calls=%async_computation | async-start | bytes 4194304 | tf_op jit(solution)/shard_map/all_to_all | solution.py:323
  26.6 0.0 copy-start.5
  26.6 0.0 copy-start.6
  26.6 0.0 copy-start.9
  26.7 0.0 all-gather.3.cloned.1.call-start
  26.7 0.0 copy-done.3
  26.7 0.0 copy-done.7
  26.7 0.0 copy-done.8
  26.7 0.8 shard_map.111
  27.5 0.0 all-gather.3.cloned.1.call-update
  27.6 52.6 %all-gather.3.cloned.1.call-done = bf16[64,72,128]{2,1,0:T(8,128)(2,1)} async-done(((bf16[2,72,128]{2,1,0:T(8,128)(2,1)}), bf16[64,72,128]{2,1,0:T(8,128)(2,1)}) %all-gather.3.cloned.1.call-update) | async-done | bytes 1179664 | tf_op jit(solution)/shard_map/all_gather | solution.py:321
  80.2 0.0 all-to-all-done.x_ref
  80.2 0.0 copy-start.1
  80.2 1.3 copy-done.1
  81.4 13.5 %shard_map.113 = (bf16[4,4096,256]{2,1,0:T(8,128)(2,1)}, f32[4,4096,256]{2,1,0:T(8,128)}, f32[16,8,128]{2,1,0:T(8,128)S(1)}, bf16[4,256,256]{2,1,0:T(8,128)(2,1)S(1)}, f32[8,256]{1,0:T(8,128)S(1)}) custom-call(s32[1]{0:T(128)} %bitcast.core_ref, bf16[32,2,72,128]{3,2,1,0:T(8,128)(2,1)S(1)} %bitcast.6, bf16[16,256,256]{2,1,0:T(8,128)(2,1)S(1)} %all-to-all-done.x_ref), custom_call_target="tpu_custom_call" | custom-call | tf_op jit(solution)/shard_map/pallas_call | solution.py:138
  94.9 14.8 %all_to_all.20.table_ref = f32[16,8,128]{2,1,0:T(8,128)S(1)} all-to-all(f32[16,8,128]{2,1,0:T(8,128)S(1)} %get-tuple-element.17), channel_id=1, replica_groups=mesh['z'=8,'xy'=16,'c'=2] {'z','c'}, dimensions={0} | all-to-all | bytes 131072 | tf_op jit(solution)/shard_map/all_to_all | solution.py:325
  109.7 0.0 copy-done.5
  109.8 0.0 copy-done.6
  109.8 0.0 copy-done.9
  109.8 1.5 shard_map.114
  111.3 10.4 %all_to_all.21.cot_ref = f32[16,8,128]{2,1,0:T(8,128)S(1)} all-to-all(f32[16,8,128]{2,1,0:T(8,128)S(1)} %get-tuple-element.20), channel_id=1, replica_groups=mesh['z'=8,'xy'=16,'c'=2] {'z','c'}, dimensions={0} | all-to-all | bytes 131072 | tf_op jit(solution)/shard_map/all_to_all | solution.py:327
  121.7 15.1 %shard_map.115 = f32[32,72,128]{2,1,0:T(8,128)S(1)} custom-call(f32[16,8,128]{2,1,0:T(8,128)S(1)} %all_to_all.21.cot_ref, bf16[16,256,256]{2,1,0:T(8,128)(2,1)S(1)} %all-to-all-done.x_ref, bf16[4,4096,256]{2,1,0:T(8,128)(2,1)} %get-tuple-element.21.h_ref, f32[4,4096,256]{2,1,0:T(8,128)} %get-tuple-element.22.slope_ref, ...), custom_call_target="tpu_custom_call" | custom-call | tf_op jit(solution)/shard_map/pallas_call | solution.py:275
  136.8 23.9 %all_to_all.22 = f32[32,72,128]{2,1,0:T(8,128)S(1)} all-to-all(f32[32,72,128]{2,1,0:T(8,128)S(1)} %shard_map.115), channel_id=1, replica_groups=mesh['z'=8,'xy'=16,'c'=2] {'xy','c'}, dimensions={0} | all-to-all | bytes 2359296 | tf_op jit(solution)/shard_map/all_to_all | solution.py:329
  160.7 0.7 shard_map.116
Async XLA Ops:
  7.2 1.2 copy-start.2
  8.4 0.7 copy-start.4
  15.2 1.3 copy-start
  16.5 10.2 %copy-start.3 = (bf16[2,4,8,256]{3,2,1,0:T(8,128)(2,1)S(1)}, bf16[2,4,8,256]{3,2,1,0:T(8,128)(2,1)}, u32[]{:S(2)}) copy-start(bf16[2,4,8,256]{3,2,1,0:T(8,128)(2,1)} %w_ref.1) | copy-start | bytes 98308
  16.5 10.2 %copy-start.7 = (bf16[2,4,8]{2,1,0:T(4,128)(2,1)S(1)}, bf16[2,4,8]{2,1,0:T(4,128)(2,1)}, u32[]{:S(2)}) copy-start(bf16[2,4,8]{2,1,0:T(4,128)(2,1)} %b_ref.1) | copy-start | bytes 388
  16.5 10.2 %copy-start.8 = (bf16[2,4,8]{2,1,0:T(4,128)(2,1)S(1)}, bf16[2,4,8]{2,1,0:T(4,128)(2,1)}, u32[]{:S(2)}) copy-start(bf16[2,4,8]{2,1,0:T(4,128)(2,1)} %h_ref.1) | copy-start | bytes 388
  16.5 63.7 %all-to-all-start = ((bf16[16,256,256]{2,1,0:T(8,128)(2,1)}), bf16[16,256,256]{2,1,0:T(8,128)(2,1)S(1)}, u32[]{:S(2)}, u32[]{:S(2)}) async-start(bf16[16,256,256]{2,1,0:T(8,128)(2,1)} %copy-done), calls=%async_computation | async-start | bytes 4194304 | tf_op jit(solution)/shard_map/all_to_all | solution.py:323
  26.6 83.1 %copy-start.5 = (f32[16,128]{1,0:T(8,128)S(1)}, f32[16,128]{1,0:T(8,128)}, u32[]{:S(2)}) copy-start(f32[16,128]{1,0:T(8,128)} %delta_ref.1) | copy-start | bytes 24580
  26.6 83.1 %copy-start.6 = (bf16[16,128]{1,0:T(8,128)(2,1)S(1)}, bf16[16,128]{1,0:T(8,128)(2,1)}, u32[]{:S(2)}) copy-start(bf16[16,128]{1,0:T(8,128)(2,1)} %gate_ref.1) | copy-start | bytes 12292
  26.6 83.1 %copy-start.9 = (f32[3,16]{1,0:T(4,128)S(1)}, f32[3,16]{1,0:T(4,128)}, u32[]{:S(2)}) copy-start(f32[3,16]{1,0:T(4,128)} %target_ref.1) | copy-start | bytes 580
  26.7 53.5 %all-gather.3.cloned.1.call-start = ((), (), s32[]{:S(2)}) async-start(), calls=%async_computation.4 | async-start | bytes 1216512 | tf_op jit(solution)/shard_map/all_gather | solution.py:321
  80.2 1.3 copy-start.1
Sparse Core Ops, SparseCore 0:
  30.7 49.4 all-gather.2

commit v2 on v1

v2 whole, which is shorter than its diff:
```python
from functools import partial

import jax
import jax.numpy as jnp
import numpy as np
from jax import lax
from jax.experimental import pallas as pl
from jax.experimental.pallas import tpu as pltpu
from jax.sharding import Mesh
from jax.sharding import PartitionSpec as P

BF = jnp.bfloat16
F32 = jnp.float32
I32 = jnp.int32
K0 = float(np.sqrt(2.0 / np.pi))
K1 = 0.044715
EXPERTS = 16
CAP = 256
ROWS = 2048
RAYS = 16
S = 128
D = 256
LAYERS = 4
SHIFTS = (0, 1, -1, 3, -3, 4, 2, -2)
GROUPS = ((0, 3), (3, 3), (6, 2))
CH = 72


def dot(a, b, dims, **kw):
    return lax.dot_general(a, b, (dims, ((), ())), preferred_element_type=F32, **kw)


def params(mb=16):
    return pltpu.CompilerParams(vmem_limit_bytes=mb * 2**20)


def prep_kernel(w_ref, b_ref, h_ref, out_ref):
    eye = lax.broadcasted_iota(I32, (8, 128), 0) == lax.broadcasted_iota(I32, (8, 128), 1)
    for e in range(2):
        parts = []
        for l in range(LAYERS):
            rows = w_ref[e, l].astype(F32)
            parts += [rows[:, :128], rows[:, 128:]]
        extra = jnp.concatenate([b_ref[e].astype(F32), h_ref[e].astype(F32)], axis=0)
        parts.append(dot(extra.astype(BF), eye.astype(F32).astype(BF), ((0,), (0,))))
        whole = jnp.concatenate(parts, axis=0).astype(BF)
        for d in range(32):
            out_ref[d, e] = whole


def prep(w, b, h):
    return pl.pallas_call(
        prep_kernel, out_shape=jax.ShapeDtypeStruct((32, 2, CH, 128), BF), compiler_params=params()
    )(w, b, h)


def unpack_kernel(g_ref, w_ref, v_ref):
    for e in range(2):
        for l in range(LAYERS):
            for half in range(2):
                at = (l * 2 + half) * 8
                part = g_ref[:, e, at : at + 8, :].astype(F32).reshape(D, 128)
                w_ref[e, l, :, half * 128 : half * 128 + 128] = part.astype(BF)
        extra = g_ref[:, e, 64:72, :].astype(F32).reshape(D, 128)
        v_ref[e] = extra.T[0:8]


def unpack(gathered):
    return pl.pallas_call(
        unpack_kernel,
        out_shape=[
            jax.ShapeDtypeStruct((2, LAYERS, D, D), BF),
            jax.ShapeDtypeStruct((2, 8, D), F32),
        ],
        compiler_params=params(),
    )(gathered)


def slots_of(route):
    member = jnp.concatenate([(route == e).astype(F32) for e in range(EXPERTS)], axis=0)
    member16 = member.astype(BF)
    row = lax.broadcasted_iota(I32, (256, 256), 0)
    col = lax.broadcasted_iota(I32, (256, 256), 1)
    before = ((row // RAYS == col // RAYS) & (col < row)).astype(F32).astype(BF)
    lane_r = lax.broadcasted_iota(I32, (128, 128), 0)
    lane_c = lax.broadcasted_iota(I32, (128, 128), 1)
    upto = (lane_r <= lane_c).astype(F32).astype(BF)
    within = dot(member16, upto, ((1,), (0,)))
    earlier = dot(before, member16, ((1,), (0,)))
    earlier = dot(earlier.astype(BF), jnp.ones((128, 128), BF), ((1,), (0,)))
    rank = within + earlier - 1.0
    slot = jnp.zeros((RAYS, S), F32)
    for e in range(EXPERTS):
        part = slice(e * RAYS, (e + 1) * RAYS)
        slot = slot + member[part] * (rank[part] + float(e * CAP))
    return slot.astype(I32)


def pack_block(plane, slot_ref, x_ref, out_ref):
    place = lax.broadcasted_iota(I32, (CAP, S), 0)
    for half in range(2):
        base = (plane * 2 + half) * CAP
        hot = jnp.concatenate(
            [
                jnp.where(slot_ref[j : j + 1, :] - base == place, 1.0, 0.0).astype(BF)
                for j in range(RAYS)
            ],
            axis=1,
        )
        out_ref[half] = dot(hot, x_ref[...], ((1,), (0,))).astype(BF)


def pack_kernel(shifts, first, *refs):
    if first:
        route_ref, x_ref, *out_refs, slot_ref = refs
        slot_ref[...] = slots_of(route_ref[...])
    else:
        slot_ref, x_ref, *out_refs = refs
    plane = lax.axis_index("z")
    for k, out_ref in zip(shifts, out_refs):
        pack_block((plane + (k & 7)) & 7, slot_ref, x_ref, out_ref)


def pack(shifts, first, route, x):
    out_shape = [jax.ShapeDtypeStruct((2, CAP, D), BF) for _ in shifts]
    if first:
        out_shape.append(jax.ShapeDtypeStruct((RAYS, S), I32))
    return pl.pallas_call(
        partial(pack_kernel, shifts, first), out_shape=out_shape, compiler_params=params()
    )(route, x)


def forward_kernel(n, olds_n, where_ref, *refs):
    x_refs, (w_ref, v_ref), refs = refs[:n], refs[n : n + 2], refs[n + 2 :]
    olds, (h_ref, slope_ref, out_ref) = refs[:olds_n], refs[olds_n:]
    hidden = [jnp.concatenate([r[e] for r in x_refs], axis=0) for e in range(2)]
    for l in range(LAYERS):
        for e in range(2):
            pre = dot(hidden[e], w_ref[e, l], ((1,), (0,))) + v_ref[e, l : l + 1, :]
            square = pre * pre
            t = jnp.tanh(pre * (K0 + (K0 * K1) * square))
            cdf = 0.5 + 0.5 * t
            value = pre * cdf
            slope_ref[e, l] = cdf + value * (1.0 - t) * (K0 + (3.0 * K0 * K1) * square)
            hidden[e] = value.astype(BF)
            h_ref[e, l] = hidden[e]
    at = 0
    for old in olds:
        for i in range(old.shape[0]):
            out_ref[where_ref[at]] = old[i]
            at += 1
    for e in range(2):
        out = dot(v_ref[e].astype(BF), hidden[e], ((1,), (1,))).astype(BF).astype(F32)
        for i in range(n):
            lo = i * CAP
            one = jnp.concatenate(
                [out[4:8, lo : lo + 128], out[4:8, lo + 128 : lo + CAP]], axis=0
            )
            if olds_n:
                out_ref[where_ref[at + i], e] = one
            else:
                out_ref[i, e] = one


def forward(where, xs, w, v, olds):
    n = len(xs)
    vmem = pl.BlockSpec(memory_space=pltpu.VMEM)
    return pl.pallas_call(
        partial(forward_kernel, n, len(olds)),
        in_specs=[pl.BlockSpec(memory_space=pltpu.SMEM)] + [vmem] * (n + 2 + len(olds)),
        out_shape=[
            jax.ShapeDtypeStruct((2, LAYERS, n * CAP, D), BF),
            jax.ShapeDtypeStruct((2, LAYERS, n * CAP, D), F32),
            jax.ShapeDtypeStruct((8 if olds else n, 2, 8, 128), F32),
        ],
        compiler_params=params(),
    )(where, *xs, w, v, *olds)


def composite_kernel(table_ref, slot_ref, gate_ref, delta_ref, target_ref, rend_ref, cot_ref):
    table = jnp.concatenate(
        [
            jnp.concatenate([table_ref[:, c, :], table_ref[:, 4 + c, :]], axis=1)
            for c in range(4)
        ],
        axis=0,
    ).astype(BF)
    slot = slot_ref[...]
    place = lax.broadcasted_iota(I32, (CAP, S), 0)
    expert = lax.broadcasted_iota(I32, (EXPERTS, S), 0)
    hots, members, rows = [], [], []
    for j in range(RAYS):
        at = slot[j : j + 1, :]
        hot = jnp.where((at & (CAP - 1)) == place, 1.0, 0.0).astype(BF)
        member = jnp.where(lax.shift_right_logical(at, 8) == expert, 1.0, 0.0)
        found = dot(table, hot, ((1,), (0,)))
        rows.append(
            [
                jnp.sum(found[c * 16 : c * 16 + 16] * member, axis=0, keepdims=True)
                for c in range(4)
            ]
        )
        hots.append(hot)
        members.append(member)
    raw = [jnp.concatenate([rows[j][c] for j in range(RAYS)], axis=0) for c in range(4)]
    gate = gate_ref[...].astype(F32)
    delta = delta_ref[...]
    gated = [gate * r for r in raw]
    lane_r = lax.broadcasted_iota(I32, (128, 128), 0)
    lane_c = lax.broadcasted_iota(I32, (128, 128), 1)
    earlier = (lane_r < lane_c).astype(F32)
    later = (lane_r > lane_c).astype(F32)
    g0 = gated[0]
    density = jnp.maximum(g0, 0.0) + jnp.log1p(jnp.exp(-jnp.abs(g0)))
    radiance = [jax.nn.sigmoid(g) for g in gated[1:]]
    optical = density * delta
    before = dot(optical, earlier, ((1,), (0,)), precision=lax.Precision.HIGHEST)
    reach = jnp.exp(-before)
    passed = jnp.exp(-optical)
    weight = reach * (1.0 - passed)
    eye = lax.broadcasted_iota(I32, (RAYS, RAYS), 0) == lax.broadcasted_iota(I32, (RAYS, RAYS), 1)
    q = jnp.zeros((RAYS, S), F32)
    grads = [None]
    for c in range(3):
        rendered = jnp.sum(weight * radiance[c], axis=1, keepdims=True)
        goal = jnp.sum(jnp.where(eye, target_ref[c : c + 1, :], 0.0), axis=1, keepdims=True)
        rend_ref[c : c + 1, :] = jnp.sum(jnp.where(eye, rendered, 0.0), axis=0, keepdims=True)
        diff = rendered - goal
        q = q + diff * radiance[c]
        grads.append(diff * weight * radiance[c] * (1.0 - radiance[c]))
    push = dot(q * weight, later, ((1,), (0,)), precision=lax.Precision.HIGHEST)
    grads[0] = (q * reach * passed - push) * delta * jax.nn.sigmoid(g0)
    cots = [(gate * g).astype(BF).astype(F32) for g in grads]
    total = jnp.zeros((64, CAP), F32)
    for j in range(RAYS):
        spread = jnp.concatenate([cots[c][j : j + 1, :] * members[j] for c in range(4)], axis=0)
        total = total + dot(spread.astype(BF), hots[j], ((1,), (1,)))
    for c in range(4):
        cot_ref[:, c, :] = total[c * 16 : c * 16 + 16, :128]
        cot_ref[:, 4 + c, :] = total[c * 16 : c * 16 + 16, 128:]


def composite(table, slot, gate, delta, target):
    return pl.pallas_call(
        composite_kernel,
        out_shape=[
            jax.ShapeDtypeStruct((3, RAYS), F32),
            jax.ShapeDtypeStruct((EXPERTS, 8, 128), F32),
        ],
        compiler_params=params(),
    )(table, slot, gate, delta, target)


def backward_kernel(flip, where_ref, cot_ref, w_ref, v_ref, *refs):
    count = len(GROUPS)
    x_refs, h_refs = refs[:8], refs[8 : 8 + count]
    slope_refs, out_ref = refs[8 + count : 8 + 2 * count], refs[-1]
    e = where_ref[9] ^ flip
    head = v_ref[e, 4:8, :].astype(BF)
    grads, grad_head = [], 0.0
    for (pos, n), h_ref in zip(GROUPS, h_refs):
        parts = []
        for i in range(n):
            one = cot_ref[where_ref[pos + i], e]
            parts += [one[0:4], one[4:8]]
        cot = jnp.concatenate(parts, axis=1).astype(BF)
        grad_head = grad_head + dot(cot, h_ref[e, LAYERS - 1], ((1,), (0,)))
        grads.append(dot(cot, head, ((0,), (0,))))
    shifts = [None] * LAYERS
    for l in range(LAYERS - 1, -1, -1):
        total, shift = 0.0, 0.0
        for g, (pos, n) in enumerate(GROUPS):
            grad_pre = (grads[g] * slope_refs[g][e, l]).astype(BF)
            if l > 0:
                below = h_refs[g][e, l - 1]
            else:
                below = jnp.concatenate([x_refs[pos + i][e] for i in range(n)], axis=0)
            total = total + dot(below, grad_pre, ((0,), (0,)))
            shift = shift + dot(jnp.ones((8, n * CAP), BF), grad_pre, ((1,), (0,)))[0:1]
            if l > 0:
                grads[g] = dot(grad_pre, w_ref[e, l], ((1,), (1,)))
        shifts[l] = shift
        for half in range(2):
            at = (l * 2 + half) * 8
            out_ref[:, at : at + 8, :] = total[:, half * 128 : half * 128 + 128].reshape(32, 8, 128)
    extra = jnp.concatenate(shifts + [grad_head, jnp.zeros((120, D), F32)], axis=0)
    out_ref[:, 64:72, :] = extra.T.reshape(32, 8, 128)


def backward(flip, where, cot, w, v, xs, hs, slopes):
    vmem = pl.BlockSpec(memory_space=pltpu.VMEM)
    return pl.pallas_call(
        partial(backward_kernel, flip),
        in_specs=[pl.BlockSpec(memory_space=pltpu.SMEM)] + [vmem] * (11 + 2 * len(GROUPS)),
        out_shape=jax.ShapeDtypeStruct((32, CH, 128), F32),
        compiler_params=params(),
    )(where, cot, w, v, *xs, *hs, *slopes)


def finish_kernel(parts_ref, gw_ref, gb_ref, gh_ref):
    for e in range(2):
        total = parts_ref[0, e]
        for j in range(1, 16):
            total = total + parts_ref[j, e]
        for l in range(LAYERS):
            at = l * 16
            gw_ref[e, l] = jnp.concatenate([total[at : at + 8], total[at + 8 : at + 16]], axis=1)
        extra = jnp.concatenate([total[64:72], jnp.zeros((120, 128), F32)], axis=0).T
        gb_ref[e] = extra[0:4, 0:8]
        gh_ref[e] = extra[4:8, 0:8]


def finish(parts):
    return pl.pallas_call(
        finish_kernel,
        out_shape=[
            jax.ShapeDtypeStruct((2, LAYERS, 8, D), F32),
            jax.ShapeDtypeStruct((2, LAYERS, 8), F32),
            jax.ShapeDtypeStruct((2, 4, 8), F32),
        ],
        compiler_params=params(),
    )(parts)


def along(x, k):
    return lax.ppermute(x, "z", [(i, (i + k) % 8) for i in range(8)])


def local(features, routes, gate_values, deltas, target, w_hidden, b_hidden, w_head):
    z = lax.axis_index("z").astype(I32)
    core = lax.axis_index("c").astype(I32)
    sources = (z - jnp.array(SHIFTS, I32)) & 7
    where = jnp.concatenate([sources, z.reshape(1), core.reshape(1)])
    x = features.reshape(ROWS, D)
    arrived = {}
    *blocks, slot = pack((4, 3, -3), True, routes.reshape(RAYS, S), x)
    for k, block in zip((4, 3, -3), blocks):
        arrived[k] = along(block, k)
    w_hidden, b_hidden, w_head, x, slot = lax.optimization_barrier(
        (w_hidden, b_hidden, w_head, x, slot)
    )
    copies = prep(w_hidden, b_hidden, w_head)
    copies, slot2, x2 = lax.optimization_barrier((copies, slot, x))
    blocks = pack((1, -1, 2, -2, 0), False, slot2, x2)
    for k, block in zip((1, -1, 2, -2), blocks):
        arrived[k] = along(block, k)
    arrived[0] = blocks[-1]
    gathered = lax.all_to_all(copies, ("xy", "c"), 0, 0, tiled=True)
    w, v = unpack(gathered)
    xs = [arrived[k] for k in SHIFTS]
    hs, slopes, olds = [], [], []
    for g, (pos, n) in enumerate(GROUPS):
        last = g == len(GROUPS) - 1
        h, slope, out = forward(where, xs[pos : pos + n], w, v, olds if last else [])
        hs.append(h)
        slopes.append(slope)
        olds.append(out)
    table = lax.all_to_all(out, "z", 0, 0, tiled=True)
    rendered, cot = composite(table.reshape(EXPERTS, 8, 128), slot, gate_values, deltas, target)
    cot = lax.all_to_all(cot.reshape(8, 2, 8, 128), "z", 0, 0, tiled=True)
    given = backward(1, where, cot, w, v, xs, hs, slopes)
    given = lax.ppermute(given, "c", [(0, 1), (1, 0)])
    grads = backward(0, where, cot, w, v, xs, hs, slopes) + given
    parts = lax.all_to_all(grads, ("xy", "c"), 0, 0, tiled=True)
    grad_w, grad_b, grad_h = finish(parts.reshape(16, 2, CH, 128))
    return rendered, grad_w, grad_b, grad_h


def solution(mesh):
    split = Mesh(mesh.devices.reshape(8, 16, 2), ("z", "xy", "c"))
    every = ("z", "xy", "c")
    ray = ("xy", "c")
    in_specs = (
        P(every, None, None),
        P(every, None, None),
        P(every, None),
        P(every, None),
        P(None, every),
        P("z", None, ray, None),
        P("z", None, ray),
        P("z", None, ray),
    )
    out_specs = (P(None, every), P("z", None, ray, None), P("z", None, ray), P("z", None, ray))
    return jax.shard_map(local, mesh=split, in_specs=in_specs, out_specs=out_specs, check_vma=False)
```

time: 169 us -> 138 us (0.82)
  waiting for transfers between devices: 52.6 us -> 24.2 us
  starting transfers between devices: 10.2 us -> 30.3 us
  between operations: 14.1 us -> 0.74 us
  Pallas kernels: 37.7 us -> 29.2 us
    all_gather x1 -> x0, waiting for transfers between devices: 52.6 us -> none  [local(): gathered = lax.all_gather(shard, ('xy', 'c'), axis=0, tiled=False)]
    ppermute x0 -> x8, waiting for transfers between devices: none -> 24.2 us  [the longest x7 24.2 us: along(): return lax.ppermute(x, 'z', [(i, (i + k) % 8) for i in range(8)])]
    ppermute x0 -> x8, starting transfers between devices: none -> 21.6 us  [the longest x7 17.6 us: along(): return lax.ppermute(x, 'z', [(i, (i + k) % 8) for i in range(8)])]
    pallas_call x4 -> x9, Pallas kernels: 35.4 us -> 27 us  [the longest x3 11.4 us: forward(): pl.pallas_call(partial(forward_kernel, n, len(olds)), in_specs=[pl.BlockS...]
    all_to_all x2, blocking collectives: 25.2 us -> 22.6 us  [the longest x1 12.9 us: local(): table = lax.all_to_all(out, 'z', 0, 0, tiled=True)]
    all_to_all x1, blocking collectives: 23.9 us -> 25.9 us  [local(): parts = lax.all_to_all(grads, ('xy', 'c'), 0, 0, tiled=True)]
    unnamed x20 -> x22, local copies, waits for them, and re-layouts: 4.54 us -> 4.07 us
  transfers between devices with their start and end apart: 2 -> 9, of which waited for: 1 -> 5; matrix products, arithmetic and copies ran while one was open for 0% -> 0% of each run, Pallas kernels for 0% -> 12%
where the time goes in v2:
time: 138 us; the launch traced here: 137 us
  blocking collectives  48.4 us (35%)
  starting transfers between devices  30.3 us (22%)
  Pallas kernels  29.2 us (21%)
  waiting for transfers between devices  24.2 us (18%)
  local copies, waits for them, and re-layouts  4.07 us (3%)
    all_to_all x1, blocking collectives, local(): parts = lax.all_to_all(grads, ('xy', 'c'), 0, 0, tiled=True)  25.9 us
    ppermute x7, waiting for transfers between devices, along(): return lax.ppermute(x, 'z', [(i, (i + k) % 8) for i in range(8)])  24.2 us
    ppermute x7, starting transfers between devices, along(): return lax.ppermute(x, 'z', [(i, (i + k) % 8) for i in range(8)])  17.6 us
    all_to_all x1, blocking collectives, local(): table = lax.all_to_all(out, 'z', 0, 0, tiled=True)  12.9 us
    pallas_call x3, Pallas kernels, forward(): pl.pallas_call(partial(forward_kernel, n, len(olds)), in_specs=[pl.BlockS...  11.4 us
    all_to_all x1, blocking collectives, local(): cot = lax.all_to_all(cot.reshape(8, 2, 8, 128), 'z', 0, 0, tiled=True)  9.62 us
    all_to_all x1, starting transfers between devices, local(): gathered = lax.all_to_all(copies, ('xy', 'c'), 0, 0, tiled=True)  8.72 us
    pallas_call x2, Pallas kernels, backward(): pl.pallas_call(partial(backward_kernel, flip), in_specs=[pl.BlockSpec(mem...  8.01 us
  transfers between devices with their start and end apart: 9, of which 5 were waited for; matrix products, arithmetic and copies ran while one was open for 0% of the time, Pallas kernels for 12%

profile of v2, /device:TPU:1, one launch (start us, length us, event | category | flops | bytes accessed | tf_op | source)
XLA Modules:
  0.0 137.2 jit_solution(15258629831009462429)
XLA Ops:
  0.6 0.0 copy-start
  0.6 1.2 copy-done
  1.9 0.0 copy-start.3
  1.9 0.7 copy-done.3
  2.6 2.8 %shard_map.120 = (bf16[2,256,256]{2,1,0:T(8,128)(2,1)S(1)}, bf16[2,256,256]{2,1,0:T(8,128)(2,1)}, bf16[2,256,256]{2,1,0:T(8,128)(2,1)}, s32[16,128]{1,0:T(8,128)S(1)}) custom-call(s32[16,128]{1,0:T(8,128)S(1)} %bitcast.12, bf16[2048,256]{1,0:T(8,128)(2,1)S(1)} %bitcast.8), custom_call_target="tpu_custom_call" | custom-call | tf_op jit(solution)/shard_map/pallas_call | solution.py:128
  5.4 0.0 copy-start.2
  5.4 0.8 copy-done.2
  6.1 0.0 copy-start.6
  6.1 0.7 copy-done.6
  6.8 0.0 copy-start.7
  6.8 0.7 copy-done.7
  7.5 1.2 shard_map.121
  8.7 0.0 copy-start.1
  8.7 0.0 copy-start.10
  8.7 8.7 %all-to-all-start = ((bf16[32,2,72,128]{3,2,1,0:T(8,128)(2,1)}), bf16[32,2,72,128]{3,2,1,0:T(8,128)(2,1)S(1)}, u32[]{:S(2)}, u32[]{:S(2)}) async-start(bf16[32,2,72,128]{3,2,1,0:T(8,128)(2,1)} %shard_map.121), calls=%async_computation | async-start | bytes 2359296 | tf_op jit(solution)/shard_map/all_to_all | solution.py:348
  17.5 0.0 copy-done.1
  17.5 3.4 %shard_map.122 = (bf16[2,256,256]{2,1,0:T(8,128)(2,1)S(1)}, bf16[2,256,256]{2,1,0:T(8,128)(2,1)S(1)}, bf16[2,256,256]{2,1,0:T(8,128)(2,1)}, bf16[2,256,256]{2,1,0:T(8,128)(2,1)S(1)}, bf16[2,256,256]{2,1,0:T(8,128)(2,1)S(1)}) custom-call(s32[16,128]{1,0:T(8,128)S(1)} %get-tuple-element.43.refs_0_.slot_ref, bf16[2048,256]{1,0:T(8,128)(2,1)S(1)} %bitcast.9), custom_call_target="tpu_custom_call" | custom-call | tf_op jit(solution)/shard_map/pallas_call | solution.py:128
  20.9 0.0 copy-start.9
  20.9 1.6 %collective-permute-start.2 = (bf16[2,256,256]{2,1,0:T(8,128)(2,1)S(1)}, bf16[2,256,256]{2,1,0:T(8,128)(2,1)S(1)}, u32[]{:S(2)}, u32[]{:S(2)}) collective-permute-start(bf16[2,256,256]{2,1,0:T(8,128)(2,1)S(1)} %get-tuple-element.51), channel_id=1, source_target_pairs={{0,32},{32,64},{64,96},{96,128},{128,160},{160,192},{192,224},{224... | collective-permute-start | bytes 786440 | tf_op jit(solution)/shard_map/ppermute | solution.py:326
  22.5 3.9 %collective-permute-start.3 = (bf16[2,256,256]{2,1,0:T(8,128)(2,1)S(1)}, bf16[2,256,256]{2,1,0:T(8,128)(2,1)S(1)}, u32[]{:S(2)}, u32[]{:S(2)}) collective-permute-start(bf16[2,256,256]{2,1,0:T(8,128)(2,1)S(1)} %get-tuple-element.52), channel_id=1, source_target_pairs={{0,224},{32,0},{64,32},{96,64},{128,96},{160,128},{192,160},{224,1... | collective-permute-start | bytes 786440 | tf_op jit(solution)/shard_map/ppermute | solution.py:326
  26.4 1.6 %collective-permute-start.4 = (bf16[2,256,256]{2,1,0:T(8,128)(2,1)}, bf16[2,256,256]{2,1,0:T(8,128)(2,1)S(1)}, u32[]{:S(2)}, u32[]{:S(2)}) collective-permute-start(bf16[2,256,256]{2,1,0:T(8,128)(2,1)} %get-tuple-element.54), channel_id=1, source_target_pairs={{0,96},{32,128},{64,160},{96,192},{128,224},{160,0},{192,32},{224,... | collective-permute-start | bytes 786440 | tf_op jit(solution)/shard_map/ppermute | solution.py:326
  28.1 2.9 %collective-permute-start.5 = (bf16[2,256,256]{2,1,0:T(8,128)(2,1)}, bf16[2,256,256]{2,1,0:T(8,128)(2,1)S(1)}, u32[]{:S(2)}, u32[]{:S(2)}) collective-permute-start(bf16[2,256,256]{2,1,0:T(8,128)(2,1)} %get-tuple-element.55), channel_id=1, source_target_pairs={{0,160},{32,192},{64,224},{96,0},{128,32},{160,64},{192,96},{224,1... | collective-permute-start | bytes 786440 | tf_op jit(solution)/shard_map/ppermute | solution.py:326
  30.9 0.0 copy-done.9
  30.9 4.0 %collective-permute-start.6 = (bf16[2,256,256]{2,1,0:T(8,128)(2,1)S(1)}, bf16[2,256,256]{2,1,0:T(8,128)(2,1)S(1)}, u32[]{:S(2)}, u32[]{:S(2)}) collective-permute-start(bf16[2,256,256]{2,1,0:T(8,128)(2,1)S(1)} %get-tuple-element.56), channel_id=1, source_target_pairs={{0,128},{32,160},{64,192},{96,224},{128,0},{160,32},{192,64},{224,... | collective-permute-start | bytes 786440 | tf_op jit(solution)/shard_map/ppermute | solution.py:326
  34.9 0.0 collective-permute-done.2.refs_1_
  34.9 0.0 collective-permute-start
  34.9 0.0 collective-permute-done.3.refs_2_
  34.9 3.6 %collective-permute-start.1 = (bf16[2,256,256]{2,1,0:T(8,128)(2,1)}, bf16[2,256,256]{2,1,0:T(8,128)(2,1)S(1)}, u32[]{:S(2)}, u32[]{:S(2)}) collective-permute-start(bf16[2,256,256]{2,1,0:T(8,128)(2,1)} %copy-done.9), channel_id=1, source_target_pairs={{0,192},{32,224},{64,0},{96,32},{128,64},{160,96},{192,128},{224,1... | collective-permute-start | bytes 786440 | tf_op jit(solution)/shard_map/ppermute | solution.py:326
  38.5 0.0 copy-done.10
  38.5 0.1 pad_add_fusion.where_ref
  38.6 0.0 all-to-all-done.g_ref
  38.6 0.2 shard_map.123
  38.8 4.2 %shard_map.124 = (bf16[2,4,768,256]{3,2,1,0:T(8,128)(2,1)S(1)}, f32[2,4,768,256]{3,2,1,0:T(8,128)S(1)}, f32[3,2,8,128]{3,2,1,0:T(8,128)S(1)}) custom-call(s32[10]{0:T(128)S(1)} %pad_add_fusion.where_ref, bf16[2,256,256]{2,1,0:T(8,128)(2,1)S(1)} %get-tuple-element.50.refs_0_, bf16[2,256,256]{2,1,0:T(8,128)(2,1)S(1)} %collective-permute-done.2.refs_1_, ...), custom_call_target="tpu_custom_call" | custom-call | tf_op jit(solution)/shard_map/pallas_call | solution.py:168
  43.0 6.3 %collective-permute-done.4.refs_0_.refs_3_ = bf16[2,256,256]{2,1,0:T(8,128)(2,1)S(1)} collective-permute-done((bf16[2,256,256]{2,1,0:T(8,128)(2,1)}, bf16[2,256,256]{2,1,0:T(8,128)(2,1)S(1)}, u32[]{:S(2)}, u32[]{:S(2)}) %collective-permute-start.4) | collective-permute-done | bytes 262176 | tf_op jit(solution)/shard_map/ppermute | solution.py:326
  49.3 0.2 collective-permute-done.5.refs_1_.refs_4_
  49.5 5.6 %collective-permute-done.6.refs_2_.refs_5_ = bf16[2,256,256]{2,1,0:T(8,128)(2,1)S(1)} collective-permute-done((bf16[2,256,256]{2,1,0:T(8,128)(2,1)S(1)}, bf16[2,256,256]{2,1,0:T(8,128)(2,1)S(1)}, u32[]{:S(2)}, u32[]{:S(2)}) %collective-permute-start.6) | collective-permute-done | bytes 262176 | tf_op jit(solution)/shard_map/ppermute | solution.py:326
  55.1 4.2 %shard_map.125 = (bf16[2,4,768,256]{3,2,1,0:T(8,128)(2,1)S(1)}, f32[2,4,768,256]{3,2,1,0:T(8,128)S(1)}, f32[3,2,8,128]{3,2,1,0:T(8,128)S(1)}) custom-call(s32[10]{0:T(128)S(1)} %pad_add_fusion.where_ref, bf16[2,256,256]{2,1,0:T(8,128)(2,1)S(1)} %collective-permute-done.4.refs_0_.refs_3_, bf16[2,256,256]{2,1,0:T(8,128)(2,1)S(1)} %collective-permute-done.5.refs_1_.refs_4_, ...), custom_call_target="tpu_custom_call" | custom-call | tf_op jit(solution)/shard_map/pallas_call | solution.py:168
  59.2 0.0 copy-start.4
  59.2 0.0 copy-start.5
  59.3 0.0 copy-start.8
  59.3 9.0 %collective-permute-done.refs_0_.refs_6_ = bf16[2,256,256]{2,1,0:T(8,128)(2,1)S(1)} collective-permute-done((bf16[2,256,256]{2,1,0:T(8,128)(2,1)}, bf16[2,256,256]{2,1,0:T(8,128)(2,1)S(1)}, u32[]{:S(2)}, u32[]{:S(2)}) %collective-permute-start) | collective-permute-done | bytes 262176 | tf_op jit(solution)/shard_map/ppermute | solution.py:326
  68.3 3.1 %collective-permute-done.1.refs_1_.refs_7_ = bf16[2,256,256]{2,1,0:T(8,128)(2,1)S(1)} collective-permute-done((bf16[2,256,256]{2,1,0:T(8,128)(2,1)}, bf16[2,256,256]{2,1,0:T(8,128)(2,1)S(1)}, u32[]{:S(2)}, u32[]{:S(2)}) %collective-permute-start.1) | collective-permute-done | bytes 262176 | tf_op jit(solution)/shard_map/ppermute | solution.py:326
  71.3 3.0 %shard_map.126 = (bf16[2,4,512,256]{3,2,1,0:T(8,128)(2,1)S(1)}, f32[2,4,512,256]{3,2,1,0:T(8,128)S(1)}, f32[8,2,8,128]{3,2,1,0:T(8,128)S(1)}) custom-call(s32[10]{0:T(128)S(1)} %pad_add_fusion.where_ref, bf16[2,256,256]{2,1,0:T(8,128)(2,1)S(1)} %collective-permute-done.refs_0_.refs_6_, bf16[2,256,256]{2,1,0:T(8,128)(2,1)S(1)} %collective-permute-done.1.refs_1_.refs_7_, ...), custom_call_target="tpu_custom_call" | custom-call | tf_op jit(solution)/shard_map/pallas_call | solution.py:168
  74.4 12.9 %all_to_all.20 = f32[8,2,8,128]{3,2,1,0:T(8,128)S(1)} all-to-all(f32[8,2,8,128]{3,2,1,0:T(8,128)S(1)} %get-tuple-element.58), channel_id=1, replica_groups=mesh['z'=8,'xy'=16,'c'=2] {'z'}, dimensions={0} | all-to-all | bytes 131072 | tf_op jit(solution)/shard_map/all_to_all | solution.py:358
  87.3 0.0 copy-done.4
  87.3 0.0 copy-done.5
  87.3 0.0 copy-done.8
  87.3 1.5 %shard_map.127 = (f32[3,16]{1,0:T(4,128)}, f32[16,8,128]{2,1,0:T(8,128)S(1)}) custom-call(f32[16,8,128]{2,1,0:T(8,128)S(1)} %bitcast.10, s32[16,128]{1,0:T(8,128)S(1)} %get-tuple-element.43.refs_0_.slot_ref, bf16[16,128]{1,0:T(8,128)(2,1)S(1)} %copy-done.5, f32[16,128]{1,0:T(8,128)S(1)} %copy-done.4, f32[3,16]{1,0:T(4,128)S(1)} %copy-done.8), custom_call_target="tpu_custom_call" | custom-call | tf_op jit(solution)/shard_map/pallas_call | solution.py:244
  88.9 9.6 %all_to_all.21.cot_ref = f32[8,2,8,128]{3,2,1,0:T(8,128)S(1)} all-to-all(f32[8,2,8,128]{3,2,1,0:T(8,128)S(1)} %bitcast.11), channel_id=1, replica_groups=mesh['z'=8,'xy'=16,'c'=2] {'z'}, dimensions={0} | all-to-all | bytes 131072 | tf_op jit(solution)/shard_map/all_to_all | solution.py:360
  98.5 4.0 %shard_map.129 = f32[32,72,128]{2,1,0:T(8,128)S(1)} custom-call(s32[10]{0:T(128)S(1)} %pad_add_fusion.where_ref, f32[8,2,8,128]{3,2,1,0:T(8,128)S(1)} %all_to_all.21.cot_ref, bf16[2,4,256,256]{3,2,1,0:T(8,128)(2,1)S(1)} %get-tuple-element.48.refs_3_.refs_2_.w_ref, f32[2,8,256]{2,1,0:T(8,128)S(1)} %get-tuple-element.49.refs_4_.refs_3_.v_ref, ...), custom_call_target="tpu_custom_call" | custom-call | tf_op jit(solution)/shard_map/pallas_call | solution.py:292
  102.5 4.0 %collective-permute-start.7 = (f32[32,72,128]{2,1,0:T(8,128)S(1)}, f32[32,72,128]{2,1,0:T(8,128)S(1)}, u32[]{:S(2)}, u32[]{:S(2)}) collective-permute-start(f32[32,72,128]{2,1,0:T(8,128)S(1)} %shard_map.129), channel_id=1, source_target_pairs={{0,1},{1,0},{2,3},{3,2},{4,5},{5,4},{6,7},{7,6},{8,9},{9,8},{10,11... | collective-permute-start | bytes 3538952 | tf_op jit(solution)/shard_map/ppermute | solution.py:362
  106.5 4.0 %shard_map.128 = f32[32,72,128]{2,1,0:T(8,128)S(1)} custom-call(s32[10]{0:T(128)S(1)} %pad_add_fusion.where_ref, f32[8,2,8,128]{3,2,1,0:T(8,128)S(1)} %all_to_all.21.cot_ref, bf16[2,4,256,256]{3,2,1,0:T(8,128)(2,1)S(1)} %get-tuple-element.48.refs_3_.refs_2_.w_ref, f32[2,8,256]{2,1,0:T(8,128)S(1)} %get-tuple-element.49.refs_4_.refs_3_.v_ref, ...), custom_call_target="tpu_custom_call" | custom-call | tf_op jit(solution)/shard_map/pallas_call | solution.py:292
  110.5 0.0 collective-permute-done.7
  110.5 0.1 add.3
  110.6 25.9 %all_to_all.22 = f32[32,72,128]{2,1,0:T(8,128)S(1)} all-to-all(f32[32,72,128]{2,1,0:T(8,128)S(1)} %add.3), channel_id=1, replica_groups=mesh['z'=8,'xy'=16,'c'=2] {'xy','c'}, dimensions={0} | all-to-all | bytes 2359296 | tf_op jit(solution)/shard_map/all_to_all | solution.py:364
  136.5 0.7 shard_map.130
  (1 shorter events, 0.0 us)
Async XLA Ops:
  0.6 1.2 copy-start
  1.9 0.7 copy-start.3
  5.4 0.8 copy-start.2
  6.1 0.7 copy-start.6
  6.8 0.7 copy-start.7
  8.7 8.7 %copy-start.1 = (bf16[16,128,256]{2,1,0:T(8,128)(2,1)S(1)}, bf16[16,128,256]{2,1,0:T(8,128)(2,1)}, u32[]{:S(2)}) copy-start(bf16[16,128,256]{2,1,0:T(8,128)(2,1)} %param.9) | copy-start | bytes 3145732
  8.7 29.8 %copy-start.10 = (s32[8]{0:T(128)S(1)}, s32[8]{0:T(128)}, u32[]{:S(2)}) copy-start(s32[8]{0:T(128)} %constant.23) | copy-start | bytes 100
  8.7 29.8 %all-to-all-start = ((bf16[32,2,72,128]{3,2,1,0:T(8,128)(2,1)}), bf16[32,2,72,128]{3,2,1,0:T(8,128)(2,1)S(1)}, u32[]{:S(2)}, u32[]{:S(2)}) async-start(bf16[32,2,72,128]{3,2,1,0:T(8,128)(2,1)} %shard_map.121), calls=%async_computation | async-start | bytes 2359296 | tf_op jit(solution)/shard_map/all_to_all | solution.py:348
  20.9 10.1 %copy-start.9 = (bf16[2,256,256]{2,1,0:T(8,128)(2,1)}, bf16[2,256,256]{2,1,0:T(8,128)(2,1)S(1)}, u32[]{:S(2)}) copy-start(bf16[2,256,256]{2,1,0:T(8,128)(2,1)S(1)} %get-tuple-element.46) | copy-start | bytes 786436
  20.9 14.1 %collective-permute-start.2 = (bf16[2,256,256]{2,1,0:T(8,128)(2,1)S(1)}, bf16[2,256,256]{2,1,0:T(8,128)(2,1)S(1)}, u32[]{:S(2)}, u32[]{:S(2)}) collective-permute-start(bf16[2,256,256]{2,1,0:T(8,128)(2,1)S(1)} %get-tuple-element.51), channel_id=1, source_target_pairs={{0,32},{32,64},{64,96},{96,128},{128,160},{160,192},{192,224},{224... | collective-permute-start | bytes 786440 | tf_op jit(solution)/shard_map/ppermute | solution.py:326
  22.5 12.4 %collective-permute-start.3 = (bf16[2,256,256]{2,1,0:T(8,128)(2,1)S(1)}, bf16[2,256,256]{2,1,0:T(8,128)(2,1)S(1)}, u32[]{:S(2)}, u32[]{:S(2)}) collective-permute-start(bf16[2,256,256]{2,1,0:T(8,128)(2,1)S(1)} %get-tuple-element.52), channel_id=1, source_target_pairs={{0,224},{32,0},{64,32},{96,64},{128,96},{160,128},{192,160},{224,1... | collective-permute-start | bytes 786440 | tf_op jit(solution)/shard_map/ppermute | solution.py:326
  26.4 22.9 %collective-permute-start.4 = (bf16[2,256,256]{2,1,0:T(8,128)(2,1)}, bf16[2,256,256]{2,1,0:T(8,128)(2,1)S(1)}, u32[]{:S(2)}, u32[]{:S(2)}) collective-permute-start(bf16[2,256,256]{2,1,0:T(8,128)(2,1)} %get-tuple-element.54), channel_id=1, source_target_pairs={{0,96},{32,128},{64,160},{96,192},{128,224},{160,0},{192,32},{224,... | collective-permute-start | bytes 786440 | tf_op jit(solution)/shard_map/ppermute | solution.py:326
  28.1 21.4 %collective-permute-start.5 = (bf16[2,256,256]{2,1,0:T(8,128)(2,1)}, bf16[2,256,256]{2,1,0:T(8,128)(2,1)S(1)}, u32[]{:S(2)}, u32[]{:S(2)}) collective-permute-start(bf16[2,256,256]{2,1,0:T(8,128)(2,1)} %get-tuple-element.55), channel_id=1, source_target_pairs={{0,160},{32,192},{64,224},{96,0},{128,32},{160,64},{192,96},{224,1... | collective-permute-start | bytes 786440 | tf_op jit(solution)/shard_map/ppermute | solution.py:326
  30.9 24.1 %collective-permute-start.6 = (bf16[2,256,256]{2,1,0:T(8,128)(2,1)S(1)}, bf16[2,256,256]{2,1,0:T(8,128)(2,1)S(1)}, u32[]{:S(2)}, u32[]{:S(2)}) collective-permute-start(bf16[2,256,256]{2,1,0:T(8,128)(2,1)S(1)} %get-tuple-element.56), channel_id=1, source_target_pairs={{0,128},{32,160},{64,192},{96,224},{128,0},{160,32},{192,64},{224,... | collective-permute-start | bytes 786440 | tf_op jit(solution)/shard_map/ppermute | solution.py:326
  34.9 33.4 %collective-permute-start = (bf16[2,256,256]{2,1,0:T(8,128)(2,1)}, bf16[2,256,256]{2,1,0:T(8,128)(2,1)S(1)}, u32[]{:S(2)}, u32[]{:S(2)}) collective-permute-start(bf16[2,256,256]{2,1,0:T(8,128)(2,1)} %get-tuple-element.45), channel_id=1, source_target_pairs={{0,64},{32,96},{64,128},{96,160},{128,192},{160,224},{192,0},{224,... | collective-permute-start | bytes 786440 | tf_op jit(solution)/shard_map/ppermute | solution.py:326
  34.9 36.4 %collective-permute-start.1 = (bf16[2,256,256]{2,1,0:T(8,128)(2,1)}, bf16[2,256,256]{2,1,0:T(8,128)(2,1)S(1)}, u32[]{:S(2)}, u32[]{:S(2)}) collective-permute-start(bf16[2,256,256]{2,1,0:T(8,128)(2,1)} %copy-done.9), channel_id=1, source_target_pairs={{0,192},{32,224},{64,0},{96,32},{128,64},{160,96},{192,128},{224,1... | collective-permute-start | bytes 786440 | tf_op jit(solution)/shard_map/ppermute | solution.py:326
  59.2 28.1 %copy-start.4 = (f32[16,128]{1,0:T(8,128)S(1)}, f32[16,128]{1,0:T(8,128)}, u32[]{:S(2)}) copy-start(f32[16,128]{1,0:T(8,128)} %delta_ref.1) | copy-start | bytes 24580
  59.2 28.1 %copy-start.5 = (bf16[16,128]{1,0:T(8,128)(2,1)S(1)}, bf16[16,128]{1,0:T(8,128)(2,1)}, u32[]{:S(2)}) copy-start(bf16[16,128]{1,0:T(8,128)(2,1)} %gate_ref.1) | copy-start | bytes 12292
  59.3 28.1 %copy-start.8 = (f32[3,16]{1,0:T(4,128)S(1)}, f32[3,16]{1,0:T(4,128)}, u32[]{:S(2)}) copy-start(f32[3,16]{1,0:T(4,128)} %target_ref.1) | copy-start | bytes 580
  102.5 8.0 %collective-permute-start.7 = (f32[32,72,128]{2,1,0:T(8,128)S(1)}, f32[32,72,128]{2,1,0:T(8,128)S(1)}, u32[]{:S(2)}, u32[]{:S(2)}) collective-permute-start(f32[32,72,128]{2,1,0:T(8,128)S(1)} %shard_map.129), channel_id=1, source_target_pairs={{0,1},{1,0},{2,3},{3,2},{4,5},{5,4},{6,7},{7,6},{8,9},{9,8},{10,11... | collective-permute-start | bytes 3538952 | tf_op jit(solution)/shard_map/ppermute | solution.py:362

commit v3 on v2

--- a/solution.py
+++ b/solution.py
@@ -21,8 +21,8 @@
 S = 128
 D = 256
 LAYERS = 4
-SHIFTS = (0, 1, -1, 3, -3, 4, 2, -2)
-GROUPS = ((0, 3), (3, 3), (6, 2))
+SHIFTS = (0, 1, -1, 2, -2, 3, -3, 4)
+GROUPS = ((0, 5), (5, 3))
 CH = 72
 
 
@@ -297,15 +297,51 @@
     )(where, cot, w, v, *xs, *hs, *slopes)
 
 
+def combine_kernel(own_ref, given_ref, out_ref):
+    lane = lax.broadcasted_iota(I32, (1, 1, 128), 2)
+    extra = own_ref[:, 64:72, :] + given_ref[:, 64:72, :]
+    powers = power_of(jnp.max(jnp.max(jnp.abs(extra), axis=0, keepdims=True), axis=1, keepdims=True))
+    extra = extra * jnp.exp2(powers)
+    note = jnp.zeros((1, 1, 128), F32)
+    for l in range(LAYERS):
+        rows = slice(l * 16, l * 16 + 16)
+        total = own_ref[:, rows, :] + given_ref[:, rows, :]
+        top = jnp.max(jnp.abs(total), axis=0)
+        top = jnp.max(jnp.max(top, axis=0, keepdims=True), axis=1, keepdims=True)
+        power = power_of(top).reshape(1, 1, 1)
+        out_ref[:, rows, :] = total * jnp.exp2(power)
+        note = jnp.where(lane == 8 + l, power, note)
+    own = pltpu.roll(powers.reshape(1, 128), 16, 1).reshape(1, 1, 128)
+    note = jnp.where((lane >= 16) & (lane < 24), own, note)
+    out_ref[:, 64:72, :] = jnp.where(lane < 8, extra, note)
+
+
+def power_of(top):
+    return jnp.clip(jnp.floor(13.0 - jnp.log2(jnp.maximum(top, 1e-37))), -120.0, 120.0)
+
+
+def combine(own, given):
+    return pl.pallas_call(
+        combine_kernel, out_shape=jax.ShapeDtypeStruct((32, CH, 128), F32), compiler_params=params()
+    )(own, given)
+
+
 def finish_kernel(parts_ref, gw_ref, gb_ref, gh_ref):
     for e in range(2):
-        total = parts_ref[0, e]
-        for j in range(1, 16):
-            total = total + parts_ref[j, e]
+        notes = parts_ref[:, e, 64:72, :]
+        lane = lax.broadcasted_iota(I32, (1, 1, 128), 2)
         for l in range(LAYERS):
-            at = l * 16
-            gw_ref[e, l] = jnp.concatenate([total[at : at + 8], total[at + 8 : at + 16]], axis=1)
-        extra = jnp.concatenate([total[64:72], jnp.zeros((120, 128), F32)], axis=0).T
+            rows = slice(l * 16, l * 16 + 16)
+            total = 0.0
+            for j in range(16):
+                power = jnp.broadcast_to(notes[j, 0:1, 8 + l : 9 + l], (1, 128))
+                total = total + parts_ref[j, e, rows, :] * jnp.exp2(-power)
+            gw_ref[e, l] = jnp.concatenate([total[0:8], total[8:16]], axis=1)
+        extra = 0.0
+        for j in range(16):
+            power = pltpu.roll(notes[j], 128 - 16, 1)
+            extra = extra + jnp.where(lane[0] < 8, notes[j] * jnp.exp2(-power), 0.0)
+        extra = jnp.concatenate([extra, jnp.zeros((120, 128), F32)], axis=0).T
         gb_ref[e] = extra[0:4, 0:8]
         gh_ref[e] = extra[4:8, 0:8]
 
@@ -333,19 +369,21 @@
     where = jnp.concatenate([sources, z.reshape(1), core.reshape(1)])
     x = features.reshape(ROWS, D)
     arrived = {}
-    *blocks, slot = pack((4, 3, -3), True, routes.reshape(RAYS, S), x)
-    for k, block in zip((4, 3, -3), blocks):
+    *blocks, slot = pack((2, -2, 1, -1), True, routes.reshape(RAYS, S), x)
+    for k, block in zip((2, -2, 1, -1), blocks):
         arrived[k] = along(block, k)
-    w_hidden, b_hidden, w_head, x, slot = lax.optimization_barrier(
-        (w_hidden, b_hidden, w_head, x, slot)
-    )
-    copies = prep(w_hidden, b_hidden, w_head)
-    copies, slot2, x2 = lax.optimization_barrier((copies, slot, x))
-    blocks = pack((1, -1, 2, -2, 0), False, slot2, x2)
-    for k, block in zip((1, -1, 2, -2), blocks):
+    blocks = pack((3, -3, 4, 0), False, slot, x)
+    for k, block in zip((3, -3, 4), blocks):
         arrived[k] = along(block, k)
     arrived[0] = blocks[-1]
-    gathered = lax.all_to_all(copies, ("xy", "c"), 0, 0, tiled=True)
+    copies = prep(w_hidden, b_hidden, w_head)
+    copies, arrived[1], arrived[-1] = lax.optimization_barrier((copies, arrived[1], arrived[-1]))
+    gathered = lax.cond(
+        core >= 0,
+        lambda a: lax.all_to_all(a, ("xy", "c"), 0, 0, tiled=True),
+        jnp.zeros_like,
+        copies,
+    )
     w, v = unpack(gathered)
     xs = [arrived[k] for k in SHIFTS]
     hs, slopes, olds = [], [], []
@@ -360,8 +398,8 @@
     cot = lax.all_to_all(cot.reshape(8, 2, 8, 128), "z", 0, 0, tiled=True)
     given = backward(1, where, cot, w, v, xs, hs, slopes)
     given = lax.ppermute(given, "c", [(0, 1), (1, 0)])
-    grads = backward(0, where, cot, w, v, xs, hs, slopes) + given
-    parts = lax.all_to_all(grads, ("xy", "c"), 0, 0, tiled=True)
+    grads = combine(backward(0, where, cot, w, v, xs, hs, slopes), given).astype(jnp.float16)
+    parts = lax.all_to_all(grads, ("xy", "c"), 0, 0, tiled=True).astype(F32)
     grad_w, grad_b, grad_h = finish(parts.reshape(16, 2, CH, 128))
     return rendered, grad_w, grad_b, grad_h
 

time: 138 us -> 120 us (0.87)
  waiting for transfers between devices: 24.2 us -> 0.02 us
  blocking collectives: 48.4 us -> 65.6 us
  starting transfers between devices: 30.3 us -> 21.6 us
  local copies, waits for them, and re-layouts: 4.07 us -> 1.97 us
    ppermute x7, waiting for transfers between devices: 24.2 us -> 0.02 us  [along(): return lax.ppermute(x, 'z', [(i, (i + k) % 8) for i in range(8)])]
    all_to_all x1 -> x2, blocking collectives: 25.9 us -> 44.3 us  [the longest x1 28.8 us: local(): lax.all_to_all(a, ('xy', 'c'), 0, 0, tiled=True)]
    all_to_all x1 -> x0, starting transfers between devices: 8.72 us -> none  [local(): gathered = lax.all_to_all(copies, ('xy', 'c'), 0, 0, tiled=True)]
    unnamed x22 -> x20, local copies, waits for them, and re-layouts: 4.07 us -> 1.97 us
    pallas_call x3 -> x2, Pallas kernels: 11.4 us -> 10.7 us  [forward(): pl.pallas_call(partial(forward_kernel, n, len(olds)), in_specs=[pl.BlockS...]
  transfers between devices with their start and end apart: 9 -> 8, of which waited for: 5 -> 0; matrix products, arithmetic and copies ran while one was open for 0% -> 0% of each run, Pallas kernels for 12% -> 13%
where the time goes in v3:
time: 120 us
  blocking collectives  65.6 us (55%)
  Pallas kernels  29.9 us (25%)
  starting transfers between devices  21.6 us (18%)
  local copies, waits for them, and re-layouts  1.97 us (2%)
    all_to_all x1, blocking collectives, local(): lax.all_to_all(a, ('xy', 'c'), 0, 0, tiled=True)  28.8 us
    ppermute x7, starting transfers between devices, along(): return lax.ppermute(x, 'z', [(i, (i + k) % 8) for i in range(8)])  18.5 us
    all_to_all x1, blocking collectives, local(): parts = lax.all_to_all(grads, ('xy', 'c'), 0, 0, tiled=True).astype(F32)  15.6 us
    all_to_all x1, blocking collectives, local(): table = lax.all_to_all(out, 'z', 0, 0, tiled=True)  11.7 us
    pallas_call x2, Pallas kernels, forward(): pl.pallas_call(partial(forward_kernel, n, len(olds)), in_specs=[pl.BlockS...  10.7 us
    all_to_all x1, blocking collectives, local(): cot = lax.all_to_all(cot.reshape(8, 2, 8, 128), 'z', 0, 0, tiled=True)  9.62 us
    pallas_call x2, Pallas kernels, backward(): pl.pallas_call(partial(backward_kernel, flip), in_specs=[pl.BlockSpec(mem...  8.23 us
    pallas_call x2, Pallas kernels, pack(): pl.pallas_call(partial(pack_kernel, shifts, first), out_shape=out_shape,...  5.49 us
  transfers between devices with their start and end apart: 8, of which 0 were waited for; matrix products, arithmetic and copies ran while one was open for 0% of the time, Pallas kernels for 13%

profile of v3, /device:TPU:1, one launch (start us, length us, event | category | flops | bytes accessed | tf_op | source)
XLA Modules:
  0.0 120.0 jit_solution(1053374722279850442)
XLA Ops:
  0.6 0.0 copy-start.6
  0.6 0.0 copy-start
  0.7 1.2 %copy-done = bf16[16,128,256]{2,1,0:T(8,128)(2,1)S(1)} copy-done((bf16[16,128,256]{2,1,0:T(8,128)(2,1)S(1)}, bf16[16,128,256]{2,1,0:T(8,128)(2,1)}, u32[]{:S(2)}) %copy-start) | copy-done | bytes 1048600
  1.9 0.0 copy-start.3
  1.9 0.7 copy-done.3
  2.6 0.0 copy-start.1
  2.6 0.0 copy-start.2
  2.6 0.0 copy-start.7
  2.6 3.2 %shard_map.120 = (bf16[2,256,256]{2,1,0:T(8,128)(2,1)S(1)}, bf16[2,256,256]{2,1,0:T(8,128)(2,1)S(1)}, bf16[2,256,256]{2,1,0:T(8,128)(2,1)}, bf16[2,256,256]{2,1,0:T(8,128)(2,1)S(1)}, s32[16,128]{1,0:T(8,128)S(1)}) custom-call(s32[16,128]{1,0:T(8,128)S(1)} %bitcast.12, bf16[2048,256]{1,0:T(8,128)(2,1)S(1)} %bitcast.8), custom_call_target="tpu_custom_call" | custom-call | tf_op jit(solution)/shard_map/pallas_call | solution.py:128
  5.7 0.0 copy-start.9
  5.7 2.5 %collective-permute-start.3 = (bf16[2,256,256]{2,1,0:T(8,128)(2,1)}, bf16[2,256,256]{2,1,0:T(8,128)(2,1)S(1)}, u32[]{:S(2)}, u32[]{:S(2)}) collective-permute-start(bf16[2,256,256]{2,1,0:T(8,128)(2,1)} %get-tuple-element.37), channel_id=1, source_target_pairs={{0,32},{32,64},{64,96},{96,128},{128,160},{160,192},{192,224},{224... | collective-permute-start | bytes 786440 | tf_op jit(solution)/shard_map/ppermute | solution.py:362
  8.2 3.9 %collective-permute-start.4 = (bf16[2,256,256]{2,1,0:T(8,128)(2,1)S(1)}, bf16[2,256,256]{2,1,0:T(8,128)(2,1)S(1)}, u32[]{:S(2)}, u32[]{:S(2)}) collective-permute-start(bf16[2,256,256]{2,1,0:T(8,128)(2,1)S(1)} %get-tuple-element.38), channel_id=1, source_target_pairs={{0,224},{32,0},{64,32},{96,64},{128,96},{160,128},{192,160},{224,1... | collective-permute-start | bytes 786440 | tf_op jit(solution)/shard_map/ppermute | solution.py:362
  12.1 0.0 collective-permute-start.5
  12.2 3.6 %collective-permute-start.6 = (bf16[2,256,256]{2,1,0:T(8,128)(2,1)S(1)}, bf16[2,256,256]{2,1,0:T(8,128)(2,1)S(1)}, u32[]{:S(2)}, u32[]{:S(2)}) collective-permute-start(bf16[2,256,256]{2,1,0:T(8,128)(2,1)S(1)} %get-tuple-element.46), channel_id=1, source_target_pairs={{0,192},{32,224},{64,0},{96,32},{128,64},{160,96},{192,128},{224,1... | collective-permute-start | bytes 786440 | tf_op jit(solution)/shard_map/ppermute | solution.py:362
  15.7 0.0 copy-done.1
  15.7 2.3 %shard_map.121 = (bf16[2,256,256]{2,1,0:T(8,128)(2,1)S(1)}, bf16[2,256,256]{2,1,0:T(8,128)(2,1)S(1)}, bf16[2,256,256]{2,1,0:T(8,128)(2,1)S(1)}, bf16[2,256,256]{2,1,0:T(8,128)(2,1)S(1)}) custom-call(s32[16,128]{1,0:T(8,128)S(1)} %get-tuple-element.33.refs_0_.slot_ref, bf16[2048,256]{1,0:T(8,128)(2,1)S(1)} %bitcast.9), custom_call_target="tpu_custom_call" | custom-call | tf_op jit(solution)/shard_map/pallas_call | solution.py:128
  18.1 0.5 collective-permute-start
  18.5 0.0 copy-done.6
  18.5 0.0 copy-done.2
  18.6 0.0 copy-done.7
  18.6 1.2 %shard_map.122 = bf16[32,2,72,128]{3,2,1,0:T(8,128)(2,1)} custom-call(bf16[2,4,8,256]{3,2,1,0:T(8,128)(2,1)S(1)} %copy-done.2, bf16[2,4,8]{2,1,0:T(4,128)(2,1)S(1)} %copy-done.6, bf16[2,4,8]{2,1,0:T(4,128)(2,1)S(1)} %copy-done.7), custom_call_target="tpu_custom_call" | custom-call | tf_op jit(solution)/shard_map/pallas_call | solution.py:52
  19.8 0.0 collective-permute-done.3.refs_1_
  19.8 4.1 %collective-permute-start.1 = (bf16[2,256,256]{2,1,0:T(8,128)(2,1)S(1)}, bf16[2,256,256]{2,1,0:T(8,128)(2,1)S(1)}, u32[]{:S(2)}, u32[]{:S(2)}) collective-permute-start(bf16[2,256,256]{2,1,0:T(8,128)(2,1)S(1)} %get-tuple-element.35), channel_id=1, source_target_pairs={{0,160},{32,192},{64,224},{96,0},{128,32},{160,64},{192,96},{224,1... | collective-permute-start | bytes 786440 | tf_op jit(solution)/shard_map/ppermute | solution.py:362
  23.9 0.0 collective-permute-done.4.refs_2_
  23.9 4.0 %collective-permute-start.2 = (bf16[2,256,256]{2,1,0:T(8,128)(2,1)S(1)}, bf16[2,256,256]{2,1,0:T(8,128)(2,1)S(1)}, u32[]{:S(2)}, u32[]{:S(2)}) collective-permute-start(bf16[2,256,256]{2,1,0:T(8,128)(2,1)S(1)} %get-tuple-element.36), channel_id=1, source_target_pairs={{0,128},{32,160},{64,192},{96,224},{128,0},{160,32},{192,64},{224,... | collective-permute-start | bytes 786440 | tf_op jit(solution)/shard_map/ppermute | solution.py:362
  27.9 0.0 copy-done.9
  27.9 0.1 pad_add_fusion.where_ref
  28.0 28.8 %conditional.1 = (bf16[32,2,72,128]{3,2,1,0:T(8,128)(2,1)}) conditional(s32[]{:T(128)} %convert_element_type.7, () %tuple.15, bf16[32,2,72,128]{3,2,1,0:T(8,128)(2,1)} %shard_map.122), branch_computations={%region_0.0_spmd, %region_1.0_spmd} | conditional | bytes 2359304 | solution.py:381
  28.0 28.8 %all_to_all.19 = bf16[32,2,72,128]{3,2,1,0:T(8,128)(2,1)} all-to-all(bf16[32,2,72,128]{3,2,1,0:T(8,128)(2,1)} %param.1), channel_id=1, replica_groups=mesh['z'=8,'xy'=16,'c'=2] {'xy','c'}, dimensions={0} | all-to-all | bytes 2359296 | tf_op jit(solution)/shard_map/cond/branch_1_fun/all_to_all | solution.py:383
  56.7 1.5 %shard_map.123 = (bf16[2,4,256,256]{3,2,1,0:T(8,128)(2,1)S(1)}, f32[2,8,256]{2,1,0:T(8,128)S(1)}) custom-call(bf16[32,2,72,128]{3,2,1,0:T(8,128)(2,1)} %get-tuple-element.58.g_ref), custom_call_target="tpu_custom_call" | custom-call | tf_op jit(solution)/shard_map/pallas_call | solution.py:69
  58.2 0.0 collective-permute-done.5.refs_3_
  58.2 0.0 collective-permute-done.6.refs_4_
  58.2 6.5 %shard_map.124 = (bf16[2,4,1280,256]{3,2,1,0:T(8,128)(2,1)S(1)}, f32[2,4,1280,256]{3,2,1,0:T(8,128)S(1)}, f32[5,2,8,128]{3,2,1,0:T(8,128)S(1)}) custom-call(s32[10]{0:T(128)S(1)} %pad_add_fusion.where_ref, bf16[2,256,256]{2,1,0:T(8,128)(2,1)S(1)} %get-tuple-element.42.refs_0_, bf16[2,256,256]{2,1,0:T(8,128)(2,1)S(1)} %collective-permute-done.3.refs_1_, ...), custom_call_target="tpu_custom_call" | custom-call | tf_op jit(solution)/shard_map/pallas_call | solution.py:168
  64.7 0.0 copy-start.4
  64.7 0.0 copy-start.5
  64.7 0.0 copy-start.8
  64.7 0.0 collective-permute-done.refs_0_.refs_5_
  64.8 0.0 collective-permute-done.1.refs_1_.refs_6_
  64.8 0.0 collective-permute-done.2.refs_2_.refs_7_
  64.8 4.2 %shard_map.125 = (bf16[2,4,768,256]{3,2,1,0:T(8,128)(2,1)S(1)}, f32[2,4,768,256]{3,2,1,0:T(8,128)S(1)}, f32[8,2,8,128]{3,2,1,0:T(8,128)S(1)}) custom-call(s32[10]{0:T(128)S(1)} %pad_add_fusion.where_ref, bf16[2,256,256]{2,1,0:T(8,128)(2,1)S(1)} %collective-permute-done.refs_0_.refs_5_, bf16[2,256,256]{2,1,0:T(8,128)(2,1)S(1)} %collective-permute-done.1.refs_1_.refs_6_, ...), custom_call_target="tpu_custom_call" | custom-call | tf_op jit(solution)/shard_map/pallas_call | solution.py:168
  69.0 11.7 %all_to_all.20 = f32[8,2,8,128]{3,2,1,0:T(8,128)S(1)} all-to-all(f32[8,2,8,128]{3,2,1,0:T(8,128)S(1)} %get-tuple-element.48), channel_id=1, replica_groups=mesh['z'=8,'xy'=16,'c'=2] {'z'}, dimensions={0} | all-to-all | bytes 131072 | tf_op jit(solution)/shard_map/all_to_all | solution.py:396
  80.6 0.0 copy-done.4
  80.6 0.0 copy-done.5
  80.6 0.0 copy-done.8
  80.6 1.5 %shard_map.126 = (f32[3,16]{1,0:T(4,128)}, f32[16,8,128]{2,1,0:T(8,128)S(1)}) custom-call(f32[16,8,128]{2,1,0:T(8,128)S(1)} %bitcast.10, s32[16,128]{1,0:T(8,128)S(1)} %get-tuple-element.33.refs_0_.slot_ref, bf16[16,128]{1,0:T(8,128)(2,1)S(1)} %copy-done.5, f32[16,128]{1,0:T(8,128)S(1)} %copy-done.4, f32[3,16]{1,0:T(4,128)S(1)} %copy-done.8), custom_call_target="tpu_custom_call" | custom-call | tf_op jit(solution)/shard_map/pallas_call | solution.py:244
  82.2 9.6 %all_to_all.21.cot_ref = f32[8,2,8,128]{3,2,1,0:T(8,128)S(1)} all-to-all(f32[8,2,8,128]{3,2,1,0:T(8,128)S(1)} %bitcast.11), channel_id=1, replica_groups=mesh['z'=8,'xy'=16,'c'=2] {'z'}, dimensions={0} | all-to-all | bytes 131072 | tf_op jit(solution)/shard_map/all_to_all | solution.py:398
  91.8 4.1 %shard_map.128 = f32[32,72,128]{2,1,0:T(8,128)S(1)} custom-call(s32[10]{0:T(128)S(1)} %pad_add_fusion.where_ref, f32[8,2,8,128]{3,2,1,0:T(8,128)S(1)} %all_to_all.21.cot_ref, bf16[2,4,256,256]{3,2,1,0:T(8,128)(2,1)S(1)} %get-tuple-element.40.refs_5_.refs_3_.w_ref, f32[2,8,256]{2,1,0:T(8,128)S(1)} %get-tuple-element.41.refs_6_.refs_4_.v_ref, ...), custom_call_target="tpu_custom_call" | custom-call | tf_op jit(solution)/shard_map/pallas_call | solution.py:292
  95.9 3.0 %collective-permute-start.7 = (f32[32,72,128]{2,1,0:T(8,128)S(1)}, f32[32,72,128]{2,1,0:T(8,128)S(1)}, u32[]{:S(2)}, u32[]{:S(2)}) collective-permute-start(f32[32,72,128]{2,1,0:T(8,128)S(1)} %shard_map.128), channel_id=1, source_target_pairs={{0,1},{1,0},{2,3},{3,2},{4,5},{5,4},{6,7},{7,6},{8,9},{9,8},{10,11... | collective-permute-start | bytes 3538952 | tf_op jit(solution)/shard_map/ppermute | solution.py:400
  99.0 4.1 %shard_map.127.own_ref = f32[32,72,128]{2,1,0:T(8,128)S(1)} custom-call(s32[10]{0:T(128)S(1)} %pad_add_fusion.where_ref, f32[8,2,8,128]{3,2,1,0:T(8,128)S(1)} %all_to_all.21.cot_ref, bf16[2,4,256,256]{3,2,1,0:T(8,128)(2,1)S(1)} %get-tuple-element.40.refs_5_.refs_3_.w_ref, f32[2,8,256]{2,1,0:T(8,128)S(1)} %get-tuple-element.41.refs_6_.refs_4_.v_ref, ...), custom_call_target="tpu_custom_call" | custom-call | tf_op jit(solution)/shard_map/pallas_call | solution.py:292
  103.1 0.0 collective-permute-done.7.given_ref
  103.1 0.3 shard_map.129
  103.4 0.1 convert_element_type.8
  103.5 15.6 %all_to_all.22 = f16[32,72,128]{2,1,0:T(8,128)(2,1)S(1)} all-to-all(f16[32,72,128]{2,1,0:T(8,128)(2,1)S(1)} %convert_element_type.8), channel_id=1, replica_groups=mesh['z'=8,'xy'=16,'c'=2] {'xy','c'}, dimensions={0} | all-to-all | bytes 1179648 | tf_op jit(solution)/shard_map/all_to_all | solution.py:402
  119.1 0.1 convert.1.parts_ref
  119.1 0.9 shard_map.130
  (1 shorter events, 0.0 us)
Async XLA Ops:
  0.6 17.9 %copy-start.6 = (bf16[2,4,8]{2,1,0:T(4,128)(2,1)S(1)}, bf16[2,4,8]{2,1,0:T(4,128)(2,1)}, u32[]{:S(2)}) copy-start(bf16[2,4,8]{2,1,0:T(4,128)(2,1)} %b_ref.1) | copy-start | bytes 388
  0.6 1.2 %copy-start = (bf16[16,128,256]{2,1,0:T(8,128)(2,1)S(1)}, bf16[16,128,256]{2,1,0:T(8,128)(2,1)}, u32[]{:S(2)}) copy-start(bf16[16,128,256]{2,1,0:T(8,128)(2,1)} %param.11) | copy-start | bytes 3145732
  1.9 0.7 copy-start.3
  2.6 13.2 %copy-start.1 = (bf16[16,128,256]{2,1,0:T(8,128)(2,1)S(1)}, bf16[16,128,256]{2,1,0:T(8,128)(2,1)}, u32[]{:S(2)}) copy-start(bf16[16,128,256]{2,1,0:T(8,128)(2,1)} %param.11) | copy-start | bytes 3145732
  2.6 16.0 %copy-start.2 = (bf16[2,4,8,256]{3,2,1,0:T(8,128)(2,1)S(1)}, bf16[2,4,8,256]{3,2,1,0:T(8,128)(2,1)}, u32[]{:S(2)}) copy-start(bf16[2,4,8,256]{3,2,1,0:T(8,128)(2,1)} %w_ref.1) | copy-start | bytes 98308
  2.6 16.0 %copy-start.7 = (bf16[2,4,8]{2,1,0:T(4,128)(2,1)S(1)}, bf16[2,4,8]{2,1,0:T(4,128)(2,1)}, u32[]{:S(2)}) copy-start(bf16[2,4,8]{2,1,0:T(4,128)(2,1)} %h_ref.1) | copy-start | bytes 388
  5.7 22.1 %copy-start.9 = (s32[8]{0:T(128)S(1)}, s32[8]{0:T(128)}, u32[]{:S(2)}) copy-start(s32[8]{0:T(128)} %constant.27) | copy-start | bytes 100
  5.7 14.0 %collective-permute-start.3 = (bf16[2,256,256]{2,1,0:T(8,128)(2,1)}, bf16[2,256,256]{2,1,0:T(8,128)(2,1)S(1)}, u32[]{:S(2)}, u32[]{:S(2)}) collective-permute-start(bf16[2,256,256]{2,1,0:T(8,128)(2,1)} %get-tuple-element.37), channel_id=1, source_target_pairs={{0,32},{32,64},{64,96},{96,128},{128,160},{160,192},{192,224},{224... | collective-permute-start | bytes 786440 | tf_op jit(solution)/shard_map/ppermute | solution.py:362
  8.2 15.7 %collective-permute-start.4 = (bf16[2,256,256]{2,1,0:T(8,128)(2,1)S(1)}, bf16[2,256,256]{2,1,0:T(8,128)(2,1)S(1)}, u32[]{:S(2)}, u32[]{:S(2)}) collective-permute-start(bf16[2,256,256]{2,1,0:T(8,128)(2,1)S(1)} %get-tuple-element.38), channel_id=1, source_target_pairs={{0,224},{32,0},{64,32},{96,64},{128,96},{160,128},{192,160},{224,1... | collective-permute-start | bytes 786440 | tf_op jit(solution)/shard_map/ppermute | solution.py:362
  12.1 46.1 %collective-permute-start.5 = (bf16[2,256,256]{2,1,0:T(8,128)(2,1)S(1)}, bf16[2,256,256]{2,1,0:T(8,128)(2,1)S(1)}, u32[]{:S(2)}, u32[]{:S(2)}) collective-permute-start(bf16[2,256,256]{2,1,0:T(8,128)(2,1)S(1)} %get-tuple-element.45), channel_id=1, source_target_pairs={{0,64},{32,96},{64,128},{96,160},{128,192},{160,224},{192,0},{224,... | collective-permute-start | bytes 786440 | tf_op jit(solution)/shard_map/ppermute | solution.py:362
  12.2 46.1 %collective-permute-start.6 = (bf16[2,256,256]{2,1,0:T(8,128)(2,1)S(1)}, bf16[2,256,256]{2,1,0:T(8,128)(2,1)S(1)}, u32[]{:S(2)}, u32[]{:S(2)}) collective-permute-start(bf16[2,256,256]{2,1,0:T(8,128)(2,1)S(1)} %get-tuple-element.46), channel_id=1, source_target_pairs={{0,192},{32,224},{64,0},{96,32},{128,64},{160,96},{192,128},{224,1... | collective-permute-start | bytes 786440 | tf_op jit(solution)/shard_map/ppermute | solution.py:362
  18.1 46.7 %collective-permute-start = (bf16[2,256,256]{2,1,0:T(8,128)(2,1)S(1)}, bf16[2,256,256]{2,1,0:T(8,128)(2,1)S(1)}, u32[]{:S(2)}, u32[]{:S(2)}) collective-permute-start(bf16[2,256,256]{2,1,0:T(8,128)(2,1)S(1)} %get-tuple-element.34), channel_id=1, source_target_pairs={{0,96},{32,128},{64,160},{96,192},{128,224},{160,0},{192,32},{224,... | collective-permute-start | bytes 786440 | tf_op jit(solution)/shard_map/ppermute | solution.py:362
  19.8 45.0 %collective-permute-start.1 = (bf16[2,256,256]{2,1,0:T(8,128)(2,1)S(1)}, bf16[2,256,256]{2,1,0:T(8,128)(2,1)S(1)}, u32[]{:S(2)}, u32[]{:S(2)}) collective-permute-start(bf16[2,256,256]{2,1,0:T(8,128)(2,1)S(1)} %get-tuple-element.35), channel_id=1, source_target_pairs={{0,160},{32,192},{64,224},{96,0},{128,32},{160,64},{192,96},{224,1... | collective-permute-start | bytes 786440 | tf_op jit(solution)/shard_map/ppermute | solution.py:362
  23.9 40.9 %collective-permute-start.2 = (bf16[2,256,256]{2,1,0:T(8,128)(2,1)S(1)}, bf16[2,256,256]{2,1,0:T(8,128)(2,1)S(1)}, u32[]{:S(2)}, u32[]{:S(2)}) collective-permute-start(bf16[2,256,256]{2,1,0:T(8,128)(2,1)S(1)} %get-tuple-element.36), channel_id=1, source_target_pairs={{0,128},{32,160},{64,192},{96,224},{128,0},{160,32},{192,64},{224,... | collective-permute-start | bytes 786440 | tf_op jit(solution)/shard_map/ppermute | solution.py:362
  64.7 15.9 %copy-start.4 = (f32[16,128]{1,0:T(8,128)S(1)}, f32[16,128]{1,0:T(8,128)}, u32[]{:S(2)}) copy-start(f32[16,128]{1,0:T(8,128)} %delta_ref.1) | copy-start | bytes 24580
  64.7 15.9 %copy-start.5 = (bf16[16,128]{1,0:T(8,128)(2,1)S(1)}, bf16[16,128]{1,0:T(8,128)(2,1)}, u32[]{:S(2)}) copy-start(bf16[16,128]{1,0:T(8,128)(2,1)} %gate_ref.1) | copy-start | bytes 12292
  64.7 15.9 %copy-start.8 = (f32[3,16]{1,0:T(4,128)S(1)}, f32[3,16]{1,0:T(4,128)}, u32[]{:S(2)}) copy-start(f32[3,16]{1,0:T(4,128)} %target_ref.1) | copy-start | bytes 580
  95.9 7.2 %collective-permute-start.7 = (f32[32,72,128]{2,1,0:T(8,128)S(1)}, f32[32,72,128]{2,1,0:T(8,128)S(1)}, u32[]{:S(2)}, u32[]{:S(2)}) collective-permute-start(f32[32,72,128]{2,1,0:T(8,128)S(1)} %shard_map.128), channel_id=1, source_target_pairs={{0,1},{1,0},{2,3},{3,2},{4,5},{5,4},{6,7},{7,6},{8,9},{9,8},{10,11... | collective-permute-start | bytes 3538952 | tf_op jit(solution)/shard_map/ppermute | solution.py:400

commit v4 on v3

--- a/solution.py
+++ b/solution.py
@@ -60,9 +60,10 @@
             for half in range(2):
                 at = (l * 2 + half) * 8
                 part = g_ref[:, e, at : at + 8, :].astype(F32).reshape(D, 128)
-                w_ref[e, l, :, half * 128 : half * 128 + 128] = part.astype(BF)
+                w_ref[e, l, :, half * 128 : half * 128 + 128] = (0.5 * part).astype(BF)
         extra = g_ref[:, e, 64:72, :].astype(F32).reshape(D, 128)
-        v_ref[e] = extra.T[0:8]
+        extra = extra.T[0:8]
+        v_ref[e] = jnp.concatenate([0.5 * extra[0:4], extra[4:8]], axis=0)
 
 
 def unpack(gathered):
@@ -137,29 +138,27 @@
     for l in range(LAYERS):
         for e in range(2):
             pre = dot(hidden[e], w_ref[e, l], ((1,), (0,))) + v_ref[e, l : l + 1, :]
-            square = pre * pre
-            t = jnp.tanh(pre * (K0 + (K0 * K1) * square))
-            cdf = 0.5 + 0.5 * t
-            value = pre * cdf
-            slope_ref[e, l] = cdf + value * (1.0 - t) * (K0 + (3.0 * K0 * K1) * square)
+            cubic = (8.0 * K0 * K1) * (pre * pre)
+            t = jnp.tanh(pre * (2.0 * K0 + cubic))
+            twice = 1.0 + t
+            value = pre * twice
+            slope_ref[e, l] = twice + value * (1.0 - t) * (2.0 * K0 + 3.0 * cubic)
             hidden[e] = value.astype(BF)
             h_ref[e, l] = hidden[e]
-    at = 0
+    pos = 0
     for old in olds:
         for i in range(old.shape[0]):
-            out_ref[where_ref[at]] = old[i]
-            at += 1
-    for e in range(2):
-        out = dot(v_ref[e].astype(BF), hidden[e], ((1,), (1,))).astype(BF).astype(F32)
-        for i in range(n):
-            lo = i * CAP
-            one = jnp.concatenate(
-                [out[4:8, lo : lo + 128], out[4:8, lo + 128 : lo + CAP]], axis=0
-            )
-            if olds_n:
-                out_ref[where_ref[at + i], e] = one
-            else:
-                out_ref[i, e] = one
+            out_ref[where_ref[pos]] = old[i]
+            pos += 1
+    outs = [dot(v_ref[e].astype(BF), hidden[e], ((1,), (1,)))[4:8] for e in range(2)]
+    for i in range(n):
+        lo = i * CAP
+        one = [out[:, at : at + 128] for out in outs for at in (lo, lo + 128)]
+        one = jnp.concatenate(one, axis=0).astype(BF)
+        if olds_n:
+            out_ref[where_ref[pos + i]] = one
+        else:
+            out_ref[i] = one
 
 
 def forward(where, xs, w, v, olds):
@@ -171,13 +170,16 @@
         out_shape=[
             jax.ShapeDtypeStruct((2, LAYERS, n * CAP, D), BF),
             jax.ShapeDtypeStruct((2, LAYERS, n * CAP, D), F32),
-            jax.ShapeDtypeStruct((8 if olds else n, 2, 8, 128), F32),
+            jax.ShapeDtypeStruct((8 if olds else n, 16, 128), BF),
         ],
         compiler_params=params(),
     )(where, *xs, w, v, *olds)
 
 
-def composite_kernel(table_ref, slot_ref, gate_ref, delta_ref, target_ref, rend_ref, cot_ref):
+def composite_kernel(
+    table16_ref, slot_ref, gate_ref, delta_ref, target_ref, rend_ref, cot16_ref, table_ref, cot_ref
+):
+    table_ref[...] = table16_ref[...].astype(F32).reshape(EXPERTS, 8, 128)
     table = jnp.concatenate(
         [
             jnp.concatenate([table_ref[:, c, :], table_ref[:, 4 + c, :]], axis=1)
@@ -238,6 +240,7 @@
     for c in range(4):
         cot_ref[:, c, :] = total[c * 16 : c * 16 + 16, :128]
         cot_ref[:, 4 + c, :] = total[c * 16 : c * 16 + 16, 128:]
+    cot16_ref[...] = cot_ref[...].reshape(8, 16, 128).astype(BF)
 
 
 def composite(table, slot, gate, delta, target):
@@ -245,8 +248,9 @@
         composite_kernel,
         out_shape=[
             jax.ShapeDtypeStruct((3, RAYS), F32),
-            jax.ShapeDtypeStruct((EXPERTS, 8, 128), F32),
+            jax.ShapeDtypeStruct((8, 16, 128), BF),
         ],
+        scratch_shapes=[pltpu.VMEM((EXPERTS, 8, 128), F32)] * 2,
         compiler_params=params(),
     )(table, slot, gate, delta, target)
 
@@ -256,12 +260,13 @@
     x_refs, h_refs = refs[:8], refs[8 : 8 + count]
     slope_refs, out_ref = refs[8 + count : 8 + 2 * count], refs[-1]
     e = where_ref[9] ^ flip
-    head = v_ref[e, 4:8, :].astype(BF)
+    head = (0.5 * v_ref[e, 4:8, :]).astype(BF)
     grads, grad_head = [], 0.0
     for (pos, n), h_ref in zip(GROUPS, h_refs):
         parts = []
         for i in range(n):
-            one = cot_ref[where_ref[pos + i], e]
+            one = cot_ref[where_ref[pos + i]].astype(F32)
+            one = jnp.where(e == 0, one[0:8], one[8:16])
             parts += [one[0:4], one[4:8]]
         cot = jnp.concatenate(parts, axis=1).astype(BF)
         grad_head = grad_head + dot(cot, h_ref[e, LAYERS - 1], ((1,), (0,)))
@@ -394,8 +399,8 @@
         slopes.append(slope)
         olds.append(out)
     table = lax.all_to_all(out, "z", 0, 0, tiled=True)
-    rendered, cot = composite(table.reshape(EXPERTS, 8, 128), slot, gate_values, deltas, target)
-    cot = lax.all_to_all(cot.reshape(8, 2, 8, 128), "z", 0, 0, tiled=True)
+    rendered, cot = composite(table, slot, gate_values, deltas, target)
+    cot = lax.all_to_all(cot, "z", 0, 0, tiled=True)
     given = backward(1, where, cot, w, v, xs, hs, slopes)
     given = lax.ppermute(given, "c", [(0, 1), (1, 0)])
     grads = combine(backward(0, where, cot, w, v, xs, hs, slopes), given).astype(jnp.float16)

time: 120 us -> 119 us (level)
  no operation moved by 1% of the time
where the time goes in v4:
time: 119 us
  blocking collectives  65 us (55%)
  Pallas kernels  29.1 us (24%)
  starting transfers between devices  21.5 us (18%)
  local copies, waits for them, and re-layouts  1.96 us (2%)
    all_to_all x1, blocking collectives, local(): lax.all_to_all(a, ('xy', 'c'), 0, 0, tiled=True)  28.8 us
    ppermute x7, starting transfers between devices, along(): return lax.ppermute(x, 'z', [(i, (i + k) % 8) for i in range(8)])  18.5 us
    all_to_all x1, blocking collectives, local(): parts = lax.all_to_all(grads, ('xy', 'c'), 0, 0, tiled=True).astype(F32)  15.6 us
    all_to_all x1, blocking collectives, local(): table = lax.all_to_all(out, 'z', 0, 0, tiled=True)  11.4 us
    pallas_call x2, Pallas kernels, forward(): pl.pallas_call(partial(forward_kernel, n, len(olds)), in_specs=[pl.BlockS...  10.1 us
    all_to_all x1, blocking collectives, local(): cot = lax.all_to_all(cot, 'z', 0, 0, tiled=True)  9.24 us
    pallas_call x2, Pallas kernels, backward(): pl.pallas_call(partial(backward_kernel, flip), in_specs=[pl.BlockSpec(mem...  8.02 us
    pallas_call x2, Pallas kernels, pack(): pl.pallas_call(partial(pack_kernel, shifts, first), out_shape=out_shape,...  5.49 us
  transfers between devices with their start and end apart: 8, of which 0 were waited for; matrix products, arithmetic and copies ran while one was open for 0% of the time, Pallas kernels for 13%

profile of v4, /device:TPU:1, one launch (start us, length us, event | category | flops | bytes accessed | tf_op | source)
XLA Modules:
  0.0 118.6 jit_solution(12696676975268382672)
XLA Ops:
  0.6 0.0 copy-start.6
  0.6 0.0 copy-start
  0.7 1.2 %copy-done = bf16[16,128,256]{2,1,0:T(8,128)(2,1)S(1)} copy-done((bf16[16,128,256]{2,1,0:T(8,128)(2,1)S(1)}, bf16[16,128,256]{2,1,0:T(8,128)(2,1)}, u32[]{:S(2)}) %copy-start) | copy-done | bytes 1048600
  1.9 0.0 copy-start.3
  1.9 0.7 copy-done.3
  2.6 0.0 copy-start.1
  2.6 0.0 copy-start.2
  2.6 0.0 copy-start.7
  2.6 3.2 %shard_map.120 = (bf16[2,256,256]{2,1,0:T(8,128)(2,1)S(1)}, bf16[2,256,256]{2,1,0:T(8,128)(2,1)S(1)}, bf16[2,256,256]{2,1,0:T(8,128)(2,1)}, bf16[2,256,256]{2,1,0:T(8,128)(2,1)S(1)}, s32[16,128]{1,0:T(8,128)S(1)}) custom-call(s32[16,128]{1,0:T(8,128)S(1)} %bitcast.8, bf16[2048,256]{1,0:T(8,128)(2,1)S(1)} %bitcast.6), custom_call_target="tpu_custom_call" | custom-call | tf_op jit(solution)/shard_map/pallas_call | solution.py:129
  5.7 0.0 copy-start.9
  5.7 2.5 %collective-permute-start.3 = (bf16[2,256,256]{2,1,0:T(8,128)(2,1)}, bf16[2,256,256]{2,1,0:T(8,128)(2,1)S(1)}, u32[]{:S(2)}, u32[]{:S(2)}) collective-permute-start(bf16[2,256,256]{2,1,0:T(8,128)(2,1)} %get-tuple-element.37), channel_id=1, source_target_pairs={{0,32},{32,64},{64,96},{96,128},{128,160},{160,192},{192,224},{224... | collective-permute-start | bytes 786440 | tf_op jit(solution)/shard_map/ppermute | solution.py:367
  8.2 3.9 %collective-permute-start.4 = (bf16[2,256,256]{2,1,0:T(8,128)(2,1)S(1)}, bf16[2,256,256]{2,1,0:T(8,128)(2,1)S(1)}, u32[]{:S(2)}, u32[]{:S(2)}) collective-permute-start(bf16[2,256,256]{2,1,0:T(8,128)(2,1)S(1)} %get-tuple-element.38), channel_id=1, source_target_pairs={{0,224},{32,0},{64,32},{96,64},{128,96},{160,128},{192,160},{224,1... | collective-permute-start | bytes 786440 | tf_op jit(solution)/shard_map/ppermute | solution.py:367
  12.1 0.0 collective-permute-start.5
  12.2 3.6 %collective-permute-start.6 = (bf16[2,256,256]{2,1,0:T(8,128)(2,1)S(1)}, bf16[2,256,256]{2,1,0:T(8,128)(2,1)S(1)}, u32[]{:S(2)}, u32[]{:S(2)}) collective-permute-start(bf16[2,256,256]{2,1,0:T(8,128)(2,1)S(1)} %get-tuple-element.46), channel_id=1, source_target_pairs={{0,192},{32,224},{64,0},{96,32},{128,64},{160,96},{192,128},{224,1... | collective-permute-start | bytes 786440 | tf_op jit(solution)/shard_map/ppermute | solution.py:367
  15.7 0.0 copy-done.1
  15.7 2.3 %shard_map.121 = (bf16[2,256,256]{2,1,0:T(8,128)(2,1)S(1)}, bf16[2,256,256]{2,1,0:T(8,128)(2,1)S(1)}, bf16[2,256,256]{2,1,0:T(8,128)(2,1)S(1)}, bf16[2,256,256]{2,1,0:T(8,128)(2,1)S(1)}) custom-call(s32[16,128]{1,0:T(8,128)S(1)} %get-tuple-element.33.refs_0_.slot_ref, bf16[2048,256]{1,0:T(8,128)(2,1)S(1)} %bitcast.7), custom_call_target="tpu_custom_call" | custom-call | tf_op jit(solution)/shard_map/pallas_call | solution.py:129
  18.1 0.5 collective-permute-start
  18.5 0.0 copy-done.6
  18.5 0.0 copy-done.2
  18.6 0.0 copy-done.7
  18.6 1.2 %shard_map.122 = bf16[32,2,72,128]{3,2,1,0:T(8,128)(2,1)} custom-call(bf16[2,4,8,256]{3,2,1,0:T(8,128)(2,1)S(1)} %copy-done.2, bf16[2,4,8]{2,1,0:T(4,128)(2,1)S(1)} %copy-done.6, bf16[2,4,8]{2,1,0:T(4,128)(2,1)S(1)} %copy-done.7), custom_call_target="tpu_custom_call" | custom-call | tf_op jit(solution)/shard_map/pallas_call | solution.py:52
  19.8 0.0 collective-permute-done.3.refs_1_
  19.8 4.1 %collective-permute-start.1 = (bf16[2,256,256]{2,1,0:T(8,128)(2,1)S(1)}, bf16[2,256,256]{2,1,0:T(8,128)(2,1)S(1)}, u32[]{:S(2)}, u32[]{:S(2)}) collective-permute-start(bf16[2,256,256]{2,1,0:T(8,128)(2,1)S(1)} %get-tuple-element.35), channel_id=1, source_target_pairs={{0,160},{32,192},{64,224},{96,0},{128,32},{160,64},{192,96},{224,1... | collective-permute-start | bytes 786440 | tf_op jit(solution)/shard_map/ppermute | solution.py:367
  23.9 0.0 collective-permute-done.4.refs_2_
  23.9 4.0 %collective-permute-start.2 = (bf16[2,256,256]{2,1,0:T(8,128)(2,1)S(1)}, bf16[2,256,256]{2,1,0:T(8,128)(2,1)S(1)}, u32[]{:S(2)}, u32[]{:S(2)}) collective-permute-start(bf16[2,256,256]{2,1,0:T(8,128)(2,1)S(1)} %get-tuple-element.36), channel_id=1, source_target_pairs={{0,128},{32,160},{64,192},{96,224},{128,0},{160,32},{192,64},{224,... | collective-permute-start | bytes 786440 | tf_op jit(solution)/shard_map/ppermute | solution.py:367
  27.9 0.0 copy-done.9
  27.9 0.1 pad_add_fusion.where_ref
  28.0 28.8 %conditional.1 = (bf16[32,2,72,128]{3,2,1,0:T(8,128)(2,1)}) conditional(s32[]{:T(128)} %convert_element_type.7, () %tuple.15, bf16[32,2,72,128]{3,2,1,0:T(8,128)(2,1)} %shard_map.122), branch_computations={%region_0.0_spmd, %region_1.0_spmd} | conditional | bytes 2359304 | solution.py:386
  28.0 28.8 %all_to_all.19 = bf16[32,2,72,128]{3,2,1,0:T(8,128)(2,1)} all-to-all(bf16[32,2,72,128]{3,2,1,0:T(8,128)(2,1)} %param.1), channel_id=1, replica_groups=mesh['z'=8,'xy'=16,'c'=2] {'xy','c'}, dimensions={0} | all-to-all | bytes 2359296 | tf_op jit(solution)/shard_map/cond/branch_1_fun/all_to_all | solution.py:388
  56.7 1.5 %shard_map.123 = (bf16[2,4,256,256]{3,2,1,0:T(8,128)(2,1)S(1)}, f32[2,8,256]{2,1,0:T(8,128)S(1)}) custom-call(bf16[32,2,72,128]{3,2,1,0:T(8,128)(2,1)} %get-tuple-element.58.g_ref), custom_call_target="tpu_custom_call" | custom-call | tf_op jit(solution)/shard_map/pallas_call | solution.py:70
  58.2 0.0 collective-permute-done.5.refs_3_
  58.3 0.0 collective-permute-done.6.refs_4_
  58.3 6.1 %shard_map.124 = (bf16[2,4,1280,256]{3,2,1,0:T(8,128)(2,1)S(1)}, f32[2,4,1280,256]{3,2,1,0:T(8,128)S(1)}, bf16[5,16,128]{2,1,0:T(8,128)(2,1)S(1)}) custom-call(s32[10]{0:T(128)S(1)} %pad_add_fusion.where_ref, bf16[2,256,256]{2,1,0:T(8,128)(2,1)S(1)} %get-tuple-element.42.refs_0_, bf16[2,256,256]{2,1,0:T(8,128)(2,1)S(1)} %collective-permute-done.3.refs_1_, ...), custom_call_target="tpu_custom_call" | custom-call | tf_op jit(solution)/shard_map/pallas_call | solution.py:167
  64.4 0.0 copy-start.4
  64.4 0.0 copy-start.5
  64.4 0.0 copy-start.8
  64.4 0.0 collective-permute-done.refs_0_.refs_5_
  64.4 0.0 collective-permute-done.1.refs_1_.refs_6_
  64.4 0.0 collective-permute-done.2.refs_2_.refs_7_
  64.4 4.0 %shard_map.125 = (bf16[2,4,768,256]{3,2,1,0:T(8,128)(2,1)S(1)}, f32[2,4,768,256]{3,2,1,0:T(8,128)S(1)}, bf16[8,16,128]{2,1,0:T(8,128)(2,1)S(1)}) custom-call(s32[10]{0:T(128)S(1)} %pad_add_fusion.where_ref, bf16[2,256,256]{2,1,0:T(8,128)(2,1)S(1)} %collective-permute-done.refs_0_.refs_5_, bf16[2,256,256]{2,1,0:T(8,128)(2,1)S(1)} %collective-permute-done.1.refs_1_.refs_6_, ...), custom_call_target="tpu_custom_call" | custom-call | tf_op jit(solution)/shard_map/pallas_call | solution.py:167
  68.4 11.4 %all_to_all.20.table16_ref = bf16[8,16,128]{2,1,0:T(8,128)(2,1)S(1)} all-to-all(bf16[8,16,128]{2,1,0:T(8,128)(2,1)S(1)} %get-tuple-element.48), channel_id=1, replica_groups=mesh['z'=8,'xy'=16,'c'=2] {'z'}, dimensions={0} | all-to-all | bytes 65536 | tf_op jit(solution)/shard_map/all_to_all | solution.py:401
  79.8 0.0 copy-done.4
  79.8 0.0 copy-done.5
  79.8 0.0 copy-done.8
  79.8 1.5 %shard_map.126 = (f32[3,16]{1,0:T(4,128)}, bf16[8,16,128]{2,1,0:T(8,128)(2,1)S(1)}) custom-call(bf16[8,16,128]{2,1,0:T(8,128)(2,1)S(1)} %all_to_all.20.table16_ref, s32[16,128]{1,0:T(8,128)S(1)} %get-tuple-element.33.refs_0_.slot_ref, bf16[16,128]{1,0:T(8,128)(2,1)S(1)} %copy-done.5, f32[16,128]{1,0:T(8,128)S(1)} %copy-done.4, f32[3,16]{1,0:T(4,128)S(1)} %copy-done.8), custom_call_target="tpu_custom_call" | custom-call | tf_op jit(solution)/shard_map/pallas_call | solution.py:247
  81.4 9.2 %all_to_all.21.cot_ref = bf16[8,16,128]{2,1,0:T(8,128)(2,1)S(1)} all-to-all(bf16[8,16,128]{2,1,0:T(8,128)(2,1)S(1)} %get-tuple-element.50), channel_id=1, replica_groups=mesh['z'=8,'xy'=16,'c'=2] {'z'}, dimensions={0} | all-to-all | bytes 65536 | tf_op jit(solution)/shard_map/all_to_all | solution.py:403
  90.6 4.0 %shard_map.128 = f32[32,72,128]{2,1,0:T(8,128)S(1)} custom-call(s32[10]{0:T(128)S(1)} %pad_add_fusion.where_ref, bf16[8,16,128]{2,1,0:T(8,128)(2,1)S(1)} %all_to_all.21.cot_ref, bf16[2,4,256,256]{3,2,1,0:T(8,128)(2,1)S(1)} %get-tuple-element.40.refs_5_.refs_3_.w_ref, f32[2,8,256]{2,1,0:T(8,128)S(1)} %get-tuple-element.41.refs_6_.refs_4_.v_ref, ...), custom_call_target="tpu_custom_call" | custom-call | tf_op jit(solution)/shard_map/pallas_call | solution.py:297
  94.7 3.0 %collective-permute-start.7 = (f32[32,72,128]{2,1,0:T(8,128)S(1)}, f32[32,72,128]{2,1,0:T(8,128)S(1)}, u32[]{:S(2)}, u32[]{:S(2)}) collective-permute-start(f32[32,72,128]{2,1,0:T(8,128)S(1)} %shard_map.128), channel_id=1, source_target_pairs={{0,1},{1,0},{2,3},{3,2},{4,5},{5,4},{6,7},{7,6},{8,9},{9,8},{10,11... | collective-permute-start | bytes 3538952 | tf_op jit(solution)/shard_map/ppermute | solution.py:405
  97.6 4.0 %shard_map.127.own_ref = f32[32,72,128]{2,1,0:T(8,128)S(1)} custom-call(s32[10]{0:T(128)S(1)} %pad_add_fusion.where_ref, bf16[8,16,128]{2,1,0:T(8,128)(2,1)S(1)} %all_to_all.21.cot_ref, bf16[2,4,256,256]{3,2,1,0:T(8,128)(2,1)S(1)} %get-tuple-element.40.refs_5_.refs_3_.w_ref, f32[2,8,256]{2,1,0:T(8,128)S(1)} %get-tuple-element.41.refs_6_.refs_4_.v_ref, ...), custom_call_target="tpu_custom_call" | custom-call | tf_op jit(solution)/shard_map/pallas_call | solution.py:297
  101.6 0.0 collective-permute-done.7.given_ref
  101.7 0.3 shard_map.129
  101.9 0.1 convert_element_type.8
  102.0 15.6 %all_to_all.22 = f16[32,72,128]{2,1,0:T(8,128)(2,1)S(1)} all-to-all(f16[32,72,128]{2,1,0:T(8,128)(2,1)S(1)} %convert_element_type.8), channel_id=1, replica_groups=mesh['z'=8,'xy'=16,'c'=2] {'xy','c'}, dimensions={0} | all-to-all | bytes 1179648 | tf_op jit(solution)/shard_map/all_to_all | solution.py:407
  117.6 0.1 convert.1.parts_ref
  117.7 0.9 shard_map.130
  (1 shorter events, 0.0 us)
Async XLA Ops:
  0.6 17.9 %copy-start.6 = (bf16[2,4,8]{2,1,0:T(4,128)(2,1)S(1)}, bf16[2,4,8]{2,1,0:T(4,128)(2,1)}, u32[]{:S(2)}) copy-start(bf16[2,4,8]{2,1,0:T(4,128)(2,1)} %b_ref.1) | copy-start | bytes 388
  0.6 1.2 %copy-start = (bf16[16,128,256]{2,1,0:T(8,128)(2,1)S(1)}, bf16[16,128,256]{2,1,0:T(8,128)(2,1)}, u32[]{:S(2)}) copy-start(bf16[16,128,256]{2,1,0:T(8,128)(2,1)} %param.11) | copy-start | bytes 3145732
  1.9 0.7 copy-start.3
  2.6 13.2 %copy-start.1 = (bf16[16,128,256]{2,1,0:T(8,128)(2,1)S(1)}, bf16[16,128,256]{2,1,0:T(8,128)(2,1)}, u32[]{:S(2)}) copy-start(bf16[16,128,256]{2,1,0:T(8,128)(2,1)} %param.11) | copy-start | bytes 3145732
  2.6 16.0 %copy-start.2 = (bf16[2,4,8,256]{3,2,1,0:T(8,128)(2,1)S(1)}, bf16[2,4,8,256]{3,2,1,0:T(8,128)(2,1)}, u32[]{:S(2)}) copy-start(bf16[2,4,8,256]{3,2,1,0:T(8,128)(2,1)} %w_ref.1) | copy-start | bytes 98308
  2.6 16.0 %copy-start.7 = (bf16[2,4,8]{2,1,0:T(4,128)(2,1)S(1)}, bf16[2,4,8]{2,1,0:T(4,128)(2,1)}, u32[]{:S(2)}) copy-start(bf16[2,4,8]{2,1,0:T(4,128)(2,1)} %h_ref.1) | copy-start | bytes 388
  5.7 22.1 %copy-start.9 = (s32[8]{0:T(128)S(1)}, s32[8]{0:T(128)}, u32[]{:S(2)}) copy-start(s32[8]{0:T(128)} %constant.27) | copy-start | bytes 100
  5.7 14.0 %collective-permute-start.3 = (bf16[2,256,256]{2,1,0:T(8,128)(2,1)}, bf16[2,256,256]{2,1,0:T(8,128)(2,1)S(1)}, u32[]{:S(2)}, u32[]{:S(2)}) collective-permute-start(bf16[2,256,256]{2,1,0:T(8,128)(2,1)} %get-tuple-element.37), channel_id=1, source_target_pairs={{0,32},{32,64},{64,96},{96,128},{128,160},{160,192},{192,224},{224... | collective-permute-start | bytes 786440 | tf_op jit(solution)/shard_map/ppermute | solution.py:367
  8.2 15.7 %collective-permute-start.4 = (bf16[2,256,256]{2,1,0:T(8,128)(2,1)S(1)}, bf16[2,256,256]{2,1,0:T(8,128)(2,1)S(1)}, u32[]{:S(2)}, u32[]{:S(2)}) collective-permute-start(bf16[2,256,256]{2,1,0:T(8,128)(2,1)S(1)} %get-tuple-element.38), channel_id=1, source_target_pairs={{0,224},{32,0},{64,32},{96,64},{128,96},{160,128},{192,160},{224,1... | collective-permute-start | bytes 786440 | tf_op jit(solution)/shard_map/ppermute | solution.py:367
  12.1 46.1 %collective-permute-start.5 = (bf16[2,256,256]{2,1,0:T(8,128)(2,1)S(1)}, bf16[2,256,256]{2,1,0:T(8,128)(2,1)S(1)}, u32[]{:S(2)}, u32[]{:S(2)}) collective-permute-start(bf16[2,256,256]{2,1,0:T(8,128)(2,1)S(1)} %get-tuple-element.45), channel_id=1, source_target_pairs={{0,64},{32,96},{64,128},{96,160},{128,192},{160,224},{192,0},{224,... | collective-permute-start | bytes 786440 | tf_op jit(solution)/shard_map/ppermute | solution.py:367
  12.2 46.1 %collective-permute-start.6 = (bf16[2,256,256]{2,1,0:T(8,128)(2,1)S(1)}, bf16[2,256,256]{2,1,0:T(8,128)(2,1)S(1)}, u32[]{:S(2)}, u32[]{:S(2)}) collective-permute-start(bf16[2,256,256]{2,1,0:T(8,128)(2,1)S(1)} %get-tuple-element.46), channel_id=1, source_target_pairs={{0,192},{32,224},{64,0},{96,32},{128,64},{160,96},{192,128},{224,1... | collective-permute-start | bytes 786440 | tf_op jit(solution)/shard_map/ppermute | solution.py:367
  18.1 46.4 %collective-permute-start = (bf16[2,256,256]{2,1,0:T(8,128)(2,1)S(1)}, bf16[2,256,256]{2,1,0:T(8,128)(2,1)S(1)}, u32[]{:S(2)}, u32[]{:S(2)}) collective-permute-start(bf16[2,256,256]{2,1,0:T(8,128)(2,1)S(1)} %get-tuple-element.34), channel_id=1, source_target_pairs={{0,96},{32,128},{64,160},{96,192},{128,224},{160,0},{192,32},{224,... | collective-permute-start | bytes 786440 | tf_op jit(solution)/shard_map/ppermute | solution.py:367
  19.8 44.6 %collective-permute-start.1 = (bf16[2,256,256]{2,1,0:T(8,128)(2,1)S(1)}, bf16[2,256,256]{2,1,0:T(8,128)(2,1)S(1)}, u32[]{:S(2)}, u32[]{:S(2)}) collective-permute-start(bf16[2,256,256]{2,1,0:T(8,128)(2,1)S(1)} %get-tuple-element.35), channel_id=1, source_target_pairs={{0,160},{32,192},{64,224},{96,0},{128,32},{160,64},{192,96},{224,1... | collective-permute-start | bytes 786440 | tf_op jit(solution)/shard_map/ppermute | solution.py:367
  23.9 40.6 %collective-permute-start.2 = (bf16[2,256,256]{2,1,0:T(8,128)(2,1)S(1)}, bf16[2,256,256]{2,1,0:T(8,128)(2,1)S(1)}, u32[]{:S(2)}, u32[]{:S(2)}) collective-permute-start(bf16[2,256,256]{2,1,0:T(8,128)(2,1)S(1)} %get-tuple-element.36), channel_id=1, source_target_pairs={{0,128},{32,160},{64,192},{96,224},{128,0},{160,32},{192,64},{224,... | collective-permute-start | bytes 786440 | tf_op jit(solution)/shard_map/ppermute | solution.py:367
  64.4 15.4 %copy-start.4 = (f32[16,128]{1,0:T(8,128)S(1)}, f32[16,128]{1,0:T(8,128)}, u32[]{:S(2)}) copy-start(f32[16,128]{1,0:T(8,128)} %delta_ref.1) | copy-start | bytes 24580
  64.4 15.4 %copy-start.5 = (bf16[16,128]{1,0:T(8,128)(2,1)S(1)}, bf16[16,128]{1,0:T(8,128)(2,1)}, u32[]{:S(2)}) copy-start(bf16[16,128]{1,0:T(8,128)(2,1)} %gate_ref.1) | copy-start | bytes 12292
  64.4 15.4 %copy-start.8 = (f32[3,16]{1,0:T(4,128)S(1)}, f32[3,16]{1,0:T(4,128)}, u32[]{:S(2)}) copy-start(f32[3,16]{1,0:T(4,128)} %target_ref.1) | copy-start | bytes 580
  94.7 7.0 %collective-permute-start.7 = (f32[32,72,128]{2,1,0:T(8,128)S(1)}, f32[32,72,128]{2,1,0:T(8,128)S(1)}, u32[]{:S(2)}, u32[]{:S(2)}) collective-permute-start(f32[32,72,128]{2,1,0:T(8,128)S(1)} %shard_map.128), channel_id=1, source_target_pairs={{0,1},{1,0},{2,3},{3,2},{4,5},{5,4},{6,7},{7,6},{8,9},{9,8},{10,11... | collective-permute-start | bytes 3538952 | tf_op jit(solution)/shard_map/ppermute | solution.py:405

commit v5 on v4

--- a/solution.py
+++ b/solution.py
@@ -64,17 +64,6 @@
         extra = g_ref[:, e, 64:72, :].astype(F32).reshape(D, 128)
         extra = extra.T[0:8]
         v_ref[e] = jnp.concatenate([0.5 * extra[0:4], extra[4:8]], axis=0)
-
-
-def unpack(gathered):
-    return pl.pallas_call(
-        unpack_kernel,
-        out_shape=[
-            jax.ShapeDtypeStruct((2, LAYERS, D, D), BF),
-            jax.ShapeDtypeStruct((2, 8, D), F32),
-        ],
-        compiler_params=params(),
-    )(gathered)
 
 
 def slots_of(route):
@@ -132,8 +121,13 @@
 
 
 def forward_kernel(n, olds_n, where_ref, *refs):
-    x_refs, (w_ref, v_ref), refs = refs[:n], refs[n : n + 2], refs[n + 2 :]
-    olds, (h_ref, slope_ref, out_ref) = refs[:olds_n], refs[olds_n:]
+    x_refs, refs = refs[:n], refs[n:]
+    if olds_n:
+        (w_ref, v_ref), olds, (h_ref, slope_ref, out_ref) = refs[:2], refs[2:-3], refs[-3:]
+    else:
+        g_ref, h_ref, slope_ref, out_ref, w_ref, v_ref = refs
+        olds = ()
+        unpack_kernel(g_ref, w_ref, v_ref)
     hidden = [jnp.concatenate([r[e] for r in x_refs], axis=0) for e in range(2)]
     for l in range(LAYERS):
         for e in range(2):
@@ -161,19 +155,24 @@
             out_ref[i] = one
 
 
-def forward(where, xs, w, v, olds):
+def forward(where, xs, weights, olds):
     n = len(xs)
     vmem = pl.BlockSpec(memory_space=pltpu.VMEM)
+    out_shape = [
+        jax.ShapeDtypeStruct((2, LAYERS, n * CAP, D), BF),
+        jax.ShapeDtypeStruct((2, LAYERS, n * CAP, D), F32),
+        jax.ShapeDtypeStruct((8 if olds else n, 16, 128), BF),
+    ]
+    if not olds:
+        out_shape.append(jax.ShapeDtypeStruct((2, LAYERS, D, D), BF))
+        out_shape.append(jax.ShapeDtypeStruct((2, 8, D), F32))
+    count = n + len(weights) + len(olds)
     return pl.pallas_call(
         partial(forward_kernel, n, len(olds)),
-        in_specs=[pl.BlockSpec(memory_space=pltpu.SMEM)] + [vmem] * (n + 2 + len(olds)),
-        out_shape=[
-            jax.ShapeDtypeStruct((2, LAYERS, n * CAP, D), BF),
-            jax.ShapeDtypeStruct((2, LAYERS, n * CAP, D), F32),
-            jax.ShapeDtypeStruct((8 if olds else n, 16, 128), BF),
-        ],
+        in_specs=[pl.BlockSpec(memory_space=pltpu.SMEM)] + [vmem] * count,
+        out_shape=out_shape,
         compiler_params=params(),
-    )(where, *xs, w, v, *olds)
+    )(where, *xs, *weights, *olds)
 
 
 def composite_kernel(
@@ -389,15 +388,11 @@
         jnp.zeros_like,
         copies,
     )
-    w, v = unpack(gathered)
     xs = [arrived[k] for k in SHIFTS]
-    hs, slopes, olds = [], [], []
-    for g, (pos, n) in enumerate(GROUPS):
-        last = g == len(GROUPS) - 1
-        h, slope, out = forward(where, xs[pos : pos + n], w, v, olds if last else [])
-        hs.append(h)
-        slopes.append(slope)
-        olds.append(out)
+    (pos, n), (pos2, n2) = GROUPS
+    h, slope, out, w, v = forward(where, xs[pos : pos + n], (gathered,), [])
+    h2, slope2, out = forward(where, xs[pos2 : pos2 + n2], (w, v), [out])
+    hs, slopes = (h, h2), (slope, slope2)
     table = lax.all_to_all(out, "z", 0, 0, tiled=True)
     rendered, cot = composite(table, slot, gate_values, deltas, target)
     cot = lax.all_to_all(cot, "z", 0, 0, tiled=True)

time: 119 us -> 119 us (level)
    pallas_call x1 -> x0, Pallas kernels: 1.52 us -> none  [unpack(): pl.pallas_call(unpack_kernel, out_shape=[jax.ShapeDtypeStruct((2, LAYERS,...]
where the time goes in v5:
time: 119 us; the launch traced here: 118 us
  blocking collectives  65 us (55%)
  Pallas kernels  28.7 us (24%)
  starting transfers between devices  21.5 us (18%)
  local copies, waits for them, and re-layouts  1.95 us (2%)
    all_to_all x1, blocking collectives, local(): lax.all_to_all(a, ('xy', 'c'), 0, 0, tiled=True)  28.8 us
    ppermute x7, starting transfers between devices, along(): return lax.ppermute(x, 'z', [(i, (i + k) % 8) for i in range(8)])  18.5 us
    all_to_all x1, blocking collectives, local(): parts = lax.all_to_all(grads, ('xy', 'c'), 0, 0, tiled=True).astype(F32)  15.6 us
    all_to_all x1, blocking collectives, local(): table = lax.all_to_all(out, 'z', 0, 0, tiled=True)  11.4 us
    pallas_call x2, Pallas kernels, forward(): pl.pallas_call(partial(forward_kernel, n, len(olds)), in_specs=[pl.BlockS...  11.3 us
    all_to_all x1, blocking collectives, local(): cot = lax.all_to_all(cot, 'z', 0, 0, tiled=True)  9.24 us
    pallas_call x2, Pallas kernels, backward(): pl.pallas_call(partial(backward_kernel, flip), in_specs=[pl.BlockSpec(mem...  8.02 us
    pallas_call x2, Pallas kernels, pack(): pl.pallas_call(partial(pack_kernel, shifts, first), out_shape=out_shape,...  5.49 us
  transfers between devices with their start and end apart: 8, of which 0 were waited for; matrix products, arithmetic and copies ran while one was open for 0% of the time, Pallas kernels for 13%

profile of v5, /device:TPU:1, one launch (start us, length us, event | category | flops | bytes accessed | tf_op | source)
XLA Modules:
  0.0 118.2 jit_solution(14261012764455076841)
XLA Ops:
  0.6 0.0 copy-start.6
  0.6 0.0 copy-start
  0.7 1.2 %copy-done = bf16[16,128,256]{2,1,0:T(8,128)(2,1)S(1)} copy-done((bf16[16,128,256]{2,1,0:T(8,128)(2,1)S(1)}, bf16[16,128,256]{2,1,0:T(8,128)(2,1)}, u32[]{:S(2)}) %copy-start) | copy-done | bytes 1048600
  1.9 0.0 copy-start.3
  1.9 0.7 copy-done.3
  2.6 0.0 copy-start.1
  2.6 0.0 copy-start.2
  2.6 0.0 copy-start.7
  2.6 3.2 %shard_map.120 = (bf16[2,256,256]{2,1,0:T(8,128)(2,1)S(1)}, bf16[2,256,256]{2,1,0:T(8,128)(2,1)S(1)}, bf16[2,256,256]{2,1,0:T(8,128)(2,1)}, bf16[2,256,256]{2,1,0:T(8,128)(2,1)S(1)}, s32[16,128]{1,0:T(8,128)S(1)}) custom-call(s32[16,128]{1,0:T(8,128)S(1)} %bitcast.8, bf16[2048,256]{1,0:T(8,128)(2,1)S(1)} %bitcast.6), custom_call_target="tpu_custom_call" | custom-call | tf_op jit(solution)/shard_map/pallas_call | solution.py:118
  5.7 0.0 copy-start.9
  5.7 2.5 %collective-permute-start.3 = (bf16[2,256,256]{2,1,0:T(8,128)(2,1)}, bf16[2,256,256]{2,1,0:T(8,128)(2,1)S(1)}, u32[]{:S(2)}, u32[]{:S(2)}) collective-permute-start(bf16[2,256,256]{2,1,0:T(8,128)(2,1)} %get-tuple-element.38), channel_id=1, source_target_pairs={{0,32},{32,64},{64,96},{96,128},{128,160},{160,192},{192,224},{224... | collective-permute-start | bytes 786440 | tf_op jit(solution)/shard_map/ppermute | solution.py:366
  8.2 3.9 %collective-permute-start.4 = (bf16[2,256,256]{2,1,0:T(8,128)(2,1)S(1)}, bf16[2,256,256]{2,1,0:T(8,128)(2,1)S(1)}, u32[]{:S(2)}, u32[]{:S(2)}) collective-permute-start(bf16[2,256,256]{2,1,0:T(8,128)(2,1)S(1)} %get-tuple-element.39), channel_id=1, source_target_pairs={{0,224},{32,0},{64,32},{96,64},{128,96},{160,128},{192,160},{224,1... | collective-permute-start | bytes 786440 | tf_op jit(solution)/shard_map/ppermute | solution.py:366
  12.2 0.0 collective-permute-start.5
  12.2 3.6 %collective-permute-start.6 = (bf16[2,256,256]{2,1,0:T(8,128)(2,1)S(1)}, bf16[2,256,256]{2,1,0:T(8,128)(2,1)S(1)}, u32[]{:S(2)}, u32[]{:S(2)}) collective-permute-start(bf16[2,256,256]{2,1,0:T(8,128)(2,1)S(1)} %get-tuple-element.43), channel_id=1, source_target_pairs={{0,192},{32,224},{64,0},{96,32},{128,64},{160,96},{192,128},{224,1... | collective-permute-start | bytes 786440 | tf_op jit(solution)/shard_map/ppermute | solution.py:366
  15.7 0.0 copy-done.1
  15.7 2.3 %shard_map.121 = (bf16[2,256,256]{2,1,0:T(8,128)(2,1)S(1)}, bf16[2,256,256]{2,1,0:T(8,128)(2,1)S(1)}, bf16[2,256,256]{2,1,0:T(8,128)(2,1)S(1)}, bf16[2,256,256]{2,1,0:T(8,128)(2,1)S(1)}) custom-call(s32[16,128]{1,0:T(8,128)S(1)} %get-tuple-element.33.refs_0_.slot_ref, bf16[2048,256]{1,0:T(8,128)(2,1)S(1)} %bitcast.7), custom_call_target="tpu_custom_call" | custom-call | tf_op jit(solution)/shard_map/pallas_call | solution.py:118
  18.1 0.5 collective-permute-start
  18.5 0.0 copy-done.6
  18.6 0.0 copy-done.2
  18.6 0.0 copy-done.7
  18.6 1.2 %shard_map.122 = bf16[32,2,72,128]{3,2,1,0:T(8,128)(2,1)} custom-call(bf16[2,4,8,256]{3,2,1,0:T(8,128)(2,1)S(1)} %copy-done.2, bf16[2,4,8]{2,1,0:T(4,128)(2,1)S(1)} %copy-done.6, bf16[2,4,8]{2,1,0:T(4,128)(2,1)S(1)} %copy-done.7), custom_call_target="tpu_custom_call" | custom-call | tf_op jit(solution)/shard_map/pallas_call | solution.py:52
  19.8 0.0 collective-permute-done.3.refs_1_
  19.8 4.1 %collective-permute-start.1 = (bf16[2,256,256]{2,1,0:T(8,128)(2,1)S(1)}, bf16[2,256,256]{2,1,0:T(8,128)(2,1)S(1)}, u32[]{:S(2)}, u32[]{:S(2)}) collective-permute-start(bf16[2,256,256]{2,1,0:T(8,128)(2,1)S(1)} %get-tuple-element.35), channel_id=1, source_target_pairs={{0,160},{32,192},{64,224},{96,0},{128,32},{160,64},{192,96},{224,1... | collective-permute-start | bytes 786440 | tf_op jit(solution)/shard_map/ppermute | solution.py:366
  23.8 0.0 collective-permute-done.4.refs_2_
  23.9 4.0 %collective-permute-start.2 = (bf16[2,256,256]{2,1,0:T(8,128)(2,1)S(1)}, bf16[2,256,256]{2,1,0:T(8,128)(2,1)S(1)}, u32[]{:S(2)}, u32[]{:S(2)}) collective-permute-start(bf16[2,256,256]{2,1,0:T(8,128)(2,1)S(1)} %get-tuple-element.36), channel_id=1, source_target_pairs={{0,128},{32,160},{64,192},{96,224},{128,0},{160,32},{192,64},{224,... | collective-permute-start | bytes 786440 | tf_op jit(solution)/shard_map/ppermute | solution.py:366
  27.9 0.0 copy-done.9
  27.9 0.1 pad_add_fusion.where_ref
  27.9 28.8 %conditional.1 = (bf16[32,2,72,128]{3,2,1,0:T(8,128)(2,1)}) conditional(s32[]{:T(128)} %convert_element_type.7, () %tuple.16, bf16[32,2,72,128]{3,2,1,0:T(8,128)(2,1)} %shard_map.122), branch_computations={%region_0.0_spmd, %region_1.0_spmd} | conditional | bytes 2359304 | solution.py:385
  27.9 28.8 %all_to_all.19 = bf16[32,2,72,128]{3,2,1,0:T(8,128)(2,1)} all-to-all(bf16[32,2,72,128]{3,2,1,0:T(8,128)(2,1)} %param.1), channel_id=1, replica_groups=mesh['z'=8,'xy'=16,'c'=2] {'xy','c'}, dimensions={0} | all-to-all | bytes 2359296 | tf_op jit(solution)/shard_map/cond/branch_1_fun/all_to_all | solution.py:387
  56.7 0.0 collective-permute-done.5.refs_3_
  56.7 0.0 collective-permute-done.6.refs_4_
  56.7 7.3 %shard_map.123 = (bf16[2,4,1280,256]{3,2,1,0:T(8,128)(2,1)S(1)}, f32[2,4,1280,256]{3,2,1,0:T(8,128)S(1)}, bf16[5,16,128]{2,1,0:T(8,128)(2,1)S(1)}, bf16[2,4,256,256]{3,2,1,0:T(8,128)(2,1)S(1)}, f32[2,8,256]{2,1,0:T(8,128)S(1)}) custom-call(s32[10]{0:T(128)S(1)} %pad_add_fusion.where_ref, bf16[2,256,256]{2,1,0:T(8,128)(2,1)S(1)} %get-tuple-element.37.refs_0_, ...), custom_call_target="tpu_custom_call" | custom-call | tf_op jit(solution)/shard_map/pallas_call | solution.py:170
  64.0 0.0 copy-start.4
  64.0 0.0 copy-start.5
  64.0 0.0 copy-start.8
  64.0 0.0 collective-permute-done.refs_0_.refs_5_
  64.0 0.0 collective-permute-done.1.refs_1_.refs_6_
  64.1 0.0 collective-permute-done.2.refs_2_.refs_7_
  64.1 4.0 %shard_map.124 = (bf16[2,4,768,256]{3,2,1,0:T(8,128)(2,1)S(1)}, f32[2,4,768,256]{3,2,1,0:T(8,128)S(1)}, bf16[8,16,128]{2,1,0:T(8,128)(2,1)S(1)}) custom-call(s32[10]{0:T(128)S(1)} %pad_add_fusion.where_ref, bf16[2,256,256]{2,1,0:T(8,128)(2,1)S(1)} %collective-permute-done.refs_0_.refs_5_, bf16[2,256,256]{2,1,0:T(8,128)(2,1)S(1)} %collective-permute-done.1.refs_1_.refs_6_, ...), custom_call_target="tpu_custom_call" | custom-call | tf_op jit(solution)/shard_map/pallas_call | solution.py:170
  68.0 11.4 %all_to_all.20.table16_ref = bf16[8,16,128]{2,1,0:T(8,128)(2,1)S(1)} all-to-all(bf16[8,16,128]{2,1,0:T(8,128)(2,1)S(1)} %get-tuple-element.48), channel_id=1, replica_groups=mesh['z'=8,'xy'=16,'c'=2] {'z'}, dimensions={0} | all-to-all | bytes 65536 | tf_op jit(solution)/shard_map/all_to_all | solution.py:396
  79.5 0.0 copy-done.4
  79.5 0.0 copy-done.5
  79.5 0.0 copy-done.8
  79.5 1.5 %shard_map.125 = (f32[3,16]{1,0:T(4,128)}, bf16[8,16,128]{2,1,0:T(8,128)(2,1)S(1)}) custom-call(bf16[8,16,128]{2,1,0:T(8,128)(2,1)S(1)} %all_to_all.20.table16_ref, s32[16,128]{1,0:T(8,128)S(1)} %get-tuple-element.33.refs_0_.slot_ref, bf16[16,128]{1,0:T(8,128)(2,1)S(1)} %copy-done.5, f32[16,128]{1,0:T(8,128)S(1)} %copy-done.4, f32[3,16]{1,0:T(4,128)S(1)} %copy-done.8), custom_call_target="tpu_custom_call" | custom-call | tf_op jit(solution)/shard_map/pallas_call | solution.py:246
  81.0 9.2 %all_to_all.21.cot_ref = bf16[8,16,128]{2,1,0:T(8,128)(2,1)S(1)} all-to-all(bf16[8,16,128]{2,1,0:T(8,128)(2,1)S(1)} %get-tuple-element.50), channel_id=1, replica_groups=mesh['z'=8,'xy'=16,'c'=2] {'z'}, dimensions={0} | all-to-all | bytes 65536 | tf_op jit(solution)/shard_map/all_to_all | solution.py:398
  90.3 4.0 %shard_map.127 = f32[32,72,128]{2,1,0:T(8,128)S(1)} custom-call(s32[10]{0:T(128)S(1)} %pad_add_fusion.where_ref, bf16[8,16,128]{2,1,0:T(8,128)(2,1)S(1)} %all_to_all.21.cot_ref, bf16[2,4,256,256]{3,2,1,0:T(8,128)(2,1)S(1)} %get-tuple-element.45.refs_3_.w_ref, f32[2,8,256]{2,1,0:T(8,128)S(1)} %get-tuple-element.46.refs_4_.v_ref, ...), custom_call_target="tpu_custom_call" | custom-call | tf_op jit(solution)/shard_map/pallas_call | solution.py:296
  94.3 3.0 %collective-permute-start.7 = (f32[32,72,128]{2,1,0:T(8,128)S(1)}, f32[32,72,128]{2,1,0:T(8,128)S(1)}, u32[]{:S(2)}, u32[]{:S(2)}) collective-permute-start(f32[32,72,128]{2,1,0:T(8,128)S(1)} %shard_map.127), channel_id=1, source_target_pairs={{0,1},{1,0},{2,3},{3,2},{4,5},{5,4},{6,7},{7,6},{8,9},{9,8},{10,11... | collective-permute-start | bytes 3538952 | tf_op jit(solution)/shard_map/ppermute | solution.py:400
  97.2 4.0 %shard_map.126.own_ref = f32[32,72,128]{2,1,0:T(8,128)S(1)} custom-call(s32[10]{0:T(128)S(1)} %pad_add_fusion.where_ref, bf16[8,16,128]{2,1,0:T(8,128)(2,1)S(1)} %all_to_all.21.cot_ref, bf16[2,4,256,256]{3,2,1,0:T(8,128)(2,1)S(1)} %get-tuple-element.45.refs_3_.w_ref, f32[2,8,256]{2,1,0:T(8,128)S(1)} %get-tuple-element.46.refs_4_.v_ref, ...), custom_call_target="tpu_custom_call" | custom-call | tf_op jit(solution)/shard_map/pallas_call | solution.py:296
  101.3 0.0 collective-permute-done.7.given_ref
  101.3 0.3 shard_map.128
  101.6 0.1 convert_element_type.8
  101.7 15.6 %all_to_all.22 = f16[32,72,128]{2,1,0:T(8,128)(2,1)S(1)} all-to-all(f16[32,72,128]{2,1,0:T(8,128)(2,1)S(1)} %convert_element_type.8), channel_id=1, replica_groups=mesh['z'=8,'xy'=16,'c'=2] {'xy','c'}, dimensions={0} | all-to-all | bytes 1179648 | tf_op jit(solution)/shard_map/all_to_all | solution.py:402
  117.2 0.1 convert.1.parts_ref
  117.3 0.9 shard_map.129
  (1 shorter events, 0.0 us)
Async XLA Ops:
  0.6 17.9 %copy-start.6 = (bf16[2,4,8]{2,1,0:T(4,128)(2,1)S(1)}, bf16[2,4,8]{2,1,0:T(4,128)(2,1)}, u32[]{:S(2)}) copy-start(bf16[2,4,8]{2,1,0:T(4,128)(2,1)} %b_ref.1) | copy-start | bytes 388
  0.6 1.2 %copy-start = (bf16[16,128,256]{2,1,0:T(8,128)(2,1)S(1)}, bf16[16,128,256]{2,1,0:T(8,128)(2,1)}, u32[]{:S(2)}) copy-start(bf16[16,128,256]{2,1,0:T(8,128)(2,1)} %param.11) | copy-start | bytes 3145732
  1.9 0.7 copy-start.3
  2.6 13.2 %copy-start.1 = (bf16[16,128,256]{2,1,0:T(8,128)(2,1)S(1)}, bf16[16,128,256]{2,1,0:T(8,128)(2,1)}, u32[]{:S(2)}) copy-start(bf16[16,128,256]{2,1,0:T(8,128)(2,1)} %param.11) | copy-start | bytes 3145732
  2.6 16.0 %copy-start.2 = (bf16[2,4,8,256]{3,2,1,0:T(8,128)(2,1)S(1)}, bf16[2,4,8,256]{3,2,1,0:T(8,128)(2,1)}, u32[]{:S(2)}) copy-start(bf16[2,4,8,256]{3,2,1,0:T(8,128)(2,1)} %w_ref.1) | copy-start | bytes 98308
  2.6 16.0 %copy-start.7 = (bf16[2,4,8]{2,1,0:T(4,128)(2,1)S(1)}, bf16[2,4,8]{2,1,0:T(4,128)(2,1)}, u32[]{:S(2)}) copy-start(bf16[2,4,8]{2,1,0:T(4,128)(2,1)} %h_ref.1) | copy-start | bytes 388
  5.7 22.1 %copy-start.9 = (s32[8]{0:T(128)S(1)}, s32[8]{0:T(128)}, u32[]{:S(2)}) copy-start(s32[8]{0:T(128)} %constant.27) | copy-start | bytes 100
  5.7 14.0 %collective-permute-start.3 = (bf16[2,256,256]{2,1,0:T(8,128)(2,1)}, bf16[2,256,256]{2,1,0:T(8,128)(2,1)S(1)}, u32[]{:S(2)}, u32[]{:S(2)}) collective-permute-start(bf16[2,256,256]{2,1,0:T(8,128)(2,1)} %get-tuple-element.38), channel_id=1, source_target_pairs={{0,32},{32,64},{64,96},{96,128},{128,160},{160,192},{192,224},{224... | collective-permute-start | bytes 786440 | tf_op jit(solution)/shard_map/ppermute | solution.py:366
  8.2 15.6 %collective-permute-start.4 = (bf16[2,256,256]{2,1,0:T(8,128)(2,1)S(1)}, bf16[2,256,256]{2,1,0:T(8,128)(2,1)S(1)}, u32[]{:S(2)}, u32[]{:S(2)}) collective-permute-start(bf16[2,256,256]{2,1,0:T(8,128)(2,1)S(1)} %get-tuple-element.39), channel_id=1, source_target_pairs={{0,224},{32,0},{64,32},{96,64},{128,96},{160,128},{192,160},{224,1... | collective-permute-start | bytes 786440 | tf_op jit(solution)/shard_map/ppermute | solution.py:366
  12.2 44.6 %collective-permute-start.5 = (bf16[2,256,256]{2,1,0:T(8,128)(2,1)S(1)}, bf16[2,256,256]{2,1,0:T(8,128)(2,1)S(1)}, u32[]{:S(2)}, u32[]{:S(2)}) collective-permute-start(bf16[2,256,256]{2,1,0:T(8,128)(2,1)S(1)} %get-tuple-element.42), channel_id=1, source_target_pairs={{0,64},{32,96},{64,128},{96,160},{128,192},{160,224},{192,0},{224,... | collective-permute-start | bytes 786440 | tf_op jit(solution)/shard_map/ppermute | solution.py:366
  12.2 44.6 %collective-permute-start.6 = (bf16[2,256,256]{2,1,0:T(8,128)(2,1)S(1)}, bf16[2,256,256]{2,1,0:T(8,128)(2,1)S(1)}, u32[]{:S(2)}, u32[]{:S(2)}) collective-permute-start(bf16[2,256,256]{2,1,0:T(8,128)(2,1)S(1)} %get-tuple-element.43), channel_id=1, source_target_pairs={{0,192},{32,224},{64,0},{96,32},{128,64},{160,96},{192,128},{224,1... | collective-permute-start | bytes 786440 | tf_op jit(solution)/shard_map/ppermute | solution.py:366
  18.1 46.0 %collective-permute-start = (bf16[2,256,256]{2,1,0:T(8,128)(2,1)S(1)}, bf16[2,256,256]{2,1,0:T(8,128)(2,1)S(1)}, u32[]{:S(2)}, u32[]{:S(2)}) collective-permute-start(bf16[2,256,256]{2,1,0:T(8,128)(2,1)S(1)} %get-tuple-element.34), channel_id=1, source_target_pairs={{0,96},{32,128},{64,160},{96,192},{128,224},{160,0},{192,32},{224,... | collective-permute-start | bytes 786440 | tf_op jit(solution)/shard_map/ppermute | solution.py:366
  19.8 44.3 %collective-permute-start.1 = (bf16[2,256,256]{2,1,0:T(8,128)(2,1)S(1)}, bf16[2,256,256]{2,1,0:T(8,128)(2,1)S(1)}, u32[]{:S(2)}, u32[]{:S(2)}) collective-permute-start(bf16[2,256,256]{2,1,0:T(8,128)(2,1)S(1)} %get-tuple-element.35), channel_id=1, source_target_pairs={{0,160},{32,192},{64,224},{96,0},{128,32},{160,64},{192,96},{224,1... | collective-permute-start | bytes 786440 | tf_op jit(solution)/shard_map/ppermute | solution.py:366
  23.9 40.2 %collective-permute-start.2 = (bf16[2,256,256]{2,1,0:T(8,128)(2,1)S(1)}, bf16[2,256,256]{2,1,0:T(8,128)(2,1)S(1)}, u32[]{:S(2)}, u32[]{:S(2)}) collective-permute-start(bf16[2,256,256]{2,1,0:T(8,128)(2,1)S(1)} %get-tuple-element.36), channel_id=1, source_target_pairs={{0,128},{32,160},{64,192},{96,224},{128,0},{160,32},{192,64},{224,... | collective-permute-start | bytes 786440 | tf_op jit(solution)/shard_map/ppermute | solution.py:366
  64.0 15.5 %copy-start.4 = (f32[16,128]{1,0:T(8,128)S(1)}, f32[16,128]{1,0:T(8,128)}, u32[]{:S(2)}) copy-start(f32[16,128]{1,0:T(8,128)} %delta_ref.1) | copy-start | bytes 24580
  64.0 15.5 %copy-start.5 = (bf16[16,128]{1,0:T(8,128)(2,1)S(1)}, bf16[16,128]{1,0:T(8,128)(2,1)}, u32[]{:S(2)}) copy-start(bf16[16,128]{1,0:T(8,128)(2,1)} %gate_ref.1) | copy-start | bytes 12292
  64.0 15.4 %copy-start.8 = (f32[3,16]{1,0:T(4,128)S(1)}, f32[3,16]{1,0:T(4,128)}, u32[]{:S(2)}) copy-start(f32[3,16]{1,0:T(4,128)} %target_ref.1) | copy-start | bytes 580
  94.3 7.0 %collective-permute-start.7 = (f32[32,72,128]{2,1,0:T(8,128)S(1)}, f32[32,72,128]{2,1,0:T(8,128)S(1)}, u32[]{:S(2)}, u32[]{:S(2)}) collective-permute-start(f32[32,72,128]{2,1,0:T(8,128)S(1)} %shard_map.127), channel_id=1, source_target_pairs={{0,1},{1,0},{2,3},{3,2},{4,5},{5,4},{6,7},{7,6},{8,9},{9,8},{10,11... | collective-permute-start | bytes 3538952 | tf_op jit(solution)/shard_map/ppermute | solution.py:400

commit v6 on v5

--- a/solution.py
+++ b/solution.py
@@ -280,7 +280,7 @@
             else:
                 below = jnp.concatenate([x_refs[pos + i][e] for i in range(n)], axis=0)
             total = total + dot(below, grad_pre, ((0,), (0,)))
-            shift = shift + dot(jnp.ones((8, n * CAP), BF), grad_pre, ((1,), (0,)))[0:1]
+            shift = shift + jnp.sum(grad_pre.astype(F32), axis=0, keepdims=True)
             if l > 0:
                 grads[g] = dot(grad_pre, w_ref[e, l], ((1,), (1,)))
         shifts[l] = shift

time: 119 us -> 117 us (0.983)
  Pallas kernels: 28.7 us -> 27.1 us
    pallas_call x2, Pallas kernels: 8.02 us -> 6.41 us  [backward(): pl.pallas_call(partial(backward_kernel, flip), in_specs=[pl.BlockSpec(mem...]
  transfers between devices with their start and end apart: 8 -> 8, of which waited for: 0 -> 0; matrix products, arithmetic and copies ran while one was open for 0% -> 0% of each run, Pallas kernels for 13% -> 12%
where the time goes in v6:
time: 117 us
  blocking collectives  65 us (56%)
  Pallas kernels  27.1 us (23%)
  starting transfers between devices  21.5 us (18%)
  local copies, waits for them, and re-layouts  1.95 us (2%)
    all_to_all x1, blocking collectives, local(): lax.all_to_all(a, ('xy', 'c'), 0, 0, tiled=True)  28.8 us
    ppermute x7, starting transfers between devices, along(): return lax.ppermute(x, 'z', [(i, (i + k) % 8) for i in range(8)])  18.5 us
    all_to_all x1, blocking collectives, local(): parts = lax.all_to_all(grads, ('xy', 'c'), 0, 0, tiled=True).astype(F32)  15.6 us
    all_to_all x1, blocking collectives, local(): table = lax.all_to_all(out, 'z', 0, 0, tiled=True)  11.4 us
    pallas_call x2, Pallas kernels, forward(): pl.pallas_call(partial(forward_kernel, n, len(olds)), in_specs=[pl.BlockS...  11.3 us
    all_to_all x1, blocking collectives, local(): cot = lax.all_to_all(cot, 'z', 0, 0, tiled=True)  9.24 us
    pallas_call x2, Pallas kernels, backward(): pl.pallas_call(partial(backward_kernel, flip), in_specs=[pl.BlockSpec(mem...  6.41 us
    pallas_call x2, Pallas kernels, pack(): pl.pallas_call(partial(pack_kernel, shifts, first), out_shape=out_shape,...  5.49 us
  transfers between devices with their start and end apart: 8, of which 0 were waited for; matrix products, arithmetic and copies ran while one was open for 0% of the time, Pallas kernels for 12%

profile of v6, /device:TPU:1, one launch (start us, length us, event | category | flops | bytes accessed | tf_op | source)
XLA Modules:
  0.0 116.6 jit_solution(10661636444903173912)
XLA Ops:
  0.6 0.0 copy-start.6
  0.6 0.0 copy-start
  0.7 1.2 %copy-done = bf16[16,128,256]{2,1,0:T(8,128)(2,1)S(1)} copy-done((bf16[16,128,256]{2,1,0:T(8,128)(2,1)S(1)}, bf16[16,128,256]{2,1,0:T(8,128)(2,1)}, u32[]{:S(2)}) %copy-start) | copy-done | bytes 1048600
  1.9 0.0 copy-start.3
  1.9 0.7 copy-done.3
  2.6 0.0 copy-start.1
  2.6 0.0 copy-start.2
  2.6 0.0 copy-start.7
  2.6 3.2 %shard_map.120 = (bf16[2,256,256]{2,1,0:T(8,128)(2,1)S(1)}, bf16[2,256,256]{2,1,0:T(8,128)(2,1)S(1)}, bf16[2,256,256]{2,1,0:T(8,128)(2,1)}, bf16[2,256,256]{2,1,0:T(8,128)(2,1)S(1)}, s32[16,128]{1,0:T(8,128)S(1)}) custom-call(s32[16,128]{1,0:T(8,128)S(1)} %bitcast.8, bf16[2048,256]{1,0:T(8,128)(2,1)S(1)} %bitcast.6), custom_call_target="tpu_custom_call" | custom-call | tf_op jit(solution)/shard_map/pallas_call | solution.py:118
  5.7 0.0 copy-start.9
  5.7 2.5 %collective-permute-start.3 = (bf16[2,256,256]{2,1,0:T(8,128)(2,1)}, bf16[2,256,256]{2,1,0:T(8,128)(2,1)S(1)}, u32[]{:S(2)}, u32[]{:S(2)}) collective-permute-start(bf16[2,256,256]{2,1,0:T(8,128)(2,1)} %get-tuple-element.38), channel_id=1, source_target_pairs={{0,32},{32,64},{64,96},{96,128},{128,160},{160,192},{192,224},{224... | collective-permute-start | bytes 786440 | tf_op jit(solution)/shard_map/ppermute | solution.py:366
  8.2 3.9 %collective-permute-start.4 = (bf16[2,256,256]{2,1,0:T(8,128)(2,1)S(1)}, bf16[2,256,256]{2,1,0:T(8,128)(2,1)S(1)}, u32[]{:S(2)}, u32[]{:S(2)}) collective-permute-start(bf16[2,256,256]{2,1,0:T(8,128)(2,1)S(1)} %get-tuple-element.39), channel_id=1, source_target_pairs={{0,224},{32,0},{64,32},{96,64},{128,96},{160,128},{192,160},{224,1... | collective-permute-start | bytes 786440 | tf_op jit(solution)/shard_map/ppermute | solution.py:366
  12.2 0.0 collective-permute-start.5
  12.2 3.6 %collective-permute-start.6 = (bf16[2,256,256]{2,1,0:T(8,128)(2,1)S(1)}, bf16[2,256,256]{2,1,0:T(8,128)(2,1)S(1)}, u32[]{:S(2)}, u32[]{:S(2)}) collective-permute-start(bf16[2,256,256]{2,1,0:T(8,128)(2,1)S(1)} %get-tuple-element.43), channel_id=1, source_target_pairs={{0,192},{32,224},{64,0},{96,32},{128,64},{160,96},{192,128},{224,1... | collective-permute-start | bytes 786440 | tf_op jit(solution)/shard_map/ppermute | solution.py:366
  15.7 0.0 copy-done.1
  15.7 2.3 %shard_map.121 = (bf16[2,256,256]{2,1,0:T(8,128)(2,1)S(1)}, bf16[2,256,256]{2,1,0:T(8,128)(2,1)S(1)}, bf16[2,256,256]{2,1,0:T(8,128)(2,1)S(1)}, bf16[2,256,256]{2,1,0:T(8,128)(2,1)S(1)}) custom-call(s32[16,128]{1,0:T(8,128)S(1)} %get-tuple-element.33.refs_0_.slot_ref, bf16[2048,256]{1,0:T(8,128)(2,1)S(1)} %bitcast.7), custom_call_target="tpu_custom_call" | custom-call | tf_op jit(solution)/shard_map/pallas_call | solution.py:118
  18.1 0.5 collective-permute-start
  18.5 0.0 copy-done.6
  18.6 0.0 copy-done.2
  18.6 0.0 copy-done.7
  18.6 1.2 %shard_map.122 = bf16[32,2,72,128]{3,2,1,0:T(8,128)(2,1)} custom-call(bf16[2,4,8,256]{3,2,1,0:T(8,128)(2,1)S(1)} %copy-done.2, bf16[2,4,8]{2,1,0:T(4,128)(2,1)S(1)} %copy-done.6, bf16[2,4,8]{2,1,0:T(4,128)(2,1)S(1)} %copy-done.7), custom_call_target="tpu_custom_call" | custom-call | tf_op jit(solution)/shard_map/pallas_call | solution.py:52
  19.8 0.0 collective-permute-done.3.refs_1_
  19.8 4.1 %collective-permute-start.1 = (bf16[2,256,256]{2,1,0:T(8,128)(2,1)S(1)}, bf16[2,256,256]{2,1,0:T(8,128)(2,1)S(1)}, u32[]{:S(2)}, u32[]{:S(2)}) collective-permute-start(bf16[2,256,256]{2,1,0:T(8,128)(2,1)S(1)} %get-tuple-element.35), channel_id=1, source_target_pairs={{0,160},{32,192},{64,224},{96,0},{128,32},{160,64},{192,96},{224,1... | collective-permute-start | bytes 786440 | tf_op jit(solution)/shard_map/ppermute | solution.py:366
  23.8 0.0 collective-permute-done.4.refs_2_
  23.9 4.0 %collective-permute-start.2 = (bf16[2,256,256]{2,1,0:T(8,128)(2,1)S(1)}, bf16[2,256,256]{2,1,0:T(8,128)(2,1)S(1)}, u32[]{:S(2)}, u32[]{:S(2)}) collective-permute-start(bf16[2,256,256]{2,1,0:T(8,128)(2,1)S(1)} %get-tuple-element.36), channel_id=1, source_target_pairs={{0,128},{32,160},{64,192},{96,224},{128,0},{160,32},{192,64},{224,... | collective-permute-start | bytes 786440 | tf_op jit(solution)/shard_map/ppermute | solution.py:366
  27.9 0.0 copy-done.9
  27.9 0.1 pad_add_fusion.where_ref
  27.9 28.8 %conditional.1 = (bf16[32,2,72,128]{3,2,1,0:T(8,128)(2,1)}) conditional(s32[]{:T(128)} %convert_element_type.7, () %tuple.16, bf16[32,2,72,128]{3,2,1,0:T(8,128)(2,1)} %shard_map.122), branch_computations={%region_0.0_spmd, %region_1.0_spmd} | conditional | bytes 2359304 | solution.py:385
  27.9 28.8 %all_to_all.19 = bf16[32,2,72,128]{3,2,1,0:T(8,128)(2,1)} all-to-all(bf16[32,2,72,128]{3,2,1,0:T(8,128)(2,1)} %param.1), channel_id=1, replica_groups=mesh['z'=8,'xy'=16,'c'=2] {'xy','c'}, dimensions={0} | all-to-all | bytes 2359296 | tf_op jit(solution)/shard_map/cond/branch_1_fun/all_to_all | solution.py:387
  56.7 0.0 collective-permute-done.5.refs_3_
  56.7 0.0 collective-permute-done.6.refs_4_
  56.7 7.3 %shard_map.123 = (bf16[2,4,1280,256]{3,2,1,0:T(8,128)(2,1)S(1)}, f32[2,4,1280,256]{3,2,1,0:T(8,128)S(1)}, bf16[5,16,128]{2,1,0:T(8,128)(2,1)S(1)}, bf16[2,4,256,256]{3,2,1,0:T(8,128)(2,1)S(1)}, f32[2,8,256]{2,1,0:T(8,128)S(1)}) custom-call(s32[10]{0:T(128)S(1)} %pad_add_fusion.where_ref, bf16[2,256,256]{2,1,0:T(8,128)(2,1)S(1)} %get-tuple-element.37.refs_0_, ...), custom_call_target="tpu_custom_call" | custom-call | tf_op jit(solution)/shard_map/pallas_call | solution.py:170
  64.0 0.0 copy-start.4
  64.0 0.0 copy-start.5
  64.0 0.0 copy-start.8
  64.0 0.0 collective-permute-done.refs_0_.refs_5_
  64.0 0.0 collective-permute-done.1.refs_1_.refs_6_
  64.1 0.0 collective-permute-done.2.refs_2_.refs_7_
  64.1 4.0 %shard_map.124 = (bf16[2,4,768,256]{3,2,1,0:T(8,128)(2,1)S(1)}, f32[2,4,768,256]{3,2,1,0:T(8,128)S(1)}, bf16[8,16,128]{2,1,0:T(8,128)(2,1)S(1)}) custom-call(s32[10]{0:T(128)S(1)} %pad_add_fusion.where_ref, bf16[2,256,256]{2,1,0:T(8,128)(2,1)S(1)} %collective-permute-done.refs_0_.refs_5_, bf16[2,256,256]{2,1,0:T(8,128)(2,1)S(1)} %collective-permute-done.1.refs_1_.refs_6_, ...), custom_call_target="tpu_custom_call" | custom-call | tf_op jit(solution)/shard_map/pallas_call | solution.py:170
  68.0 11.4 %all_to_all.20.table16_ref = bf16[8,16,128]{2,1,0:T(8,128)(2,1)S(1)} all-to-all(bf16[8,16,128]{2,1,0:T(8,128)(2,1)S(1)} %get-tuple-element.48), channel_id=1, replica_groups=mesh['z'=8,'xy'=16,'c'=2] {'z'}, dimensions={0} | all-to-all | bytes 65536 | tf_op jit(solution)/shard_map/all_to_all | solution.py:396
  79.5 0.0 copy-done.4
  79.5 0.0 copy-done.5
  79.5 0.0 copy-done.8
  79.5 1.5 %shard_map.125 = (f32[3,16]{1,0:T(4,128)}, bf16[8,16,128]{2,1,0:T(8,128)(2,1)S(1)}) custom-call(bf16[8,16,128]{2,1,0:T(8,128)(2,1)S(1)} %all_to_all.20.table16_ref, s32[16,128]{1,0:T(8,128)S(1)} %get-tuple-element.33.refs_0_.slot_ref, bf16[16,128]{1,0:T(8,128)(2,1)S(1)} %copy-done.5, f32[16,128]{1,0:T(8,128)S(1)} %copy-done.4, f32[3,16]{1,0:T(4,128)S(1)} %copy-done.8), custom_call_target="tpu_custom_call" | custom-call | tf_op jit(solution)/shard_map/pallas_call | solution.py:246
  81.0 9.2 %all_to_all.21.cot_ref = bf16[8,16,128]{2,1,0:T(8,128)(2,1)S(1)} all-to-all(bf16[8,16,128]{2,1,0:T(8,128)(2,1)S(1)} %get-tuple-element.50), channel_id=1, replica_groups=mesh['z'=8,'xy'=16,'c'=2] {'z'}, dimensions={0} | all-to-all | bytes 65536 | tf_op jit(solution)/shard_map/all_to_all | solution.py:398
  90.3 3.2 %shard_map.127 = f32[32,72,128]{2,1,0:T(8,128)S(1)} custom-call(s32[10]{0:T(128)S(1)} %pad_add_fusion.where_ref, bf16[8,16,128]{2,1,0:T(8,128)(2,1)S(1)} %all_to_all.21.cot_ref, bf16[2,4,256,256]{3,2,1,0:T(8,128)(2,1)S(1)} %get-tuple-element.45.refs_3_.w_ref, f32[2,8,256]{2,1,0:T(8,128)S(1)} %get-tuple-element.46.refs_4_.v_ref, ...), custom_call_target="tpu_custom_call" | custom-call | tf_op jit(solution)/shard_map/pallas_call | solution.py:296
  93.5 3.0 %collective-permute-start.7 = (f32[32,72,128]{2,1,0:T(8,128)S(1)}, f32[32,72,128]{2,1,0:T(8,128)S(1)}, u32[]{:S(2)}, u32[]{:S(2)}) collective-permute-start(f32[32,72,128]{2,1,0:T(8,128)S(1)} %shard_map.127), channel_id=1, source_target_pairs={{0,1},{1,0},{2,3},{3,2},{4,5},{5,4},{6,7},{7,6},{8,9},{9,8},{10,11... | collective-permute-start | bytes 3538952 | tf_op jit(solution)/shard_map/ppermute | solution.py:400
  96.4 3.2 %shard_map.126.own_ref = f32[32,72,128]{2,1,0:T(8,128)S(1)} custom-call(s32[10]{0:T(128)S(1)} %pad_add_fusion.where_ref, bf16[8,16,128]{2,1,0:T(8,128)(2,1)S(1)} %all_to_all.21.cot_ref, bf16[2,4,256,256]{3,2,1,0:T(8,128)(2,1)S(1)} %get-tuple-element.45.refs_3_.w_ref, f32[2,8,256]{2,1,0:T(8,128)S(1)} %get-tuple-element.46.refs_4_.v_ref, ...), custom_call_target="tpu_custom_call" | custom-call | tf_op jit(solution)/shard_map/pallas_call | solution.py:296
  99.7 0.0 collective-permute-done.7.given_ref
  99.7 0.3 shard_map.128
  100.0 0.1 convert_element_type.8
  100.0 15.6 %all_to_all.22 = f16[32,72,128]{2,1,0:T(8,128)(2,1)S(1)} all-to-all(f16[32,72,128]{2,1,0:T(8,128)(2,1)S(1)} %convert_element_type.8), channel_id=1, replica_groups=mesh['z'=8,'xy'=16,'c'=2] {'xy','c'}, dimensions={0} | all-to-all | bytes 1179648 | tf_op jit(solution)/shard_map/all_to_all | solution.py:402
  115.6 0.1 convert.1.parts_ref
  115.7 0.9 shard_map.129
  (1 shorter events, 0.0 us)
Async XLA Ops:
  0.6 17.9 %copy-start.6 = (bf16[2,4,8]{2,1,0:T(4,128)(2,1)S(1)}, bf16[2,4,8]{2,1,0:T(4,128)(2,1)}, u32[]{:S(2)}) copy-start(bf16[2,4,8]{2,1,0:T(4,128)(2,1)} %b_ref.1) | copy-start | bytes 388
  0.6 1.2 %copy-start = (bf16[16,128,256]{2,1,0:T(8,128)(2,1)S(1)}, bf16[16,128,256]{2,1,0:T(8,128)(2,1)}, u32[]{:S(2)}) copy-start(bf16[16,128,256]{2,1,0:T(8,128)(2,1)} %param.11) | copy-start | bytes 3145732
  1.9 0.7 copy-start.3
  2.6 13.2 %copy-start.1 = (bf16[16,128,256]{2,1,0:T(8,128)(2,1)S(1)}, bf16[16,128,256]{2,1,0:T(8,128)(2,1)}, u32[]{:S(2)}) copy-start(bf16[16,128,256]{2,1,0:T(8,128)(2,1)} %param.11) | copy-start | bytes 3145732
  2.6 16.0 %copy-start.2 = (bf16[2,4,8,256]{3,2,1,0:T(8,128)(2,1)S(1)}, bf16[2,4,8,256]{3,2,1,0:T(8,128)(2,1)}, u32[]{:S(2)}) copy-start(bf16[2,4,8,256]{3,2,1,0:T(8,128)(2,1)} %w_ref.1) | copy-start | bytes 98308
  2.6 16.0 %copy-start.7 = (bf16[2,4,8]{2,1,0:T(4,128)(2,1)S(1)}, bf16[2,4,8]{2,1,0:T(4,128)(2,1)}, u32[]{:S(2)}) copy-start(bf16[2,4,8]{2,1,0:T(4,128)(2,1)} %h_ref.1) | copy-start | bytes 388
  5.7 22.1 %copy-start.9 = (s32[8]{0:T(128)S(1)}, s32[8]{0:T(128)}, u32[]{:S(2)}) copy-start(s32[8]{0:T(128)} %constant.27) | copy-start | bytes 100
  5.7 14.0 %collective-permute-start.3 = (bf16[2,256,256]{2,1,0:T(8,128)(2,1)}, bf16[2,256,256]{2,1,0:T(8,128)(2,1)S(1)}, u32[]{:S(2)}, u32[]{:S(2)}) collective-permute-start(bf16[2,256,256]{2,1,0:T(8,128)(2,1)} %get-tuple-element.38), channel_id=1, source_target_pairs={{0,32},{32,64},{64,96},{96,128},{128,160},{160,192},{192,224},{224... | collective-permute-start | bytes 786440 | tf_op jit(solution)/shard_map/ppermute | solution.py:366
  8.2 15.6 %collective-permute-start.4 = (bf16[2,256,256]{2,1,0:T(8,128)(2,1)S(1)}, bf16[2,256,256]{2,1,0:T(8,128)(2,1)S(1)}, u32[]{:S(2)}, u32[]{:S(2)}) collective-permute-start(bf16[2,256,256]{2,1,0:T(8,128)(2,1)S(1)} %get-tuple-element.39), channel_id=1, source_target_pairs={{0,224},{32,0},{64,32},{96,64},{128,96},{160,128},{192,160},{224,1... | collective-permute-start | bytes 786440 | tf_op jit(solution)/shard_map/ppermute | solution.py:366
  12.2 44.6 %collective-permute-start.5 = (bf16[2,256,256]{2,1,0:T(8,128)(2,1)S(1)}, bf16[2,256,256]{2,1,0:T(8,128)(2,1)S(1)}, u32[]{:S(2)}, u32[]{:S(2)}) collective-permute-start(bf16[2,256,256]{2,1,0:T(8,128)(2,1)S(1)} %get-tuple-element.42), channel_id=1, source_target_pairs={{0,64},{32,96},{64,128},{96,160},{128,192},{160,224},{192,0},{224,... | collective-permute-start | bytes 786440 | tf_op jit(solution)/shard_map/ppermute | solution.py:366
  12.2 44.6 %collective-permute-start.6 = (bf16[2,256,256]{2,1,0:T(8,128)(2,1)S(1)}, bf16[2,256,256]{2,1,0:T(8,128)(2,1)S(1)}, u32[]{:S(2)}, u32[]{:S(2)}) collective-permute-start(bf16[2,256,256]{2,1,0:T(8,128)(2,1)S(1)} %get-tuple-element.43), channel_id=1, source_target_pairs={{0,192},{32,224},{64,0},{96,32},{128,64},{160,96},{192,128},{224,1... | collective-permute-start | bytes 786440 | tf_op jit(solution)/shard_map/ppermute | solution.py:366
  18.1 46.0 %collective-permute-start = (bf16[2,256,256]{2,1,0:T(8,128)(2,1)S(1)}, bf16[2,256,256]{2,1,0:T(8,128)(2,1)S(1)}, u32[]{:S(2)}, u32[]{:S(2)}) collective-permute-start(bf16[2,256,256]{2,1,0:T(8,128)(2,1)S(1)} %get-tuple-element.34), channel_id=1, source_target_pairs={{0,96},{32,128},{64,160},{96,192},{128,224},{160,0},{192,32},{224,... | collective-permute-start | bytes 786440 | tf_op jit(solution)/shard_map/ppermute | solution.py:366
  19.8 44.3 %collective-permute-start.1 = (bf16[2,256,256]{2,1,0:T(8,128)(2,1)S(1)}, bf16[2,256,256]{2,1,0:T(8,128)(2,1)S(1)}, u32[]{:S(2)}, u32[]{:S(2)}) collective-permute-start(bf16[2,256,256]{2,1,0:T(8,128)(2,1)S(1)} %get-tuple-element.35), channel_id=1, source_target_pairs={{0,160},{32,192},{64,224},{96,0},{128,32},{160,64},{192,96},{224,1... | collective-permute-start | bytes 786440 | tf_op jit(solution)/shard_map/ppermute | solution.py:366
  23.9 40.2 %collective-permute-start.2 = (bf16[2,256,256]{2,1,0:T(8,128)(2,1)S(1)}, bf16[2,256,256]{2,1,0:T(8,128)(2,1)S(1)}, u32[]{:S(2)}, u32[]{:S(2)}) collective-permute-start(bf16[2,256,256]{2,1,0:T(8,128)(2,1)S(1)} %get-tuple-element.36), channel_id=1, source_target_pairs={{0,128},{32,160},{64,192},{96,224},{128,0},{160,32},{192,64},{224,... | collective-permute-start | bytes 786440 | tf_op jit(solution)/shard_map/ppermute | solution.py:366
  64.0 15.5 %copy-start.4 = (f32[16,128]{1,0:T(8,128)S(1)}, f32[16,128]{1,0:T(8,128)}, u32[]{:S(2)}) copy-start(f32[16,128]{1,0:T(8,128)} %delta_ref.1) | copy-start | bytes 24580
  64.0 15.5 %copy-start.5 = (bf16[16,128]{1,0:T(8,128)(2,1)S(1)}, bf16[16,128]{1,0:T(8,128)(2,1)}, u32[]{:S(2)}) copy-start(bf16[16,128]{1,0:T(8,128)(2,1)} %gate_ref.1) | copy-start | bytes 12292
  64.0 15.4 %copy-start.8 = (f32[3,16]{1,0:T(4,128)S(1)}, f32[3,16]{1,0:T(4,128)}, u32[]{:S(2)}) copy-start(f32[3,16]{1,0:T(4,128)} %target_ref.1) | copy-start | bytes 580
  93.5 6.2 %collective-permute-start.7 = (f32[32,72,128]{2,1,0:T(8,128)S(1)}, f32[32,72,128]{2,1,0:T(8,128)S(1)}, u32[]{:S(2)}, u32[]{:S(2)}) collective-permute-start(f32[32,72,128]{2,1,0:T(8,128)S(1)} %shard_map.127), channel_id=1, source_target_pairs={{0,1},{1,0},{2,3},{3,2},{4,5},{5,4},{6,7},{7,6},{8,9},{9,8},{10,11... | collective-permute-start | bytes 3538952 | tf_op jit(solution)/shard_map/ppermute | solution.py:400
